TPU v7x, 32 devices: a whole 2x2x4 slice. The times are simulated.
32 devices in a mesh: seq: 8 (over y, x, core), ch: 4 (over z).
Axes of the slice: x: 2, y: 2, z: 4, core: 2. Of those that a mesh axis runs over, the one named last changes fastest.
Arguments:
- query_feat: bfloat16 [8192, 4096], P('seq', 'ch'), may hold values from -6 to 6
- key_feat: bfloat16 [8192, 4096], P('seq', 'ch'), may hold values from -6 to 6
- value_feat: bfloat16 [8192, 4096], P('seq', 'ch'), may hold values from -6 to 6
- decay_rates: float32 [256, 16], P('ch'), may hold values from 2.4414063e-05 to 0.041666667
- residues: float32 [256, 16], P('ch'), may hold values from -0.28867513 to 0.28867513
- out_weight: bfloat16 [4096, 4096], P('ch', 'seq'), may hold values from -0.09375 to 0.09375
Outputs:
- mixed: bfloat16 [8192, 4096], P(('seq', 'ch'))
All inputs are finite; a program needn't handle non-finite values.
Results may differ from a plain program's by a relative error of at most 0.014.
Values may be sent and summed in bfloat16 or wider, within the bound.
No kernel may reach another device: no remote copies, remote signals or barrier semaphores. Data moves between devices by JAX's collectives and lax.ppermute only.
A program may use at most 128 MiB of HBM per device.

v0:
```python
import jax
import jax.numpy as jnp
from jax import lax
from jax.sharding import PartitionSpec as P

SUB = 256


def band_matrix(filter_taps, block):
    group_count = filter_taps.shape[0]
    flipped = jnp.concatenate(
        [jnp.flip(filter_taps, axis=1), jnp.zeros((group_count, block), filter_taps.dtype)], axis=1
    )
    tiled = jnp.tile(flipped, (1, block))[:, : block * (2 * block - 1)]
    return tiled.reshape(group_count, block, 2 * block - 1)[:, :, block - 1 :]


def on_device(query_feat, key_feat, value_feat, decay_rates, residues, out_weight):
    tok_rows, width_dev = query_feat.shape
    group_count, mode_count = decay_rates.shape
    group_width = width_dev // group_count
    block_count = tok_rows // SUB
    hi = lax.Precision.HIGHEST
    mixed_u = (key_feat.astype(jnp.float32) * value_feat.astype(jnp.float32)).astype(jnp.bfloat16)
    lag_steps = jnp.arange(SUB, dtype=jnp.float32)
    filter_taps = jnp.sum(
        residues[:, :, None] * jnp.exp(-decay_rates[:, :, None] * lag_steps), axis=1
    ).astype(jnp.bfloat16)
    toeplitz = band_matrix(filter_taps, SUB)
    inject = jnp.exp(-decay_rates[:, :, None] * (SUB - 1.0 - lag_steps)).astype(jnp.bfloat16)
    readout = residues[:, :, None] * jnp.exp(-decay_rates[:, :, None] * (lag_steps + 1.0))
    rates_mode = decay_rates.T[:, :, None]
    step_decay = jnp.exp(-rates_mode * SUB)
    blocks_u = mixed_u.reshape(block_count, SUB, group_count, group_width)
    local_part = jnp.einsum(
        "gab,nbgc->nagc", toeplitz, blocks_u, preferred_element_type=jnp.float32
    )
    block_sums = jnp.einsum("gmb,nbgc->nmgc", inject, blocks_u, preferred_element_type=jnp.float32)
    prefix = [jnp.zeros((mode_count, group_count, group_width), jnp.float32)]
    for block in range(block_count):
        prefix.append(step_decay * prefix[-1] + block_sums[block])
    final_state = prefix[block_count]
    starts = jnp.stack(prefix[:block_count])
    my_index = lax.axis_index("seq")
    piece = lax.all_gather(
        final_state[None].astype(jnp.bfloat16), "seq", axis=0, tiled=True
    ).astype(jnp.float32)
    positions = jnp.arange(piece.shape[0], dtype=jnp.int32)
    lag_count = my_index - 1 - positions
    live = lag_count >= 0
    lag_float = jnp.maximum(lag_count, 0).astype(jnp.float32) * tok_rows
    weights = jnp.exp(-rates_mode[None] * lag_float[:, None, None, None])
    weights = jnp.where(live[:, None, None, None], weights, 0.0)
    incoming = jnp.zeros_like(final_state) + jnp.sum(weights * piece, axis=0)
    offsets = (SUB * jnp.arange(block_count, dtype=jnp.float32))[:, None, None, None]
    entering = starts + jnp.exp(-rates_mode[None] * offsets) * incoming[None]
    carried = jnp.einsum("gma,nmgc->nagc", readout, entering, precision=hi)
    gate_q = query_feat.reshape(block_count, SUB, group_count, group_width).astype(jnp.float32)
    gated = (gate_q * (local_part + carried)).astype(jnp.bfloat16).reshape(tok_rows, width_dev)
    weight_cols = lax.all_gather(out_weight, "seq", axis=1, tiled=True)
    return lax.psum_scatter(
        jnp.dot(gated, weight_cols, preferred_element_type=jnp.float32).astype(jnp.bfloat16),
        "ch",
        scatter_dimension=0,
        tiled=True,
    )


def solution(mesh):
    in_specs = (
        P("seq", "ch"),
        P("seq", "ch"),
        P("seq", "ch"),
        P("ch", None),
        P("ch", None),
        P("ch", "seq"),
    )
    out_specs = P(("seq", "ch"), None)
    return jax.shard_map(
        on_device, mesh=mesh, in_specs=in_specs, out_specs=out_specs, check_vma=False
    )
```

profile of v0, /device:TPU:0, one launch (start us, length us, event | category | flops | bytes accessed | tf_op | source)
XLA Modules:
  0.0 312.6 jit_solution(4421169243908400067)
XLA Ops:
  6.5 0.0 all-gather.2.cloned.1.call-start
  6.5 0.7 all-gather.2.cloned.1.call-update
  7.3 0.0 reduce-scatter.2.cloned.1.call-start
  7.3 0.7 negate_bitcast_fusion
  8.0 0.1 copy.73
  8.1 3.2 %multiply_convert_fusion = bf16[1024,1024]{1,0:T(8,128)(2,1)S(1)} fusion(bf16[1024,1024]{1,0:T(8,128)(2,1)} %param.8, bf16[1024,1024]{1,0:T(8,128)(2,1)} %param.7), kind=kLoop, calls=%fused_computation.5 | loop fusion | flops 4194304 | bytes 6291456 | tf_op jit(solution)/shard_map/convert_element_type | solution.py:24
  11.3 2.6 copy.71
  13.8 3.3 %reshape.69 = bf16[4,256,64,16]{1,0,3,2:T(4,128)(2,1)S(1)} reshape(bf16[1024,1024]{0,1:T(8,128)(2,1)} %copy.71) | data formatting | bytes 4194304 | tf_op jit(solution)/shard_map/reshape | solution.py:34
  17.2 0.0 copy-start.1
  17.2 2.1 fusion.2
  19.3 0.0 copy-done.1
  19.3 0.0 copy-start.2
  19.3 3.0 copy.76
  22.3 0.0 copy-done.2
  22.3 0.1 fusion.16
  22.4 13.7 %all_gather.6 = bf16[8,16,64,16]{2,3,1,0:T(8,128)(2,1)S(1)} all-gather(bf16[1,16,64,16]{2,3,1,0:T(8,128)(2,1)S(1)} %get-tuple-element.5), channel_id=1, replica_groups=mesh['seq'=8,'ch'=4] {'seq'}, dimensions={0}, use_global_device_ids=true | all-gather | bytes 294912 | tf_op jit(solution)/shard_map/all_gather | solution.py:45
  36.1 0.1 exponential_select_fusion
  36.1 0.0 copy-start.3
  36.2 0.1 multiply_reduce_fusion
  36.3 0.1 multiply_exponential_fusion
  36.4 0.1 maximum_add_fusion
  36.5 1.9 copy.79
  38.4 0.0 copy-done.3
  38.4 0.1 copy.72
  38.5 0.4 multiply_reduce_fusion.1
  38.9 0.4 rev.4
  39.3 1.4 tile.4
  40.7 38.5 %copy.86 = bf16[8,8,256,512]{3,1,2,0:T(8,128)(2,1)S(1)} copy(bf16[8,8,256,512]{3,2,1,0:T(8,128)(2,1)S(1)} %bitcast.40) | data formatting | bytes 33554432
  79.2 6.5 %slice.24 = bf16[64,130816]{1,0:T(8,128)(2,1)} slice(bf16[64,131072]{1,0:T(8,128)(2,1)S(1)} %bitcast.41), slice={[0:64], [0:130816]} | slice | bytes 33488896 | tf_op jit(solution)/shard_map/slice | solution.py:14
  85.8 36.0 %reshape.70 = bf16[64,256,511]{2,1,0:T(8,128)(2,1)} reshape(bf16[64,130816]{1,0:T(8,128)(2,1)} %slice.24) | data formatting | bytes 33488896 | tf_op jit(solution)/shard_map/reshape | solution.py:15
  121.8 4.1 %copy.70 = f32[1024,1024]{0,1:T(8,128)} copy(bf16[1024,1024]{1,0:T(8,128)(2,1)} %param.6) | data formatting | bytes 6291456 | tf_op jit(solution)/shard_map/convert_element_type | solution.py:58
  125.9 5.6 %reshape.72 = f32[4,256,64,16]{1,0,3,2:T(4,128)} reshape(f32[1024,1024]{0,1:T(8,128)} %copy.70) | data formatting | bytes 8388608 | tf_op jit(solution)/shard_map/convert_element_type | solution.py:58
  131.6 0.0 copy-start
  131.6 8.2 %fusion = f32[64,4,16,256]{3,2,1,0:T(8,128)S(1)} fusion(bf16[64,256,511]{2,1,0:T(8,128)(2,1)} %reshape.70, bf16[4,256,64,16]{1,0,3,2:T(4,128)(2,1)} %copy-done.1), kind=kOutput, calls=%fused_computation.1 | convolution fusion | flops 536870912 | bytes 14680064 | tf_op jit(solution)/shard_map/gab,nbgc->nagc/dot_general | solution.py:35
  139.8 0.0 copy-done
  139.8 4.7 %fusion.1 = bf16[4,256,64,16]{1,3,0,2:T(8,128)(2,1)S(1)} fusion(f32[4,256,64,16]{1,0,3,2:T(4,128)S(1)} %copy-done, f32[64,4,16,256]{3,2,1,0:T(8,128)S(1)} %fusion, f32[4,16,64,16]{1,3,0,2:T(8,128)S(1)} %copy.79, f32[256]{0:T(256)S(1)} %iota_add_fusion, f32[64,16]{1,0:T(8,128)S(1)} %copy.73, f32[64,16]{1,0:T(8,128)S(1)} %copy.72), kind=kOutput, calls=%fused_computation.4 | convolution fusion | flops 204996608 | bytes 10757120 | tf_op jit(solution)/shard_map/gma,nmgc->nagc/dot_general | solution.py:57
  144.5 1.1 copy.81
  145.5 0.5 copy.87
  146.0 0.0 all-gather.2.cloned.1.call-done
  146.1 14.8 %convolution_convert_fusion = bf16[1024,4096]{1,0:T(8,128)(2,1)} fusion(bf16[1024,1024]{0,1:T(8,128)(2,1)S(1)} %bitcast.44, bf16[1024,4096]{1,0:T(8,128)(2,1)} %all-gather.2.cloned.1.call-done), kind=kOutput, calls=%fused_computation.2 | convolution fusion | flops 8594128896 | bytes 18874368 | tf_op jit(solution)/shard_map/dot_general | solution.py:62
  160.8 0.0 reduce-scatter.2.cloned.1.call-update
  160.9 144.9 %reduce-scatter.2.cloned.1.call-done = bf16[256,4096]{1,0:T(8,128)(2,1)} async-done(((bf16[1024,4096]{1,0:T(8,128)(2,1)}), bf16[256,4096]{1,0:T(8,128)(2,1)}) %reduce-scatter.2.cloned.1.call-update) | async-done | bytes 2097168 | tf_op jit(solution)/shard_map/reduce_scatter | solution.py:61
  (8 shorter events, 0.1 us)
Async XLA Ops:
  6.5 139.5 %all-gather.2.cloned.1.call-start = ((), (), s32[]{:S(2)}) async-start(), calls=%async_computation.1 | async-start | bytes 9437184 | tf_op jit(solution)/shard_map/all_gather | solution.py:60
  7.3 298.5 %reduce-scatter.2.cloned.1.call-start = ((), (), s32[]{:S(2)}) async-start(), calls=%async_computation.2 | async-start | bytes 10485760 | tf_op jit(solution)/shard_map/reduce_scatter | solution.py:61
  17.2 2.1 copy-start.1
  19.3 3.0 copy-start.2
  36.1 2.2 copy-start.3
  131.6 8.2 %copy-start = (f32[4,256,64,16]{1,0,3,2:T(4,128)S(1)}, f32[4,256,64,16]{1,0,3,2:T(4,128)}, u32[]{:S(2)}) copy-start(f32[4,256,64,16]{1,0,3,2:T(4,128)} %reshape.72) | copy-start | bytes 12582916
Sparse Core Ops, SparseCore 0:
  9.2 60.7 all-gather.1
  161.0 144.7 reduce-scatter.1
where the time goes:
time: 313 us
  waiting for transfers between devices  146 us (47%)
  local copies, waits for them, and re-layouts  105 us (34%)
  matrix products  29.7 us (9%)
  blocking collectives  13.7 us (4%)
  between operations  13.6 us (4%)
  other arithmetic  4.85 us (2%)
    reduce_scatter x1, waiting for transfers between devices, on_device(): lax.psum_scatter(jnp.dot(gated, weight_cols, preferred_element_type=jnp.f...  145 us
    unnamed x11, local copies, waits for them, and re-layouts  39.1 us
    reshape x1, local copies, waits for them, and re-layouts, band_matrix(): return tiled.reshape(group_count, block, 2 * block - 1)[:, :, block - 1:]  36 us
    dot_general x1, matrix products, on_device(): jnp.dot(gated, weight_cols, preferred_element_type=jnp.float32)  14.8 us
    all_gather x1, blocking collectives, on_device(): lax.all_gather(final_state[None].astype(jnp.bfloat16), 'seq', axis=0, til...  13.7 us
    convert_element_type x2, local copies, waits for them, and re-layouts, on_device(): query_feat.reshape(block_count, SUB, group_count, group_width)  9.75 us
    dot_general x1, matrix products, on_device(): jnp.einsum('gab,nbgc->nagc', toeplitz, blocks_u, preferred_element_type=j...  8.22 us
    slice x1, local copies, waits for them, and re-layouts, band_matrix(): tiled = jnp.tile(flipped, (1, block))[:, :block * (2 * block - 1)]  6.51 us
  transfers between devices with their start and end apart: 2, of which 1 were waited for; matrix products, arithmetic and copies ran while one was open for 40% of the time, Pallas kernels for 0%

commit v1 on v0

v1 whole, which is shorter than its diff:
```python
import functools

import jax
import jax.numpy as jnp
from jax import lax
from jax.experimental import pallas as pl
from jax.experimental.pallas import tpu as pltpu
from jax.sharding import PartitionSpec as P

SUB = 256
TILE = 128
F32 = jnp.float32
BF16 = jnp.bfloat16


def dot32(a, b):
    return jnp.dot(a, b, preferred_element_type=F32)


def own_mask(rows, cols, modes, width):
    r = lax.broadcasted_iota(jnp.int32, (rows, cols), 0) // modes
    c = lax.broadcasted_iota(jnp.int32, (rows, cols), 1) // width
    return r == c


def range_state_kernel(modes, width, k_ref, v_ref, rate_ref, u_ref, f_ref):
    u = (k_ref[...].astype(F32) * v_ref[...].astype(F32)).astype(BF16)
    u_ref[...] = u
    toks, cols = u.shape
    rows = rate_ref.shape[0]
    left = (toks - 1) - lax.broadcasted_iota(jnp.int32, (rows, toks), 1)
    inject = jnp.exp(-rate_ref[...] * left.astype(F32)).astype(BF16)
    sums = jnp.where(own_mask(rows, cols, modes, width), dot32(inject, u), 0.0)
    f_ref[...] = jnp.sum(sums.reshape(rows // modes, modes, cols), axis=0).astype(BF16)


def range_state(key_feat, value_feat, rate_col, modes, width):
    toks, chans = key_feat.shape
    step = 256
    rows = step // width * modes
    feat = pl.BlockSpec((toks, step), lambda i: (0, i))
    return pl.pallas_call(
        functools.partial(range_state_kernel, modes, width),
        grid=(chans // step,),
        in_specs=[feat, feat, pl.BlockSpec((rows, 1), lambda i: (i, 0))],
        out_specs=[feat, pl.BlockSpec((modes, step), lambda i: (0, i))],
        out_shape=[
            jax.ShapeDtypeStruct((toks, chans), BF16),
            jax.ShapeDtypeStruct((modes, chans), BF16),
        ],
        compiler_params=pltpu.CompilerParams(vmem_limit_bytes=24 << 20),
        name="range_state",
    )(key_feat, value_feat, rate_col)


def local_kernel(
    modes, width, u_ref, rate_ref, res_ref, rate_row_ref, res_row_ref, z_ref, taps_ref
):
    groups = TILE // width
    rows = groups * modes
    rate, res = rate_ref[...], res_ref[...]
    toks = u_ref.shape[0]
    blocks = toks // SUB
    lag = (2 * SUB - lax.broadcasted_iota(jnp.int32, (rows, 2 * SUB), 1)) % (2 * SUB)
    terms = jnp.where(lag < SUB, res * jnp.exp(-rate * lag.astype(F32)), 0.0)
    wheel = jnp.sum(terms.reshape(groups, modes, 2 * SUB), axis=1)
    half = SUB // 2
    for g in range(groups):
        base = jnp.broadcast_to(wheel[g : g + 1], (8, 2 * SUB))
        base = pltpu.roll(base, 0, 1, stride=1, stride_axis=0)
        low = jnp.concatenate(
            [pltpu.roll(base, half + 8 * i, 1)[:, :SUB] for i in range(half // 8)], axis=0
        ).astype(BF16)
        taps_ref[g, half:, :] = low
        taps_ref[g, :half, :half] = low[:, half:]
        taps_ref[g, :half, half:] = jnp.zeros((half, half), BF16)

    mask = own_mask(rows, TILE, modes, width)
    left = (SUB - 1) - lax.broadcasted_iota(jnp.int32, (rows, SUB), 1)
    inject = jnp.exp(-rate * left.astype(F32)).astype(BF16)
    after = lax.broadcasted_iota(jnp.int32, (SUB, rows), 0) + 1
    readout = (
        res_row_ref[...] * jnp.exp(-rate_row_ref[...] * after.astype(F32))
    ).astype(BF16)
    decay = jnp.exp(-rate * SUB)
    state = None
    lane_group = (lax.broadcasted_iota(jnp.int32, (SUB, 2 * TILE), 1) % TILE) // width
    for pair in range(0, blocks, 2):
        cuts = [u_ref[(pair + i) * SUB : (pair + i + 1) * SUB, :] for i in range(2)]
        both = jnp.concatenate(cuts, axis=1)
        z = dot32(taps_ref[0], both)
        for g in range(1, groups):
            z = jnp.where(lane_group == g, dot32(taps_ref[g], both), z)
        sums = dot32(inject, both)
        for i in range(2):
            n = pair + i
            out = z[:, i * TILE : (i + 1) * TILE]
            if state is not None:
                out = out + dot32(readout, state.astype(BF16))
            z_ref[n * SUB : (n + 1) * SUB, :] = out
            own = jnp.where(mask, sums[:, i * TILE : (i + 1) * TILE], 0.0)
            state = own if state is None else decay * state + own


def local_conv(u, rate_col, res_col, rate_row, res_row, modes, width):
    toks, chans = u.shape
    rows = TILE // width * modes
    col = pl.BlockSpec((rows, 1), lambda i: (i, 0))
    row = pl.BlockSpec((1, rows), lambda i: (0, i))
    feat = pl.BlockSpec((toks, TILE), lambda i: (0, i))
    return pl.pallas_call(
        functools.partial(local_kernel, modes, width),
        grid=(chans // TILE,),
        in_specs=[feat, col, col, row, row],
        out_specs=feat,
        out_shape=jax.ShapeDtypeStruct((toks, chans), F32),
        scratch_shapes=[pltpu.VMEM((TILE // width, SUB, SUB), BF16)],
        compiler_params=pltpu.CompilerParams(vmem_limit_bytes=24 << 20),
        name="local_conv",
    )(u, rate_col, res_col, rate_row, res_row)


def gate_kernel(
    modes, width, toks, place_ref, lag_ref, z_ref, q_ref, rate_row_ref, res_row_ref,
    rate_ref, *refs
):
    y_ref, states = refs[-1], refs[:-1]
    rate = rate_ref[...]
    entering = jnp.zeros(rate.shape, F32)
    at = 0
    for piece in states:
        for j in range(piece.shape[0]):
            lag = lag_ref[at]
            span = (jnp.maximum(lag, 0) * toks).astype(F32)
            weight = jnp.where(lag >= 0, jnp.exp(-rate * span), 0.0)
            entering = entering + weight * piece[j].astype(F32)
            at += 1
    first = place_ref[0] * SUB + 1
    rows = TILE // width * modes
    mask = own_mask(rows, TILE, modes, width)
    for tile in range(q_ref.shape[1] // TILE):
        lanes = slice(tile * TILE, (tile + 1) * TILE)
        group = slice(tile * rows, (tile + 1) * rows)
        after = lax.broadcasted_iota(jnp.int32, (SUB, rows), 0) + first
        readout = (
            res_row_ref[:, group] * jnp.exp(-rate_row_ref[:, group] * after.astype(F32))
        ).astype(BF16)
        spread = jnp.concatenate([entering[:, lanes]] * (TILE // width), axis=0)
        spread = jnp.where(mask, spread, 0.0).astype(BF16)
        z = z_ref[:, lanes] + dot32(readout, spread)
        y_ref[:, lanes] = (q_ref[:, lanes].astype(F32) * z).astype(BF16)


def gate(place, lags, z, query_feat, rate_row, res_row, rate_mc, states, modes, width):
    toks, chans = query_feat.shape
    whole = lambda a: pl.BlockSpec(a.shape, lambda i, p, g: (0,) * a.ndim)
    block = pl.BlockSpec((SUB, chans), lambda i, p, g: (p[0], 0))
    return pl.pallas_call(
        functools.partial(gate_kernel, modes, width, toks),
        grid_spec=pltpu.PrefetchScalarGridSpec(
            num_scalar_prefetch=2,
            grid=(1,),
            in_specs=[block, block, whole(rate_row), whole(res_row), whole(rate_mc)]
            + [whole(s) for s in states],
            out_specs=pl.BlockSpec((SUB, chans), lambda i, p, g: (0, 0)),
        ),
        out_shape=jax.ShapeDtypeStruct((SUB, chans), BF16),
        compiler_params=pltpu.CompilerParams(vmem_limit_bytes=24 << 20),
        name="gate",
    )(place, lags, z, query_feat, rate_row, res_row, rate_mc, *states)


def share_kernel(ya_ref, yb_ref, *refs):
    out_ref, weights = refs[-1], refs[:-1]
    half = len(weights) // 2
    at = 0
    for wa, wb in zip(weights[:half], weights[half:]):
        cols = wa.shape[1]
        total = dot32(ya_ref[...], wa[...]) + dot32(yb_ref[...], wb[...])
        out_ref[:, at : at + cols] = total.astype(BF16)
        at += cols


def share(ya, yb, near, far):
    cols = sum(w.shape[1] for w in near)
    return pl.pallas_call(
        share_kernel,
        out_shape=jax.ShapeDtypeStruct((ya.shape[0], cols), BF16),
        compiler_params=pltpu.CompilerParams(vmem_limit_bytes=32 << 20),
        cost_estimate=pl.CostEstimate(
            flops=4 * ya.size * cols, bytes_accessed=4 * ya.shape[1] * cols, transcendentals=0
        ),
        name="share",
    )(ya, yb, *near, *far)


def finish_kernel(count, place_ref, ya_ref, yb_ref, got_ref, *refs):
    out_ref = refs[-1]
    weights = refs[: 2 * count]
    at = 0
    for wa, wb in zip(weights[:count], weights[count:]):
        cols = wa.shape[1]
        total = dot32(ya_ref[...], wa[...]) + dot32(yb_ref[...], wb[...])
        total = total + got_ref[:, at : at + cols].astype(F32)
        out_ref[:, at : at + cols] = total.astype(BF16)
        at += cols


def finish(place, ya, yb, got, near, far, out, all_cols):
    rows, cols = got.shape
    whole = lambda a: pl.BlockSpec(a.shape, lambda i, p: (0,) * a.ndim)
    args = [ya, yb, got, *near, *far]
    specs = [whole(a) for a in args]
    alias = {}
    if out is not None:
        alias = {1 + len(args): 0}
        args.append(out)
        specs.append(pl.BlockSpec(memory_space=pl.ANY))
    return pl.pallas_call(
        functools.partial(finish_kernel, len(near)),
        grid_spec=pltpu.PrefetchScalarGridSpec(
            num_scalar_prefetch=1,
            grid=(1,),
            in_specs=specs,
            out_specs=pl.BlockSpec((rows, cols), lambda i, p: (0, p[0])),
        ),
        out_shape=jax.ShapeDtypeStruct((rows, all_cols), BF16),
        input_output_aliases=alias,
        compiler_params=pltpu.CompilerParams(vmem_limit_bytes=32 << 20),
        cost_estimate=pl.CostEstimate(
            flops=4 * ya.size * cols, bytes_accessed=4 * ya.shape[1] * cols, transcendentals=0
        ),
        name="finish",
    )(place, *args)


def flip(x, axis, size, bits):
    return lax.ppermute(x, axis, [(i, i ^ bits) for i in range(size)])


def spread(halves, size):
    left, right = halves
    across = [flip(w, "seq", size, 2) for w in halves]
    along = [flip(w, "seq", size, 4) for w in halves]
    corner = [flip(across[0], "seq", size, 4), flip(along[1], "seq", size, 2)]
    pieces = {0: halves, 2: across, 4: along, 6: corner}
    for m in (0, 2, 4, 6):
        pieces[m + 1] = [flip(w, "seq", size, 1) for w in pieces[m]]
    return pieces


def on_device(seq_size, ch_size, query_feat, key_feat, value_feat, decay_rates, residues, out_weight):
    toks, chans = query_feat.shape
    groups, modes = decay_rates.shape
    width = chans // groups
    piece_cols = out_weight.shape[1]
    all_cols = piece_cols * seq_size
    me = lax.axis_index("seq").astype(jnp.int32)
    plane = lax.axis_index("ch").astype(jnp.int32)

    if seq_size == 8:
        mid = piece_cols // 2
        halves = [out_weight[:, :mid], out_weight[:, mid:]]
        far_halves = [flip(w, "ch", ch_size, 2) for w in halves]
        near, far = spread(halves, seq_size), spread(far_halves, seq_size)
        order = [(near[m], far[m], me ^ m) for m in range(8)]
    else:
        gather = lambda w: lax.all_gather(w, "seq", axis=1, tiled=True)
        near, far = gather(out_weight), gather(flip(out_weight, "ch", ch_size, 2))
        order = [([near], [far], jnp.int32(0))]

    rate_col = decay_rates.reshape(groups * modes, 1)
    res_col = residues.reshape(groups * modes, 1)
    rate_row = decay_rates.reshape(1, groups * modes)
    res_row = residues.reshape(1, groups * modes)
    rate_mc = jnp.repeat(decay_rates.T, width, axis=1)

    u, final_state = range_state(key_feat, value_feat, rate_col, modes, width)
    final_state = final_state[None]
    if seq_size == 8:
        states = [final_state] + [flip(final_state, "seq", seq_size, m) for m in range(1, 8)]
        origin = me ^ jnp.arange(8, dtype=jnp.int32)
    else:
        states = [lax.all_gather(final_state, "seq", axis=0, tiled=True)]
        origin = jnp.arange(seq_size, dtype=jnp.int32)
    lags = me - 1 - origin
    z = local_conv(u, rate_col, res_col, rate_row, res_row, modes, width)

    def gated(slot):
        place = (plane ^ slot).reshape(1)
        return gate(place, lags, z, query_feat, rate_row, res_row, rate_mc, states, modes, width)

    far_other = flip(gated(3), "ch", ch_size, 2)
    far_own = flip(gated(2), "ch", ch_size, 2)
    near_other, near_own = gated(1), gated(0)

    got = [flip(share(near_other, far_other, a, b), "ch", ch_size, 1) for a, b, _ in order]
    out = None
    for (a, b, place), part in zip(order, got):
        out = finish(place.reshape(1), near_own, far_own, part, a, b, out, all_cols)
    return out


def solution(mesh):
    in_specs = (
        P("seq", "ch"),
        P("seq", "ch"),
        P("seq", "ch"),
        P("ch", None),
        P("ch", None),
        P("ch", "seq"),
    )
    out_specs = P(("seq", "ch"), None)
    body = functools.partial(on_device, mesh.shape["seq"], mesh.shape["ch"])
    return jax.shard_map(
        body, mesh=mesh, in_specs=in_specs, out_specs=out_specs, check_vma=False
    )
```

time: 313 us -> 214 us (0.68)
  local copies, waits for them, and re-layouts: 105 us -> 22.2 us
  Pallas kernels: 0 us -> 60 us
  waiting for transfers between devices: 146 us -> 93.9 us
  starting transfers between devices: 0.04 us -> 37.1 us
  matrix products: 29.7 us -> 0 us
  blocking collectives: 13.7 us -> 0 us
  between operations: 13.6 us -> 0.46 us
  other arithmetic: 4.85 us -> 0.01 us
    reduce_scatter x1 -> x0, waiting for transfers between devices: 145 us -> none  [on_device(): lax.psum_scatter(jnp.dot(gated, weight_cols, preferred_element_type=jnp.f...]
    ppermute x0 -> x47, waiting for transfers between devices: none -> 93.9 us  [flip(): return lax.ppermute(x, axis, [(i, i ^ bits) for i in range(size)])]
    pallas_call x0 -> x22, Pallas kernels: none -> 60 us  [the longest x8 23.3 us: finish(): pl.pallas_call(functools.partial(finish_kernel, len(near)), grid_spec=plt...]
    reshape x2 -> x5, local copies, waits for them, and re-layouts: 39.4 us -> 1.03 us  [the longest x1 0.3 us: on_device(): res_col = residues.reshape(groups * modes, 1)]
    ppermute x0 -> x47, starting transfers between devices: none -> 37.1 us  [flip(): return lax.ppermute(x, axis, [(i, i ^ bits) for i in range(size)])]
    dot_general x4 -> x0, matrix products: 29.7 us -> none  [the longest x1 14.8 us: on_device(): jnp.dot(gated, weight_cols, preferred_element_type=jnp.float32)]
    unnamed x11 -> x72, local copies, waits for them, and re-layouts: 39.1 us -> 18.6 us
    all_gather x1 -> x0, blocking collectives: 13.7 us -> none  [on_device(): lax.all_gather(final_state[None].astype(jnp.bfloat16), 'seq', axis=0, til...]
  transfers between devices with their start and end apart: 2 -> 47, of which waited for: 1 -> 15; matrix products, arithmetic and copies ran while one was open for 40% -> 1% of each run, Pallas kernels for 0% -> 27%
where the time goes in v1:
time: 214 us
  waiting for transfers between devices  93.9 us (44%)
  Pallas kernels  60 us (28%)
  starting transfers between devices  37.1 us (17%)
  local copies, waits for them, and re-layouts  22.2 us (10%)
    ppermute x47, waiting for transfers between devices, flip(): return lax.ppermute(x, axis, [(i, i ^ bits) for i in range(size)])  93.9 us
    ppermute x47, starting transfers between devices, flip(): return lax.ppermute(x, axis, [(i, i ^ bits) for i in range(size)])  37.1 us
    pallas_call x8, Pallas kernels, finish(): pl.pallas_call(functools.partial(finish_kernel, len(near)), grid_spec=plt...  23.3 us
    unnamed x72, local copies, waits for them, and re-layouts  18.6 us
    pallas_call x8, Pallas kernels, share(): pl.pallas_call(share_kernel, out_shape=jax.ShapeDtypeStruct((ya.shape[0],...  15.4 us
    pallas_call x1, Pallas kernels, local_conv(): pl.pallas_call(functools.partial(local_kernel, modes, width), grid=(chans...  13.8 us
    pallas_call x4, Pallas kernels, gate(): pl.pallas_call(functools.partial(gate_kernel, modes, width, toks), grid_s...  5.02 us
  transfers between devices with their start and end apart: 47, of which 15 were waited for; matrix products, arithmetic and copies ran while one was open for 1% of the time, Pallas kernels for 27%

profile of v1, /device:TPU:0, one launch (start us, length us, event | category | flops | bytes accessed | tf_op | source)
XLA Modules:
  0.0 213.6 jit_solution(6792840271335225154)
XLA Ops:
  0.0 2.4 %fusion = (bf16[1024,256]{1,0:T(8,128)(2,1)}, bf16[1024,256]{1,0:T(8,128)(2,1)}) fusion(bf16[1024,512]{1,0:T(8,128)(2,1)} %param.11), kind=kLoop, calls=%fused_computation.1 | loop fusion | bytes 2097152 | tf_op jit(solution)/shard_map/slice | solution.py:263
  2.4 4.0 %collective-permute-start.15 = (bf16[1024,256]{1,0:T(8,128)(2,1)}, bf16[1024,256]{1,0:T(8,128)(2,1)}, u32[]{:S(2)}, u32[]{:S(2)}) collective-permute-start(bf16[1024,256]{1,0:T(8,128)(2,1)} %get-tuple-element.10.refs_0_), channel_id=1, source_target_pairs={{0,2},{1,3},{2,0},{3,1},{4,6},{5,7},{6,4},{7,5},{8,10},{9,11},{10,... | collective-permute-start | bytes 1572872 | tf_op jit(solution)/shard_map/ppermute | solution.py:238
  6.9 1.6 copy-done.6
  8.5 2.5 %range_state.1 = (bf16[1024,1024]{1,0:T(8,128)(2,1)S(1)}, bf16[16,1024]{1,0:T(8,128)(2,1)S(1)}) custom-call(bf16[1024,1024]{1,0:T(8,128)(2,1)S(1)} %copy-done.5, bf16[1024,1024]{1,0:T(8,128)(2,1)S(1)} %copy-done.6, f32[1024,1]{1,0:T(8,128)S(1)} %reshape.68.rate_ref), custom_call_target="tpu_custom_call" | custom-call | tf_op jit(solution)/shard_map/range_state/pallas_call | solution.py:42
  10.9 1.3 copy-done.7
  12.8 1.8 collective-permute-start.1
  14.6 0.8 collective-permute-start.2
  15.4 1.3 collective-permute-done.1.refs_2_
  16.7 1.8 collective-permute-start.3
  19.3 1.3 collective-permute-done.3.refs_4_
  20.6 3.1 %collective-permute-start.5 = (bf16[1,16,1024]{2,1,0:T(8,128)(2,1)S(1)}, bf16[1,16,1024]{2,1,0:T(8,128)(2,1)S(1)}, u32[]{:S(2)}, u32[]{:S(2)}) collective-permute-start(bf16[1,16,1024]{2,1,0:T(8,128)(2,1)S(1)} %bitcast.19), channel_id=1, source_target_pairs={{0,24},{4,28},{8,16},{12,20},{16,8},{20,12},{24,0},{28,4},{1,25},{... | collective-permute-start | bytes 98312 | tf_op jit(solution)/shard_map/ppermute | solution.py:238
  23.7 1.9 collective-permute-done.5.refs_6_
  25.6 2.3 %collective-permute-done.6.refs_7_ = bf16[1,16,1024]{2,1,0:T(8,128)(2,1)S(1)} collective-permute-done((bf16[1,16,1024]{2,1,0:T(8,128)(2,1)S(1)}, bf16[1,16,1024]{2,1,0:T(8,128)(2,1)S(1)}, u32[]{:S(2)}, u32[]{:S(2)}) %collective-permute-start.6) | collective-permute-done | bytes 32800 | tf_op jit(solution)/shard_map/ppermute | solution.py:238
  28.1 13.8 %collective-permute-done.15.refs_2_ = bf16[1024,256]{1,0:T(8,128)(2,1)} collective-permute-done((bf16[1024,256]{1,0:T(8,128)(2,1)}, bf16[1024,256]{1,0:T(8,128)(2,1)}, u32[]{:S(2)}, u32[]{:S(2)}) %collective-permute-start.15) | collective-permute-done | bytes 524320 | tf_op jit(solution)/shard_map/ppermute | solution.py:238
  42.0 1.8 collective-permute-start.34
  44.9 1.6 copy-done.8
  46.4 13.8 %local_conv.1.z_ref = f32[1024,1024]{1,0:T(8,128)S(1)} custom-call(bf16[1024,1024]{1,0:T(8,128)(2,1)S(1)} %copy-done.8, f32[1024,1]{1,0:T(8,128)S(1)} %reshape.68.rate_ref, f32[1024,1]{1,0:T(8,128)S(1)} %reshape.69.res_ref, f32[1,1024]{1,0:T(1,128)S(1)} %reshape.55.rate_row_ref, f32[1,1024]{1,0:T(1,128)S(1)} %reshape.56.res_row_ref), custom_call_target="tpu_custom_call" | custom-call | tf_op jit(solution)/shard_map/local_conv/pallas_call | solution.py:111
  60.3 1.0 gate.7
  61.3 0.9 copy-done
  62.3 1.6 collective-permute-start.12
  64.4 2.2 %copy-done.1 = f32[1024,1024]{1,0:T(8,128)S(1)} copy-done((f32[1024,1024]{1,0:T(8,128)S(1)}, f32[1024,1024]{1,0:T(8,128)}, u32[]{:S(2)}) %copy-start.1) | copy-done | bytes 4194328
  66.5 1.9 gate.5
  68.4 2.9 %collective-permute-start.7 = (bf16[256,1024]{1,0:T(8,128)(2,1)}, bf16[256,1024]{1,0:T(8,128)(2,1)}, u32[]{:S(2)}, u32[]{:S(2)}) collective-permute-start(bf16[256,1024]{1,0:T(8,128)(2,1)} %gate.5), channel_id=1, source_target_pairs={{0,2},{1,3},{2,0},{3,1},{4,6},{5,7},{6,4},{7,5},{8,10},{9,11},{10,... | collective-permute-start | bytes 1572872 | tf_op jit(solution)/shard_map/ppermute | solution.py:238
  71.3 27.8 %collective-permute-done.8.yb_ref = bf16[256,1024]{1,0:T(8,128)(2,1)S(1)} collective-permute-done((bf16[256,1024]{1,0:T(8,128)(2,1)S(1)}, bf16[256,1024]{1,0:T(8,128)(2,1)S(1)}, u32[]{:S(2)}, u32[]{:S(2)}) %collective-permute-start.8) | collective-permute-done | bytes 524320 | tf_op jit(solution)/shard_map/ppermute | solution.py:238
  99.1 2.2 %copy-done.2 = f32[1024,1024]{1,0:T(8,128)S(1)} copy-done((f32[1024,1024]{1,0:T(8,128)S(1)}, f32[1024,1024]{1,0:T(8,128)}, u32[]{:S(2)}) %copy-start.2) | copy-done | bytes 4194328
  101.3 1.1 gate.6.ya_ref
  102.3 2.2 %share.15 = bf16[256,512]{1,0:T(8,128)(2,1)S(1)} custom-call(bf16[256,1024]{1,0:T(8,128)(2,1)S(1)} %gate.6.ya_ref, bf16[256,1024]{1,0:T(8,128)(2,1)S(1)} %collective-permute-done.8.yb_ref, bf16[1024,256]{1,0:T(8,128)(2,1)} %get-tuple-element.10.refs_0_, bf16[1024,256]{1,0:T(8,128)(2,1)} %get-tuple-element.9.refs_1_, ...), custom_call_target="tpu_custom_call" | custom-call | flops 536870912 | bytes 2097152 | tf_op jit(solution)/shard_map/share/pallas_call | solution.py:186
  105.3 3.2 %collective-permute-done.7.yb_ref = bf16[256,1024]{1,0:T(8,128)(2,1)} collective-permute-done((bf16[256,1024]{1,0:T(8,128)(2,1)}, bf16[256,1024]{1,0:T(8,128)(2,1)}, u32[]{:S(2)}, u32[]{:S(2)}) %collective-permute-start.7) | collective-permute-done | bytes 524320 | tf_op jit(solution)/shard_map/ppermute | solution.py:238
  108.4 0.8 collective-permute-start.37
  109.2 4.6 %collective-permute-done.46.got_ref = bf16[256,512]{1,0:T(8,128)(2,1)S(1)} collective-permute-done((bf16[256,512]{1,0:T(8,128)(2,1)S(1)}, bf16[256,512]{1,0:T(8,128)(2,1)S(1)}, u32[]{:S(2)}, u32[]{:S(2)}) %collective-permute-start.46) | collective-permute-done | bytes 262176 | tf_op jit(solution)/shard_map/ppermute | solution.py:238
  115.1 1.5 collective-permute-start.20
  116.6 3.0 %collective-permute-done.16.refs_2_ = bf16[1024,256]{1,0:T(8,128)(2,1)S(1)} collective-permute-done((bf16[1024,256]{1,0:T(8,128)(2,1)}, bf16[1024,256]{1,0:T(8,128)(2,1)S(1)}, u32[]{:S(2)}, u32[]{:S(2)}) %collective-permute-start.16) | collective-permute-done | bytes 524320 | tf_op jit(solution)/shard_map/ppermute | solution.py:238
  119.7 1.5 collective-permute-start.28
  121.2 9.3 %collective-permute-done.37.refs_3_ = bf16[1024,256]{1,0:T(8,128)(2,1)S(1)} collective-permute-done((bf16[1024,256]{1,0:T(8,128)(2,1)}, bf16[1024,256]{1,0:T(8,128)(2,1)S(1)}, u32[]{:S(2)}, u32[]{:S(2)}) %collective-permute-start.37) | collective-permute-done | bytes 524320 | tf_op jit(solution)/shard_map/ppermute | solution.py:238
  131.0 0.8 copy-done.19
  131.8 1.5 collective-permute-start.10
  133.9 2.2 %share.14 = bf16[256,512]{1,0:T(8,128)(2,1)S(1)} custom-call(bf16[256,1024]{1,0:T(8,128)(2,1)S(1)} %gate.6.ya_ref, bf16[256,1024]{1,0:T(8,128)(2,1)S(1)} %collective-permute-done.8.yb_ref, bf16[1024,256]{1,0:T(8,128)(2,1)} %collective-permute-done.41.refs_0_, bf16[1024,256]{1,0:T(8,128)(2,1)} %collective-permute-done.42.refs_1_, ...), custom_call_target="tpu_custom_call" | custom-call | flops 536870912 | bytes 2097152 | tf_op jit(solution)/shard_map/share/pallas_call | solution.py:186
  136.1 5.3 %collective-permute-done.28.refs_2_ = bf16[1024,256]{1,0:T(8,128)(2,1)} collective-permute-done((bf16[1024,256]{1,0:T(8,128)(2,1)}, bf16[1024,256]{1,0:T(8,128)(2,1)}, u32[]{:S(2)}, u32[]{:S(2)}) %collective-permute-start.28) | collective-permute-done | bytes 524320 | tf_op jit(solution)/shard_map/ppermute | solution.py:238
  141.4 0.8 copy-done.17
  142.3 0.8 copy-done.21
  143.6 8.2 %collective-permute-done.10.refs_0_ = bf16[1024,256]{1,0:T(8,128)(2,1)} collective-permute-done((bf16[1024,256]{1,0:T(8,128)(2,1)}, bf16[1024,256]{1,0:T(8,128)(2,1)}, u32[]{:S(2)}, u32[]{:S(2)}) %collective-permute-start.10) | collective-permute-done | bytes 524320 | tf_op jit(solution)/shard_map/ppermute | solution.py:238
  151.8 1.6 collective-permute-start.17
  155.5 0.8 copy-done.27
  157.6 8.7 %collective-permute-done.17.refs_2_ = bf16[1024,256]{1,0:T(8,128)(2,1)} collective-permute-done((bf16[1024,256]{1,0:T(8,128)(2,1)S(1)}, bf16[1024,256]{1,0:T(8,128)(2,1)}, u32[]{:S(2)}, u32[]{:S(2)}) %collective-permute-start.17) | collective-permute-done | bytes 524320 | tf_op jit(solution)/shard_map/ppermute | solution.py:238
  166.3 2.0 collective-permute-done.21.refs_3_
  168.2 2.2 %copy-done.3 = f32[1024,1024]{1,0:T(8,128)S(1)} copy-done((f32[1024,1024]{1,0:T(8,128)S(1)}, f32[1024,1024]{1,0:T(8,128)}, u32[]{:S(2)}) %copy-start.3) | copy-done | bytes 4194328
  170.4 1.1 gate.4.ya_ref
  171.6 2.0 share.13
  173.7 3.2 %finish.8.refs_4_ = bf16[256,4096]{1,0:T(8,128)(2,1)} custom-call(s32[1]{0:T(128)} %bitcast.13.place_ref, bf16[256,1024]{1,0:T(8,128)(2,1)S(1)} %gate.4.ya_ref, bf16[256,1024]{1,0:T(8,128)(2,1)} %collective-permute-done.7.yb_ref, bf16[256,512]{1,0:T(8,128)(2,1)S(1)} %copy-done.30, bf16[1024,256]{1,0:T(8,128)(2,1)} %get-tuple-element.10.refs_0_, ...), custom_call_target="tpu_custom_call" | custom-call | flops 536870912 | bytes 2097152 | tf_op jit(solution)/shard_map/finish/pallas_call | solution.py:219
  177.8 2.1 collective-permute-start.39
  179.8 2.1 share.11
  182.3 1.8 share.10
  184.1 1.7 collective-permute-start.31
  185.8 2.2 %share.9 = bf16[256,512]{1,0:T(8,128)(2,1)S(1)} custom-call(bf16[256,1024]{1,0:T(8,128)(2,1)S(1)} %gate.6.ya_ref, bf16[256,1024]{1,0:T(8,128)(2,1)S(1)} %collective-permute-done.8.yb_ref, bf16[1024,256]{1,0:T(8,128)(2,1)} %collective-permute-done.10.refs_0_, bf16[1024,256]{1,0:T(8,128)(2,1)} %collective-permute-done.13.refs_1_, ...), custom_call_target="tpu_custom_call" | custom-call | flops 536870912 | bytes 2097152 | tf_op jit(solution)/shard_map/share/pallas_call | solution.py:186
  188.5 2.2 %share.8 = bf16[256,512]{1,0:T(8,128)(2,1)S(1)} custom-call(bf16[256,1024]{1,0:T(8,128)(2,1)S(1)} %gate.6.ya_ref, bf16[256,1024]{1,0:T(8,128)(2,1)S(1)} %collective-permute-done.8.yb_ref, bf16[1024,256]{1,0:T(8,128)(2,1)} %collective-permute-done.11.refs_0_, bf16[1024,256]{1,0:T(8,128)(2,1)} %collective-permute-done.14.refs_1_, ...), custom_call_target="tpu_custom_call" | custom-call | flops 536870912 | bytes 2097152 | tf_op jit(solution)/shard_map/share/pallas_call | solution.py:186
  190.7 1.7 collective-permute-start.23
  192.5 3.1 %finish.9.refs_4_ = bf16[256,4096]{1,0:T(8,128)(2,1)} custom-call(s32[1]{0:T(128)} %bitcast.12.place_ref, bf16[256,1024]{1,0:T(8,128)(2,1)S(1)} %gate.4.ya_ref, bf16[256,1024]{1,0:T(8,128)(2,1)} %collective-permute-done.7.yb_ref, bf16[256,512]{1,0:T(8,128)(2,1)S(1)} %copy-done.32, ...), custom_call_target="tpu_custom_call", output_to_operand_aliasing={{}: (8, {})} | custom-call | flops 536870912 | bytes 2097152 | tf_op jit(solution)/shard_map/finish/pallas_call | solution.py:219
  195.6 2.8 %finish.10.refs_4_ = bf16[256,4096]{1,0:T(8,128)(2,1)} custom-call(s32[1]{0:T(128)} %bitcast.11.place_ref, bf16[256,1024]{1,0:T(8,128)(2,1)S(1)} %gate.4.ya_ref, bf16[256,1024]{1,0:T(8,128)(2,1)} %collective-permute-done.7.yb_ref, bf16[256,512]{1,0:T(8,128)(2,1)S(1)} %collective-permute-done.40.got_ref, ...), custom_call_target="tpu_custom_call", output_to_operand_aliasing={{}: (8, {})} | custom-call | flops 536870912 | bytes 2097152 | tf_op jit(solution)/shard_map/finish/pallas_call | solution.py:219
  198.4 2.5 %finish.11.refs_4_ = bf16[256,4096]{1,0:T(8,128)(2,1)} custom-call(s32[1]{0:T(128)} %bitcast.10.place_ref, bf16[256,1024]{1,0:T(8,128)(2,1)S(1)} %gate.4.ya_ref, bf16[256,1024]{1,0:T(8,128)(2,1)} %collective-permute-done.7.yb_ref, bf16[256,512]{1,0:T(8,128)(2,1)S(1)} %collective-permute-done.39.got_ref, ...), custom_call_target="tpu_custom_call", output_to_operand_aliasing={{}: (8, {})} | custom-call | flops 536870912 | bytes 2097152 | tf_op jit(solution)/shard_map/finish/pallas_call | solution.py:219
  200.8 2.9 %finish.12.refs_4_ = bf16[256,4096]{1,0:T(8,128)(2,1)} custom-call(s32[1]{0:T(128)} %bitcast.9.place_ref, bf16[256,1024]{1,0:T(8,128)(2,1)S(1)} %gate.4.ya_ref, bf16[256,1024]{1,0:T(8,128)(2,1)} %collective-permute-done.7.yb_ref, bf16[256,512]{1,0:T(8,128)(2,1)S(1)} %collective-permute-done.32.got_ref, ...), custom_call_target="tpu_custom_call", output_to_operand_aliasing={{}: (8, {})} | custom-call | flops 536870912 | bytes 2097152 | tf_op jit(solution)/shard_map/finish/pallas_call | solution.py:219
  203.8 2.6 %finish.13.refs_4_ = bf16[256,4096]{1,0:T(8,128)(2,1)} custom-call(s32[1]{0:T(128)} %bitcast.8.place_ref, bf16[256,1024]{1,0:T(8,128)(2,1)S(1)} %gate.4.ya_ref, bf16[256,1024]{1,0:T(8,128)(2,1)} %collective-permute-done.7.yb_ref, bf16[256,512]{1,0:T(8,128)(2,1)S(1)} %collective-permute-done.31.got_ref, ...), custom_call_target="tpu_custom_call", output_to_operand_aliasing={{}: (8, {})} | custom-call | flops 536870912 | bytes 2097152 | tf_op jit(solution)/shard_map/finish/pallas_call | solution.py:219
  206.4 3.1 %finish.14.refs_4_ = bf16[256,4096]{1,0:T(8,128)(2,1)} custom-call(s32[1]{0:T(128)} %bitcast.7.place_ref, bf16[256,1024]{1,0:T(8,128)(2,1)S(1)} %gate.4.ya_ref, bf16[256,1024]{1,0:T(8,128)(2,1)} %collective-permute-done.7.yb_ref, bf16[256,512]{1,0:T(8,128)(2,1)S(1)} %collective-permute-done.24.got_ref, ...), custom_call_target="tpu_custom_call", output_to_operand_aliasing={{}: (8, {})} | custom-call | flops 536870912 | bytes 2097152 | tf_op jit(solution)/shard_map/finish/pallas_call | solution.py:219
  209.5 1.0 collective-permute-done.23.got_ref
  210.5 3.1 %finish.15 = bf16[256,4096]{1,0:T(8,128)(2,1)} custom-call(s32[1]{0:T(128)} %bitcast.place_ref, bf16[256,1024]{1,0:T(8,128)(2,1)S(1)} %gate.4.ya_ref, bf16[256,1024]{1,0:T(8,128)(2,1)} %collective-permute-done.7.yb_ref, bf16[256,512]{1,0:T(8,128)(2,1)S(1)} %collective-permute-done.23.got_ref, ...), custom_call_target="tpu_custom_call", output_to_operand_aliasing={{}: (8, {})} | custom-call | flops 536870912 | bytes 2097152 | tf_op jit(solution)/shard_map/finish/pallas_call | solution.py:219
  (132 shorter events, 12.2 us)
Async XLA Ops:
  0.0 6.5 %copy-start.33 = (f32[64,16]{0,1:T(8,128)S(1)}, f32[64,16]{0,1:T(8,128)}, u32[]{:S(2)}) copy-start(f32[64,16]{0,1:T(8,128)} %param.9) | copy-start | bytes 12292
  0.0 6.9 %copy-start.5 = (bf16[1024,1024]{1,0:T(8,128)(2,1)S(1)}, bf16[1024,1024]{1,0:T(8,128)(2,1)}, u32[]{:S(2)}) copy-start(bf16[1024,1024]{1,0:T(8,128)(2,1)} %k_ref.1) | copy-start | bytes 6291460
  2.4 39.6 %collective-permute-start.15 = (bf16[1024,256]{1,0:T(8,128)(2,1)}, bf16[1024,256]{1,0:T(8,128)(2,1)}, u32[]{:S(2)}, u32[]{:S(2)}) collective-permute-start(bf16[1024,256]{1,0:T(8,128)(2,1)} %get-tuple-element.10.refs_0_), channel_id=1, source_target_pairs={{0,2},{1,3},{2,0},{3,1},{4,6},{5,7},{6,4},{7,5},{8,10},{9,11},{10,... | collective-permute-start | bytes 1572872 | tf_op jit(solution)/shard_map/ppermute | solution.py:238
  6.4 55.8 %collective-permute-start.19 = (bf16[1024,256]{1,0:T(8,128)(2,1)}, bf16[1024,256]{1,0:T(8,128)(2,1)}, u32[]{:S(2)}, u32[]{:S(2)}) collective-permute-start(bf16[1024,256]{1,0:T(8,128)(2,1)} %get-tuple-element.9.refs_1_), channel_id=1, source_target_pairs={{0,2},{1,3},{2,0},{3,1},{4,6},{5,7},{6,4},{7,5},{8,10},{9,11},{10,... | collective-permute-start | bytes 1572872 | tf_op jit(solution)/shard_map/ppermute | solution.py:238
  6.5 55.8 %collective-permute-start.41 = (bf16[1024,256]{1,0:T(8,128)(2,1)}, bf16[1024,256]{1,0:T(8,128)(2,1)}, u32[]{:S(2)}, u32[]{:S(2)}) collective-permute-start(bf16[1024,256]{1,0:T(8,128)(2,1)} %get-tuple-element.10.refs_0_), channel_id=1, source_target_pairs={{0,4},{4,0},{8,12},{12,8},{16,20},{20,16},{24,28},{28,24},{1,5},{5... | collective-permute-start | bytes 1572872 | tf_op jit(solution)/shard_map/ppermute | solution.py:238
  8.5 35.4 %copy-start.34 = (f32[64,16]{0,1:T(8,128)S(1)}, f32[64,16]{0,1:T(8,128)}, u32[]{:S(2)}) copy-start(f32[64,16]{0,1:T(8,128)} %param.10) | copy-start | bytes 12292
  12.2 2.3 %collective-permute-start = (bf16[1,16,1024]{2,1,0:T(8,128)(2,1)S(1)}, bf16[1,16,1024]{2,1,0:T(8,128)(2,1)S(1)}, u32[]{:S(2)}, u32[]{:S(2)}) collective-permute-start(bf16[1,16,1024]{2,1,0:T(8,128)(2,1)S(1)} %bitcast.14), channel_id=1, source_target_pairs={{0,4},{4,0},{8,12},{12,8},{16,20},{20,16},{24,28},{28,24},{1,5},{5... | collective-permute-start | bytes 98312 | tf_op jit(solution)/shard_map/ppermute | solution.py:238
  12.8 3.9 %collective-permute-start.1 = (bf16[1,16,1024]{2,1,0:T(8,128)(2,1)S(1)}, bf16[1,16,1024]{2,1,0:T(8,128)(2,1)S(1)}, u32[]{:S(2)}, u32[]{:S(2)}) collective-permute-start(bf16[1,16,1024]{2,1,0:T(8,128)(2,1)S(1)} %bitcast.15), channel_id=1, source_target_pairs={{0,8},{4,12},{8,0},{12,4},{16,24},{20,28},{24,16},{28,20},{1,9},{5... | collective-permute-start | bytes 98312 | tf_op jit(solution)/shard_map/ppermute | solution.py:238
  14.6 3.9 %collective-permute-start.2 = (bf16[1,16,1024]{2,1,0:T(8,128)(2,1)S(1)}, bf16[1,16,1024]{2,1,0:T(8,128)(2,1)S(1)}, u32[]{:S(2)}, u32[]{:S(2)}) collective-permute-start(bf16[1,16,1024]{2,1,0:T(8,128)(2,1)S(1)} %bitcast.16), channel_id=1, source_target_pairs={{0,12},{4,8},{8,4},{12,0},{16,28},{20,24},{24,20},{28,16},{1,13},{... | collective-permute-start | bytes 98312 | tf_op jit(solution)/shard_map/ppermute | solution.py:238
  16.7 3.9 %collective-permute-start.3 = (bf16[1,16,1024]{2,1,0:T(8,128)(2,1)S(1)}, bf16[1,16,1024]{2,1,0:T(8,128)(2,1)S(1)}, u32[]{:S(2)}, u32[]{:S(2)}) collective-permute-start(bf16[1,16,1024]{2,1,0:T(8,128)(2,1)S(1)} %bitcast.17), channel_id=1, source_target_pairs={{0,16},{4,20},{8,24},{12,28},{16,0},{20,4},{24,8},{28,12},{1,17},{... | collective-permute-start | bytes 98312 | tf_op jit(solution)/shard_map/ppermute | solution.py:238
  18.5 5.2 %collective-permute-start.4 = (bf16[1,16,1024]{2,1,0:T(8,128)(2,1)S(1)}, bf16[1,16,1024]{2,1,0:T(8,128)(2,1)S(1)}, u32[]{:S(2)}, u32[]{:S(2)}) collective-permute-start(bf16[1,16,1024]{2,1,0:T(8,128)(2,1)S(1)} %bitcast.18), channel_id=1, source_target_pairs={{0,20},{4,16},{8,28},{12,24},{16,4},{20,0},{24,12},{28,8},{1,21},{... | collective-permute-start | bytes 98312 | tf_op jit(solution)/shard_map/ppermute | solution.py:238
  20.6 5.0 %collective-permute-start.5 = (bf16[1,16,1024]{2,1,0:T(8,128)(2,1)S(1)}, bf16[1,16,1024]{2,1,0:T(8,128)(2,1)S(1)}, u32[]{:S(2)}, u32[]{:S(2)}) collective-permute-start(bf16[1,16,1024]{2,1,0:T(8,128)(2,1)S(1)} %bitcast.19), channel_id=1, source_target_pairs={{0,24},{4,28},{8,16},{12,20},{16,8},{20,12},{24,0},{28,4},{1,25},{... | collective-permute-start | bytes 98312 | tf_op jit(solution)/shard_map/ppermute | solution.py:238
  23.7 4.2 %collective-permute-start.6 = (bf16[1,16,1024]{2,1,0:T(8,128)(2,1)S(1)}, bf16[1,16,1024]{2,1,0:T(8,128)(2,1)S(1)}, u32[]{:S(2)}, u32[]{:S(2)}) collective-permute-start(bf16[1,16,1024]{2,1,0:T(8,128)(2,1)S(1)} %bitcast.20), channel_id=1, source_target_pairs={{0,28},{4,24},{8,20},{12,16},{16,12},{20,8},{24,4},{28,0},{1,29},{... | collective-permute-start | bytes 98312 | tf_op jit(solution)/shard_map/ppermute | solution.py:238
  25.6 38.3 %collective-permute-start.42 = (bf16[1024,256]{1,0:T(8,128)(2,1)}, bf16[1024,256]{1,0:T(8,128)(2,1)}, u32[]{:S(2)}, u32[]{:S(2)}) collective-permute-start(bf16[1024,256]{1,0:T(8,128)(2,1)} %get-tuple-element.9.refs_1_), channel_id=1, source_target_pairs={{0,4},{4,0},{8,12},{12,8},{16,20},{20,16},{24,28},{28,24},{1,5},{5... | collective-permute-start | bytes 1572872 | tf_op jit(solution)/shard_map/ppermute | solution.py:238
  27.9 40.5 %collective-permute-start.9 = (bf16[1024,256]{1,0:T(8,128)(2,1)}, bf16[1024,256]{1,0:T(8,128)(2,1)}, u32[]{:S(2)}, u32[]{:S(2)}) collective-permute-start(bf16[1024,256]{1,0:T(8,128)(2,1)} %get-tuple-element.10.refs_0_), channel_id=1, source_target_pairs={{0,8},{4,12},{8,0},{12,4},{16,24},{20,28},{24,16},{28,20},{1,9},{5... | collective-permute-start | bytes 1572872 | tf_op jit(solution)/shard_map/ppermute | solution.py:238
  42.0 29.3 %collective-permute-start.34 = (bf16[1024,256]{1,0:T(8,128)(2,1)}, bf16[1024,256]{1,0:T(8,128)(2,1)}, u32[]{:S(2)}, u32[]{:S(2)}) collective-permute-start(bf16[1024,256]{1,0:T(8,128)(2,1)} %get-tuple-element.9.refs_1_), channel_id=1, source_target_pairs={{0,8},{4,12},{8,0},{12,4},{16,24},{20,28},{24,16},{28,20},{1,9},{5... | collective-permute-start | bytes 1572872 | tf_op jit(solution)/shard_map/ppermute | solution.py:238
  46.4 13.8 %copy-start.4 = (bf16[1024,1024]{1,0:T(8,128)(2,1)S(1)}, bf16[1024,1024]{1,0:T(8,128)(2,1)}, u32[]{:S(2)}) copy-start(bf16[1024,1024]{1,0:T(8,128)(2,1)} %q_ref.7) | copy-start | bytes 6291460
  62.2 36.8 %collective-permute-start.8 = (bf16[256,1024]{1,0:T(8,128)(2,1)S(1)}, bf16[256,1024]{1,0:T(8,128)(2,1)S(1)}, u32[]{:S(2)}, u32[]{:S(2)}) collective-permute-start(bf16[256,1024]{1,0:T(8,128)(2,1)S(1)} %gate.7), channel_id=1, source_target_pairs={{0,2},{1,3},{2,0},{3,1},{4,6},{5,7},{6,4},{7,5},{8,10},{9,11},{10,... | collective-permute-start | bytes 1572872 | tf_op jit(solution)/shard_map/ppermute | solution.py:238
  62.3 42.3 %collective-permute-start.12 = (bf16[1024,256]{1,0:T(8,128)(2,1)}, bf16[1024,256]{1,0:T(8,128)(2,1)}, u32[]{:S(2)}, u32[]{:S(2)}) collective-permute-start(bf16[1024,256]{1,0:T(8,128)(2,1)} %get-tuple-element.9.refs_1_), channel_id=1, source_target_pairs={{0,16},{4,20},{8,24},{12,28},{16,0},{20,4},{24,8},{28,12},{1,17},{... | collective-permute-start | bytes 1572872 | tf_op jit(solution)/shard_map/ppermute | solution.py:238
  63.8 40.8 %collective-permute-start.25 = (bf16[1024,256]{1,0:T(8,128)(2,1)}, bf16[1024,256]{1,0:T(8,128)(2,1)}, u32[]{:S(2)}, u32[]{:S(2)}) collective-permute-start(bf16[1024,256]{1,0:T(8,128)(2,1)} %get-tuple-element.10.refs_0_), channel_id=1, source_target_pairs={{0,16},{4,20},{8,24},{12,28},{16,0},{20,4},{24,8},{28,12},{1,17},{... | collective-permute-start | bytes 1572872 | tf_op jit(solution)/shard_map/ppermute | solution.py:238
  68.4 40.0 %collective-permute-start.7 = (bf16[256,1024]{1,0:T(8,128)(2,1)}, bf16[256,1024]{1,0:T(8,128)(2,1)}, u32[]{:S(2)}, u32[]{:S(2)}) collective-permute-start(bf16[256,1024]{1,0:T(8,128)(2,1)} %gate.5), channel_id=1, source_target_pairs={{0,2},{1,3},{2,0},{3,1},{4,6},{5,7},{6,4},{7,5},{8,10},{9,11},{10,... | collective-permute-start | bytes 1572872 | tf_op jit(solution)/shard_map/ppermute | solution.py:238
  71.3 43.4 %collective-permute-start.43 = (bf16[1024,256]{1,0:T(8,128)(2,1)}, bf16[1024,256]{1,0:T(8,128)(2,1)}, u32[]{:S(2)}, u32[]{:S(2)}) collective-permute-start(bf16[1024,256]{1,0:T(8,128)(2,1)} %collective-permute-done.15.refs_2_), channel_id=1, source_target_pairs={{0,4},{4,0},{8,12},{12,8},{16,20},{20,16},{24,28},{28,24},{1,5},{5... | collective-permute-start | bytes 1572872 | tf_op jit(solution)/shard_map/ppermute | solution.py:238
  99.1 16.0 %collective-permute-start.44 = (bf16[1024,256]{1,0:T(8,128)(2,1)}, bf16[1024,256]{1,0:T(8,128)(2,1)}, u32[]{:S(2)}, u32[]{:S(2)}) collective-permute-start(bf16[1024,256]{1,0:T(8,128)(2,1)} %collective-permute-done.19.refs_3_), channel_id=1, source_target_pairs={{0,4},{4,0},{8,12},{12,8},{16,20},{20,16},{24,28},{28,24},{1,5},{5... | collective-permute-start | bytes 1572872 | tf_op jit(solution)/shard_map/ppermute | solution.py:238
  104.6 9.3 %collective-permute-start.46 = (bf16[256,512]{1,0:T(8,128)(2,1)S(1)}, bf16[256,512]{1,0:T(8,128)(2,1)S(1)}, u32[]{:S(2)}, u32[]{:S(2)}) collective-permute-start(bf16[256,512]{1,0:T(8,128)(2,1)S(1)} %share.15), channel_id=1, source_target_pairs={{0,1},{1,0},{2,3},{3,2},{4,5},{5,4},{6,7},{7,6},{8,9},{9,8},{10,11... | collective-permute-start | bytes 786440 | tf_op jit(solution)/shard_map/ppermute | solution.py:238
  104.7 15.0 %collective-permute-start.16 = (bf16[1024,256]{1,0:T(8,128)(2,1)}, bf16[1024,256]{1,0:T(8,128)(2,1)S(1)}, u32[]{:S(2)}, u32[]{:S(2)}) collective-permute-start(bf16[1024,256]{1,0:T(8,128)(2,1)} %collective-permute-done.15.refs_2_), channel_id=1, source_target_pairs={{0,8},{4,12},{8,0},{12,4},{16,24},{20,28},{24,16},{28,20},{1,9},{5... | collective-permute-start | bytes 1572872 | tf_op jit(solution)/shard_map/ppermute | solution.py:238
  108.4 22.1 %collective-permute-start.37 = (bf16[1024,256]{1,0:T(8,128)(2,1)}, bf16[1024,256]{1,0:T(8,128)(2,1)S(1)}, u32[]{:S(2)}, u32[]{:S(2)}) collective-permute-start(bf16[1024,256]{1,0:T(8,128)(2,1)} %collective-permute-done.19.refs_3_), channel_id=1, source_target_pairs={{0,8},{4,12},{8,0},{12,4},{16,24},{20,28},{24,16},{28,20},{1,9},{5... | collective-permute-start | bytes 1572872 | tf_op jit(solution)/shard_map/ppermute | solution.py:238
  114.6 15.9 %collective-permute-start.33 = (bf16[1024,256]{1,0:T(8,128)(2,1)}, bf16[1024,256]{1,0:T(8,128)(2,1)S(1)}, u32[]{:S(2)}, u32[]{:S(2)}) collective-permute-start(bf16[1024,256]{1,0:T(8,128)(2,1)} %collective-permute-done.9.refs_0_), channel_id=1, source_target_pairs={{0,4},{4,0},{8,12},{12,8},{16,20},{20,16},{24,28},{28,24},{1,5},{5... | collective-permute-start | bytes 1572872 | tf_op jit(solution)/shard_map/ppermute | solution.py:238
  114.7 16.4 %collective-permute-start.35 = (bf16[1024,256]{1,0:T(8,128)(2,1)}, bf16[1024,256]{1,0:T(8,128)(2,1)S(1)}, u32[]{:S(2)}, u32[]{:S(2)}) collective-permute-start(bf16[1024,256]{1,0:T(8,128)(2,1)} %collective-permute-done.34.refs_1_), channel_id=1, source_target_pairs={{0,4},{4,0},{8,12},{12,8},{16,20},{20,16},{24,28},{28,24},{1,5},{5... | collective-permute-start | bytes 1572872 | tf_op jit(solution)/shard_map/ppermute | solution.py:238
  115.1 18.2 %collective-permute-start.20 = (bf16[1024,256]{1,0:T(8,128)(2,1)}, bf16[1024,256]{1,0:T(8,128)(2,1)S(1)}, u32[]{:S(2)}, u32[]{:S(2)}) collective-permute-start(bf16[1024,256]{1,0:T(8,128)(2,1)} %collective-permute-done.19.refs_3_), channel_id=1, source_target_pairs={{0,16},{4,20},{8,24},{12,28},{16,0},{20,4},{24,8},{28,12},{1,17},{... | collective-permute-start | bytes 1572872 | tf_op jit(solution)/shard_map/ppermute | solution.py:238
  119.7 32.1 %copy-start.9 = (bf16[1024,256]{1,0:T(8,128)(2,1)}, bf16[1024,256]{1,0:T(8,128)(2,1)S(1)}, u32[]{:S(2)}) copy-start(bf16[1024,256]{1,0:T(8,128)(2,1)S(1)} %collective-permute-done.16.refs_2_) | copy-start | bytes 1572868
  119.7 21.8 %collective-permute-start.28 = (bf16[1024,256]{1,0:T(8,128)(2,1)}, bf16[1024,256]{1,0:T(8,128)(2,1)}, u32[]{:S(2)}, u32[]{:S(2)}) collective-permute-start(bf16[1024,256]{1,0:T(8,128)(2,1)} %collective-permute-done.15.refs_2_), channel_id=1, source_target_pairs={{0,16},{4,20},{8,24},{12,28},{16,0},{20,4},{24,8},{28,12},{1,17},{... | collective-permute-start | bytes 1572872 | tf_op jit(solution)/shard_map/ppermute | solution.py:238
  130.5 37.7 %copy-start.15 = (bf16[1024,256]{1,0:T(8,128)(2,1)}, bf16[1024,256]{1,0:T(8,128)(2,1)S(1)}, u32[]{:S(2)}) copy-start(bf16[1024,256]{1,0:T(8,128)(2,1)S(1)} %collective-permute-done.37.refs_3_) | copy-start | bytes 1572868
  130.5 10.9 %collective-permute-start.27 = (bf16[1024,256]{1,0:T(8,128)(2,1)}, bf16[1024,256]{1,0:T(8,128)(2,1)S(1)}, u32[]{:S(2)}, u32[]{:S(2)}) collective-permute-start(bf16[1024,256]{1,0:T(8,128)(2,1)} %collective-permute-done.12.refs_1_), channel_id=1, source_target_pairs={{0,4},{4,0},{8,12},{12,8},{16,20},{20,16},{24,28},{28,24},{1,5},{5... | collective-permute-start | bytes 1572872 | tf_op jit(solution)/shard_map/ppermute | solution.py:238
  130.5 35.7 %copy-start.11 = (bf16[1024,256]{1,0:T(8,128)(2,1)}, bf16[1024,256]{1,0:T(8,128)(2,1)S(1)}, u32[]{:S(2)}) copy-start(bf16[1024,256]{1,0:T(8,128)(2,1)S(1)} %collective-permute-done.33.refs_0_) | copy-start | bytes 1572868
  130.5 11.7 %collective-permute-start.26 = (bf16[1024,256]{1,0:T(8,128)(2,1)}, bf16[1024,256]{1,0:T(8,128)(2,1)S(1)}, u32[]{:S(2)}, u32[]{:S(2)}) collective-permute-start(bf16[1024,256]{1,0:T(8,128)(2,1)} %collective-permute-done.25.refs_0_), channel_id=1, source_target_pairs={{0,4},{4,0},{8,12},{12,8},{16,20},{20,16},{24,28},{28,24},{1,5},{5... | collective-permute-start | bytes 1572872 | tf_op jit(solution)/shard_map/ppermute | solution.py:238
  131.8 20.0 %collective-permute-start.10 = (bf16[1024,256]{1,0:T(8,128)(2,1)}, bf16[1024,256]{1,0:T(8,128)(2,1)}, u32[]{:S(2)}, u32[]{:S(2)}) collective-permute-start(bf16[1024,256]{1,0:T(8,128)(2,1)} %collective-permute-done.9.refs_0_), channel_id=1, source_target_pairs={{0,16},{4,20},{8,24},{12,28},{16,0},{20,4},{24,8},{28,12},{1,17},{... | collective-permute-start | bytes 1572872 | tf_op jit(solution)/shard_map/ppermute | solution.py:238
  133.3 32.9 %copy-start.13 = (bf16[1024,256]{1,0:T(8,128)(2,1)}, bf16[1024,256]{1,0:T(8,128)(2,1)S(1)}, u32[]{:S(2)}) copy-start(bf16[1024,256]{1,0:T(8,128)(2,1)S(1)} %collective-permute-done.20.refs_3_) | copy-start | bytes 1572868
  133.3 18.5 %collective-permute-start.13 = (bf16[1024,256]{1,0:T(8,128)(2,1)}, bf16[1024,256]{1,0:T(8,128)(2,1)}, u32[]{:S(2)}, u32[]{:S(2)}) collective-permute-start(bf16[1024,256]{1,0:T(8,128)(2,1)} %collective-permute-done.12.refs_1_), channel_id=1, source_target_pairs={{0,8},{4,12},{8,0},{12,4},{16,24},{20,28},{24,16},{28,20},{1,9},{5... | collective-permute-start | bytes 1572872 | tf_op jit(solution)/shard_map/ppermute | solution.py:238
  141.4 12.0 %collective-permute-start.45 = (bf16[256,512]{1,0:T(8,128)(2,1)S(1)}, bf16[256,512]{1,0:T(8,128)(2,1)S(1)}, u32[]{:S(2)}, u32[]{:S(2)}) collective-permute-start(bf16[256,512]{1,0:T(8,128)(2,1)S(1)} %share.14), channel_id=1, source_target_pairs={{0,1},{1,0},{2,3},{3,2},{4,5},{5,4},{6,7},{7,6},{8,9},{9,8},{10,11... | collective-permute-start | bytes 786440 | tf_op jit(solution)/shard_map/ppermute | solution.py:238
  142.3 12.4 %collective-permute-start.36 = (bf16[1024,256]{1,0:T(8,128)(2,1)S(1)}, bf16[1024,256]{1,0:T(8,128)(2,1)S(1)}, u32[]{:S(2)}, u32[]{:S(2)}) collective-permute-start(bf16[1024,256]{1,0:T(8,128)(2,1)S(1)} %collective-permute-done.16.refs_2_), channel_id=1, source_target_pairs={{0,4},{4,0},{8,12},{12,8},{16,20},{20,16},{24,28},{28,24},{1,5},{5... | collective-permute-start | bytes 1572872 | tf_op jit(solution)/shard_map/ppermute | solution.py:238
  143.1 12.4 %collective-permute-start.38 = (bf16[1024,256]{1,0:T(8,128)(2,1)S(1)}, bf16[1024,256]{1,0:T(8,128)(2,1)S(1)}, u32[]{:S(2)}, u32[]{:S(2)}) collective-permute-start(bf16[1024,256]{1,0:T(8,128)(2,1)S(1)} %collective-permute-done.37.refs_3_), channel_id=1, source_target_pairs={{0,4},{4,0},{8,12},{12,8},{16,20},{20,16},{24,28},{28,24},{1,5},{5... | collective-permute-start | bytes 1572872 | tf_op jit(solution)/shard_map/ppermute | solution.py:238
  151.8 5.0 %collective-permute-start.30 = (bf16[1024,256]{1,0:T(8,128)(2,1)S(1)}, bf16[1024,256]{1,0:T(8,128)(2,1)S(1)}, u32[]{:S(2)}, u32[]{:S(2)}) collective-permute-start(bf16[1024,256]{1,0:T(8,128)(2,1)S(1)} %collective-permute-done.20.refs_3_), channel_id=1, source_target_pairs={{0,4},{4,0},{8,12},{12,8},{16,20},{20,16},{24,28},{28,24},{1,5},{5... | collective-permute-start | bytes 1572872 | tf_op jit(solution)/shard_map/ppermute | solution.py:238
  151.8 14.4 %collective-permute-start.17 = (bf16[1024,256]{1,0:T(8,128)(2,1)S(1)}, bf16[1024,256]{1,0:T(8,128)(2,1)}, u32[]{:S(2)}, u32[]{:S(2)}) collective-permute-start(bf16[1024,256]{1,0:T(8,128)(2,1)S(1)} %collective-permute-done.16.refs_2_), channel_id=1, source_target_pairs={{0,16},{4,20},{8,24},{12,28},{16,0},{20,4},{24,8},{28,12},{1,17},{... | collective-permute-start | bytes 1572872 | tf_op jit(solution)/shard_map/ppermute | solution.py:238
  154.1 14.1 %collective-permute-start.21 = (bf16[1024,256]{1,0:T(8,128)(2,1)S(1)}, bf16[1024,256]{1,0:T(8,128)(2,1)}, u32[]{:S(2)}, u32[]{:S(2)}) collective-permute-start(bf16[1024,256]{1,0:T(8,128)(2,1)S(1)} %collective-permute-done.20.refs_3_), channel_id=1, source_target_pairs={{0,8},{4,12},{8,0},{12,4},{16,24},{20,28},{24,16},{28,20},{1,9},{5... | collective-permute-start | bytes 1572872 | tf_op jit(solution)/shard_map/ppermute | solution.py:238
  155.4 18.1 %collective-permute-start.29 = (bf16[1024,256]{1,0:T(8,128)(2,1)}, bf16[1024,256]{1,0:T(8,128)(2,1)}, u32[]{:S(2)}, u32[]{:S(2)}) collective-permute-start(bf16[1024,256]{1,0:T(8,128)(2,1)} %collective-permute-done.28.refs_2_), channel_id=1, source_target_pairs={{0,4},{4,0},{8,12},{12,8},{16,20},{20,16},{24,28},{28,24},{1,5},{5... | collective-permute-start | bytes 1572872 | tf_op jit(solution)/shard_map/ppermute | solution.py:238
  156.3 21.5 %collective-permute-start.11 = (bf16[1024,256]{1,0:T(8,128)(2,1)}, bf16[1024,256]{1,0:T(8,128)(2,1)}, u32[]{:S(2)}, u32[]{:S(2)}) collective-permute-start(bf16[1024,256]{1,0:T(8,128)(2,1)} %collective-permute-done.10.refs_0_), channel_id=1, source_target_pairs={{0,4},{4,0},{8,12},{12,8},{16,20},{20,16},{24,28},{28,24},{1,5},{5... | collective-permute-start | bytes 1572872 | tf_op jit(solution)/shard_map/ppermute | solution.py:238
  157.6 24.3 %collective-permute-start.14 = (bf16[1024,256]{1,0:T(8,128)(2,1)}, bf16[1024,256]{1,0:T(8,128)(2,1)}, u32[]{:S(2)}, u32[]{:S(2)}) collective-permute-start(bf16[1024,256]{1,0:T(8,128)(2,1)} %collective-permute-done.13.refs_1_), channel_id=1, source_target_pairs={{0,4},{4,0},{8,12},{12,8},{16,20},{20,16},{24,28},{28,24},{1,5},{5... | collective-permute-start | bytes 1572872 | tf_op jit(solution)/shard_map/ppermute | solution.py:238
  166.2 17.8 %collective-permute-start.18 = (bf16[1024,256]{1,0:T(8,128)(2,1)}, bf16[1024,256]{1,0:T(8,128)(2,1)}, u32[]{:S(2)}, u32[]{:S(2)}) collective-permute-start(bf16[1024,256]{1,0:T(8,128)(2,1)} %collective-permute-done.17.refs_2_), channel_id=1, source_target_pairs={{0,4},{4,0},{8,12},{12,8},{16,20},{20,16},{24,28},{28,24},{1,5},{5... | collective-permute-start | bytes 1572872 | tf_op jit(solution)/shard_map/ppermute | solution.py:238
  168.2 19.9 %collective-permute-start.22 = (bf16[1024,256]{1,0:T(8,128)(2,1)}, bf16[1024,256]{1,0:T(8,128)(2,1)}, u32[]{:S(2)}, u32[]{:S(2)}) collective-permute-start(bf16[1024,256]{1,0:T(8,128)(2,1)} %collective-permute-done.21.refs_3_), channel_id=1, source_target_pairs={{0,4},{4,0},{8,12},{12,8},{16,20},{20,16},{24,28},{28,24},{1,5},{5... | collective-permute-start | bytes 1572872 | tf_op jit(solution)/shard_map/ppermute | solution.py:238
  173.6 17.1 %collective-permute-start.40 = (bf16[256,512]{1,0:T(8,128)(2,1)S(1)}, bf16[256,512]{1,0:T(8,128)(2,1)S(1)}, u32[]{:S(2)}, u32[]{:S(2)}) collective-permute-start(bf16[256,512]{1,0:T(8,128)(2,1)S(1)} %share.13), channel_id=1, source_target_pairs={{0,1},{1,0},{2,3},{3,2},{4,5},{5,4},{6,7},{7,6},{8,9},{9,8},{10,11... | collective-permute-start | bytes 786440 | tf_op jit(solution)/shard_map/ppermute | solution.py:238
  173.7 3.3 %copy-start.12 = (bf16[1024,256]{1,0:T(8,128)(2,1)S(1)}, bf16[1024,256]{1,0:T(8,128)(2,1)}, u32[]{:S(2)}) copy-start(bf16[1024,256]{1,0:T(8,128)(2,1)} %copy-done.11) | copy-start | bytes 1572868
  173.7 3.3 %copy-start.20 = (bf16[1024,256]{1,0:T(8,128)(2,1)S(1)}, bf16[1024,256]{1,0:T(8,128)(2,1)}, u32[]{:S(2)}) copy-start(bf16[1024,256]{1,0:T(8,128)(2,1)} %copy-done.19) | copy-start | bytes 1572868
  173.7 3.3 %copy-start.26 = (bf16[1024,256]{1,0:T(8,128)(2,1)S(1)}, bf16[1024,256]{1,0:T(8,128)(2,1)}, u32[]{:S(2)}) copy-start(bf16[1024,256]{1,0:T(8,128)(2,1)} %copy-done.25) | copy-start | bytes 1572868
  173.7 3.3 %copy-start.28 = (bf16[1024,256]{1,0:T(8,128)(2,1)S(1)}, bf16[1024,256]{1,0:T(8,128)(2,1)}, u32[]{:S(2)}) copy-start(bf16[1024,256]{1,0:T(8,128)(2,1)} %copy-done.27) | copy-start | bytes 1572868
  177.0 2.8 %copy-start.14 = (bf16[1024,256]{1,0:T(8,128)(2,1)S(1)}, bf16[1024,256]{1,0:T(8,128)(2,1)}, u32[]{:S(2)}) copy-start(bf16[1024,256]{1,0:T(8,128)(2,1)} %copy-done.13) | copy-start | bytes 1572868
  177.7 4.6 %copy-start.18 = (bf16[1024,256]{1,0:T(8,128)(2,1)S(1)}, bf16[1024,256]{1,0:T(8,128)(2,1)}, u32[]{:S(2)}) copy-start(bf16[1024,256]{1,0:T(8,128)(2,1)} %copy-done.17) | copy-start | bytes 1572868
  177.7 4.6 %copy-start.22 = (bf16[1024,256]{1,0:T(8,128)(2,1)S(1)}, bf16[1024,256]{1,0:T(8,128)(2,1)}, u32[]{:S(2)}) copy-start(bf16[1024,256]{1,0:T(8,128)(2,1)} %copy-done.21) | copy-start | bytes 1572868
  177.7 4.6 %copy-start.24 = (bf16[1024,256]{1,0:T(8,128)(2,1)S(1)}, bf16[1024,256]{1,0:T(8,128)(2,1)}, u32[]{:S(2)}) copy-start(bf16[1024,256]{1,0:T(8,128)(2,1)} %copy-done.23) | copy-start | bytes 1572868
  177.8 20.6 %collective-permute-start.39 = (bf16[256,512]{1,0:T(8,128)(2,1)S(1)}, bf16[256,512]{1,0:T(8,128)(2,1)S(1)}, u32[]{:S(2)}, u32[]{:S(2)}) collective-permute-start(bf16[256,512]{1,0:T(8,128)(2,1)S(1)} %share.12), channel_id=1, source_target_pairs={{0,1},{1,0},{2,3},{3,2},{4,5},{5,4},{6,7},{7,6},{8,9},{9,8},{10,11... | collective-permute-start | bytes 786440 | tf_op jit(solution)/shard_map/ppermute | solution.py:238
  181.9 18.9 %collective-permute-start.32 = (bf16[256,512]{1,0:T(8,128)(2,1)S(1)}, bf16[256,512]{1,0:T(8,128)(2,1)S(1)}, u32[]{:S(2)}, u32[]{:S(2)}) collective-permute-start(bf16[256,512]{1,0:T(8,128)(2,1)S(1)} %share.11), channel_id=1, source_target_pairs={{0,1},{1,0},{2,3},{3,2},{4,5},{5,4},{6,7},{7,6},{8,9},{9,8},{10,11... | collective-permute-start | bytes 786440 | tf_op jit(solution)/shard_map/ppermute | solution.py:238
  184.1 19.7 %collective-permute-start.31 = (bf16[256,512]{1,0:T(8,128)(2,1)S(1)}, bf16[256,512]{1,0:T(8,128)(2,1)S(1)}, u32[]{:S(2)}, u32[]{:S(2)}) collective-permute-start(bf16[256,512]{1,0:T(8,128)(2,1)S(1)} %share.10), channel_id=1, source_target_pairs={{0,1},{1,0},{2,3},{3,2},{4,5},{5,4},{6,7},{7,6},{8,9},{9,8},{10,11... | collective-permute-start | bytes 786440 | tf_op jit(solution)/shard_map/ppermute | solution.py:238
  188.1 4.4 %copy-start.32 = (bf16[256,512]{1,0:T(8,128)(2,1)S(1)}, bf16[256,512]{1,0:T(8,128)(2,1)}, u32[]{:S(2)}) copy-start(bf16[256,512]{1,0:T(8,128)(2,1)} %copy-done.31) | copy-start | bytes 786436
  188.1 18.3 %collective-permute-start.24 = (bf16[256,512]{1,0:T(8,128)(2,1)S(1)}, bf16[256,512]{1,0:T(8,128)(2,1)S(1)}, u32[]{:S(2)}, u32[]{:S(2)}) collective-permute-start(bf16[256,512]{1,0:T(8,128)(2,1)S(1)} %share.9), channel_id=1, source_target_pairs={{0,1},{1,0},{2,3},{3,2},{4,5},{5,4},{6,7},{7,6},{8,9},{9,8},{10,11... | collective-permute-start | bytes 786440 | tf_op jit(solution)/shard_map/ppermute | solution.py:238
  190.7 19.7 %collective-permute-start.23 = (bf16[256,512]{1,0:T(8,128)(2,1)S(1)}, bf16[256,512]{1,0:T(8,128)(2,1)S(1)}, u32[]{:S(2)}, u32[]{:S(2)}) collective-permute-start(bf16[256,512]{1,0:T(8,128)(2,1)S(1)} %share.8), channel_id=1, source_target_pairs={{0,1},{1,0},{2,3},{3,2},{4,5},{5,4},{6,7},{7,6},{8,9},{9,8},{10,11... | collective-permute-start | bytes 786440 | tf_op jit(solution)/shard_map/ppermute | solution.py:238
  (18 other events, 23.6 us)

commit v2 on v0

v2 whole, which is shorter than its diff:
```python
import functools

import jax
import jax.numpy as jnp
from jax import lax
from jax.experimental import pallas as pl
from jax.experimental.pallas import tpu as pltpu
from jax.sharding import PartitionSpec as P

SUB = 256
TILE = 128
F32 = jnp.float32
BF16 = jnp.bfloat16


def dot32(a, b):
    return jnp.dot(a, b, preferred_element_type=F32)


def own_mask(rows, cols, modes, width):
    r = lax.broadcasted_iota(jnp.int32, (rows, cols), 0) // modes
    c = lax.broadcasted_iota(jnp.int32, (rows, cols), 1) // width
    return r == c


def as_column(table, first, count):
    modes, groups = table.shape
    rows = jnp.broadcast_to(table[None], (count, modes, groups)).reshape(count * modes, groups)
    group = lax.broadcasted_iota(jnp.int32, rows.shape, 0) // modes + first
    pick = group == lax.broadcasted_iota(jnp.int32, rows.shape, 1)
    return jnp.sum(jnp.where(pick, rows, 0.0), axis=1, keepdims=True)


def as_row(column):
    size = column.shape[0]
    same = lax.broadcasted_iota(jnp.int32, (size, size), 0)
    same = same == lax.broadcasted_iota(jnp.int32, (size, size), 1)
    return jnp.sum(jnp.where(same, column, 0.0), axis=0, keepdims=True)


VMEM_BYTES = 56 << 20
SHORT = pl.CostEstimate(flops=1, bytes_accessed=1, transcendentals=0)
LONG = pl.CostEstimate(flops=1 << 36, bytes_accessed=1 << 28, transcendentals=0)


def range_state_kernel(width, me_ref, k_ref, v_ref, rate_ref, u_ref, f_ref):
    u = (k_ref[...].astype(F32) * v_ref[...].astype(F32)).astype(BF16)
    u_ref[...] = u
    toks, cols = u.shape
    modes = rate_ref.shape[0]
    count = cols // width
    rate = as_column(rate_ref[...], pl.program_id(0) * count, count)
    rows = rate.shape[0]
    left = (SUB - 1) - lax.broadcasted_iota(jnp.int32, (rows, SUB), 1)
    inject = jnp.exp(-rate * left.astype(F32)).astype(BF16)
    decay = jnp.exp(-rate * SUB)
    sums = dot32(inject, u[:SUB])
    for n in range(1, toks // SUB):
        sums = decay * sums + dot32(inject, u[n * SUB : (n + 1) * SUB])
    sums = jnp.where(own_mask(rows, cols, modes, width), sums, 0.0)
    for to in range(f_ref.shape[0]):
        lag = to - 1 - me_ref[0]
        weight = jnp.exp(-rate * (jnp.maximum(lag, 0) * toks).astype(F32))
        there = (weight * sums).reshape(rows // modes, modes, cols)
        f_ref[to] = jnp.where(lag >= 0, jnp.sum(there, axis=0), 0.0).astype(BF16)


def range_state(me, key_feat, value_feat, rates, seq_size, width):
    toks, chans = key_feat.shape
    modes = rates.shape[0]
    step = 256
    feat = pl.BlockSpec((toks, step), lambda i, p: (0, i))
    return pl.pallas_call(
        functools.partial(range_state_kernel, width),
        grid_spec=pltpu.PrefetchScalarGridSpec(
            num_scalar_prefetch=1,
            grid=(chans // step,),
            in_specs=[feat, feat, pl.BlockSpec(rates.shape, lambda i, p: (0, 0))],
            out_specs=[feat, pl.BlockSpec((seq_size, modes, step), lambda i, p: (0, 0, i))],
        ),
        out_shape=[
            jax.ShapeDtypeStruct((toks, chans), BF16),
            jax.ShapeDtypeStruct((seq_size, modes, chans), BF16),
        ],
        compiler_params=pltpu.CompilerParams(vmem_limit_bytes=VMEM_BYTES),
        cost_estimate=SHORT,
        name="range_state",
    )(me, key_feat, value_feat, rates)


def local_kernel(width, u_ref, rate_ref, res_ref, z_ref, rows_ref, taps_ref, split_ref):
    modes, groups = rate_ref.shape[0], TILE // width
    rows = groups * modes
    rate, res = (as_column(r[...], pl.program_id(0) * groups, groups) for r in (rate_ref, res_ref))
    rate_row, res_row = as_row(rate), as_row(res)
    rows_ref[0:1, :] = rate_row
    rows_ref[1:2, :] = res_row
    blocks = u_ref.shape[0] // SUB
    lag = 2 * SUB - lax.broadcasted_iota(jnp.int32, (rows, 2 * SUB), 1)
    lag = jnp.where(lag == 2 * SUB, 0, lag)
    terms = jnp.where(lag < SUB, res * jnp.exp(-rate * lag.astype(F32)), 0.0)
    wheel = jnp.sum(terms.reshape(groups, modes, 2 * SUB), axis=1)
    half = SUB // 2
    both = jnp.concatenate([u_ref[n * SUB : (n + 1) * SUB, :] for n in range(blocks)], axis=1)
    lane_group = (lax.broadcasted_iota(jnp.int32, (1, blocks * TILE), 1) % TILE) // width
    for g in range(groups):
        base = jnp.broadcast_to(wheel[g : g + 1], (half, 2 * SUB))
        low = pltpu.roll(base, half, 1, stride=1, stride_axis=0)[:, :SUB].astype(BF16)
        taps_ref[half:, g * SUB : (g + 1) * SUB] = low
        taps_ref[:half, g * SUB : g * SUB + half] = low[:, half:]
        taps_ref[:half, g * SUB + half : (g + 1) * SUB] = jnp.zeros((half, half), BF16)
        split_ref[g * SUB : (g + 1) * SUB, :] = both * (lane_group == g).astype(BF16)

    mask = own_mask(rows, TILE, modes, width)
    left = (SUB - 1) - lax.broadcasted_iota(jnp.int32, (rows, SUB), 1)
    inject = jnp.exp(-rate * left.astype(F32)).astype(BF16)
    sums = dot32(inject, both[:, : (blocks - 1) * TILE])
    decay = jnp.exp(-rate * SUB)
    state, starts = jnp.zeros((rows, TILE), F32), []
    for n in range(blocks - 1):
        own = jnp.where(mask, sums[:, n * TILE : (n + 1) * TILE], 0.0)
        state = decay * state + own
        starts.append(state.astype(BF16))
    after = lax.broadcasted_iota(jnp.int32, (SUB, rows), 0) + 1
    readout = (res_row * jnp.exp(-rate_row * after.astype(F32))).astype(BF16)
    carried = dot32(readout, jnp.concatenate(starts, axis=1))
    z = dot32(taps_ref[...], split_ref[...])
    z_ref[:SUB, :] = z[:, :TILE]
    for n in range(1, blocks):
        z_ref[n * SUB : (n + 1) * SUB, :] = (
            z[:, n * TILE : (n + 1) * TILE] + carried[:, (n - 1) * TILE : n * TILE]
        )


def local_conv(u, rates, residues, width):
    toks, chans = u.shape
    modes = rates.shape[0]
    groups = TILE // width
    rows = groups * modes
    table = pl.BlockSpec(rates.shape, lambda i: (0, 0))
    feat = pl.BlockSpec((toks, TILE), lambda i: (0, i))
    return pl.pallas_call(
        functools.partial(local_kernel, width),
        grid=(chans // TILE,),
        in_specs=[feat, table, table],
        out_specs=[feat, pl.BlockSpec((2, rows), lambda i: (0, i))],
        out_shape=[
            jax.ShapeDtypeStruct((toks, chans), F32),
            jax.ShapeDtypeStruct((2, rates.size), F32),
        ],
        scratch_shapes=[
            pltpu.VMEM((SUB, groups * SUB), BF16),
            pltpu.VMEM((groups * SUB, toks // SUB * TILE), BF16),
        ],
        compiler_params=pltpu.CompilerParams(vmem_limit_bytes=VMEM_BYTES),
        cost_estimate=SHORT,
        name="local_conv",
    )(u, rates, residues)


def gate_kernel(modes, width, counts, place_ref, z_ref, q_ref, rows_ref, state_ref, *y_refs):
    y_refs = list(zip(y_refs, counts))
    step = pl.program_id(0)
    entering = jnp.sum(state_ref[...].astype(F32), axis=0)
    first = place_ref[step] * SUB + 1
    rows = TILE // width * modes
    mask = own_mask(rows, TILE, modes, width)
    tiles = []
    for tile in range(q_ref.shape[1] // TILE):
        lanes = slice(tile * TILE, (tile + 1) * TILE)
        group = slice(tile * rows, (tile + 1) * rows)
        after = lax.broadcasted_iota(jnp.int32, (SUB, rows), 0) + first
        readout = (
            rows_ref[1:2, group] * jnp.exp(-rows_ref[0:1, group] * after.astype(F32))
        ).astype(BF16)
        spread = jnp.concatenate([entering[:, lanes]] * (TILE // width), axis=0)
        spread = jnp.where(mask, spread, 0.0).astype(BF16)
        z = z_ref[:, lanes] + dot32(readout, spread)
        tiles.append((q_ref[:, lanes].astype(F32) * z).astype(BF16))
    at = 0
    for y_ref, count in y_refs:

        @pl.when((step >= at) & (step < at + count))
        def _():
            y_ref[...] = jnp.concatenate(tiles, axis=1)

        at += count


def gate(places, counts, z, query_feat, rows, states, width):
    modes, chans = states.shape[1], query_feat.shape[1]
    whole = lambda a: pl.BlockSpec(a.shape, lambda i, p: (0,) * a.ndim)
    block = pl.BlockSpec((SUB, chans), lambda i, p: (p[i], 0))

    def result(first, count):
        return pl.BlockSpec((SUB, chans), lambda i, p: (jnp.clip(i - first, 0, count - 1), 0))

    return pl.pallas_call(
        functools.partial(gate_kernel, modes, width, counts),
        grid_spec=pltpu.PrefetchScalarGridSpec(
            num_scalar_prefetch=1,
            grid=(sum(counts),),
            in_specs=[block, block, whole(rows), whole(states)],
            out_specs=[result(sum(counts[:n]), count) for n, count in enumerate(counts)],
        ),
        out_shape=[jax.ShapeDtypeStruct((n * SUB, chans), BF16) for n in counts],
        compiler_params=pltpu.CompilerParams(vmem_limit_bytes=VMEM_BYTES),
        cost_estimate=SHORT,
        name="gate",
    )(places, z, query_feat, rows, states)


def share_kernel(sets, count, added, *refs):
    near = jnp.concatenate([r[...] for r in refs[:sets]], axis=0)
    far = jnp.concatenate([r[...] for r in refs[sets : 2 * sets]], axis=0)
    weights, outs = refs[2 * sets : 2 * sets + 2 * count], refs[2 * sets + 2 * count + added :]
    rows = near.shape[0] // len(outs)
    at = 0
    for wn, wf in zip(weights[:count], weights[count:]):
        cols = wn.shape[1]
        total = dot32(near, wn[...]) + dot32(far, wf[...])
        if added:
            total = total + refs[-len(outs) - 1][:, at : at + cols].astype(F32)
        total = total.astype(BF16)
        for i, out in enumerate(outs):
            out[:, at : at + cols] = total[i * rows : (i + 1) * rows]
        at += cols


def share(near, far, near_w, far_w, cols, parts=1, add=None, cost=SHORT):
    depth = near[0][0].shape[1]
    rows = lambda n: pl.BlockSpec((SUB, depth), lambda i: (n, 0))
    part = lambda col: pl.BlockSpec((depth, cols), lambda i: (0, col))
    whole = lambda *shape: pl.BlockSpec(shape, lambda i: (0, 0))
    height, total = len(near) * SUB, cols * len(near_w)
    extra = [] if add is None else [add]
    return pl.pallas_call(
        functools.partial(share_kernel, len(near), len(near_w), len(extra)),
        grid=(1,),
        in_specs=[rows(n) for _, n in near + far]
        + [part(col) for _, col in near_w + far_w]
        + [whole(*e.shape) for e in extra],
        out_specs=[whole(height // parts, total)] * parts,
        out_shape=[jax.ShapeDtypeStruct((height // parts, total), BF16)] * parts,
        compiler_params=pltpu.CompilerParams(vmem_limit_bytes=VMEM_BYTES),
        cost_estimate=cost,
        name="share",
    )(*[a for a, _ in near + far + near_w + far_w], *extra)


def place_kernel(spots, place_ref, *refs):
    out_ref, total_ref, sem = refs[-3:]
    cols = total_ref.shape[2]
    copies = []
    for j, spot in enumerate(spots):
        terms = [refs[i][:, n * cols : (n + 1) * cols] for i, n in spot]
        total = terms[0] if len(terms) == 1 else sum(t.astype(F32) for t in terms).astype(BF16)
        total_ref[j] = total
        to = pl.ds(pl.multiple_of(place_ref[j] * cols, cols), cols)
        copies.append(pltpu.make_async_copy(total_ref.at[j], out_ref.at[:, to], sem.at[j]))
        copies[-1].start()
    for copy in copies:
        copy.wait()


def place(places, terms, cols, out, all_cols, cost, awaited=()):
    arrays, spots = [], []
    for group in terms:
        spot = []
        for array, n in group:
            known = [i for i, a in enumerate(arrays) if a is array]
            if not known:
                known = [len(arrays)]
                arrays.append(array)
            spot.append((known[0], n))
        spots.append(spot)
    rows = arrays[0].shape[0]
    specs = [pl.BlockSpec(a.shape, lambda i, p: (0, 0)) for a in arrays]
    alias = {}
    arrays += awaited
    specs += [pl.BlockSpec(memory_space=pl.ANY)] * len(awaited)
    if out is not None:
        alias = {1 + len(arrays): 0}
        arrays.append(out)
        specs.append(pl.BlockSpec(memory_space=pl.ANY))
    return pl.pallas_call(
        functools.partial(place_kernel, spots),
        grid_spec=pltpu.PrefetchScalarGridSpec(
            num_scalar_prefetch=1,
            grid=(1,),
            in_specs=specs,
            out_specs=pl.BlockSpec(memory_space=pl.ANY),
            scratch_shapes=[
                pltpu.VMEM((len(spots), rows, cols), BF16),
                pltpu.SemaphoreType.DMA((len(spots),)),
            ],
        ),
        out_shape=jax.ShapeDtypeStruct((rows, all_cols), BF16),
        input_output_aliases=alias,
        compiler_params=pltpu.CompilerParams(vmem_limit_bytes=VMEM_BYTES),
        cost_estimate=cost,
        name="place",
    )(places, *arrays)


def flip(x, axis, size, bits):
    return lax.ppermute(x, axis, [(i, i ^ bits) for i in range(size)])


def after(x, *others):
    return lax.optimization_barrier((x, *others))[0]


def on_device(seq_size, ch_size, query_feat, key_feat, value_feat, decay_rates, residues, out_weight):
    toks, chans = query_feat.shape
    groups, modes = decay_rates.shape
    width = chans // groups
    piece_cols = out_weight.shape[1]
    all_cols = piece_cols * seq_size
    me = lax.axis_index("seq").astype(jnp.int32)
    plane = lax.axis_index("ch").astype(jnp.int32)
    far_plane = lambda x: flip(x, "ch", ch_size, 2)
    next_plane = lambda x: flip(x, "ch", ch_size, 1)

    rates, residues = decay_rates.T, residues.T
    u, ends = range_state(me.reshape(1), key_feat, value_feat, rates, seq_size, width)
    states = lax.all_to_all(ends, "seq", 0, 0, tiled=True)
    z, rows = local_conv(u, rates, residues, width)

    def gated(slots, counts, *hold):
        places = plane ^ jnp.array(slots, jnp.int32)
        return gate(places, counts, after(z, *hold), query_feat, rows, states, width)

    if seq_size != 8:
        y_3, near, y_2 = gated((3, 1, 0, 2), (1, 2, 1))
        near_w = lax.all_gather(out_weight, "seq", axis=1, tiled=True)
        far_w = lax.all_gather(far_plane(out_weight), "seq", axis=1, tiled=True)
        far_other, far_own = far_plane(y_3), far_plane(y_2)
        near_w, far_w = [(near_w, 0)], [(far_w, 0)]
        (part,) = share([(near, 0)], [(far_other, 0)], near_w, far_w, all_cols)
        (own,) = share([(near, 1)], [(far_own, 0)], near_w, far_w, all_cols)
        return (own.astype(F32) + next_plane(part).astype(F32)).astype(BF16)

    core = lambda x: flip(x, "seq", seq_size, 1)
    pairs = [(s * ch_size + c, (s ^ 1) * ch_size + (c ^ 1)) for s in range(seq_size) for c in range(ch_size)]
    next_cross = lambda x: lax.ppermute(x, ("seq", "ch"), pairs)
    across = lambda x: flip(x, "seq", seq_size, 2)
    along = lambda x: flip(x, "seq", seq_size, 4)

    half = piece_cols // 2
    first, second = slice(0, half), slice(half, None)

    n_a = out_weight[:, first]
    f_a = far_plane(n_a)
    n_x, n_y = across(out_weight), along(out_weight)
    (y_3,) = gated((3,), (1,), n_x, n_y)

    y_far_other = far_plane(y_3)
    f_a = after(f_a, y_3)
    f_ax, f_ay = across(f_a), along(f_a)
    n_ac = along(after(n_x, f_a)[:, first])
    near, y_2 = gated((1, 0, 2), (2, 1), n_x, n_y, f_a)
    near_sib = core(near)
    n_b = after(out_weight, near)[:, second]
    y_far_other, f_ax, f_ay, n_ac, n_b = lax.optimization_barrier(
        (y_far_other, f_ax, f_ay, n_ac, n_b)
    )

    f_b = far_plane(n_b)
    far_other_sib = core(y_far_other)
    f_ac = along(after(f_ax, far_other_sib))
    n_bc = across(after(n_y, near_sib, far_other_sib)[:, second])
    near_w = [(out_weight, 0), (n_x, 0), (n_y, 0), (n_ac, 0)]
    near_w += [(out_weight, 1), (n_x, 1), (n_y, 1), (n_bc, 0)]
    far_w = [(f_a, 0), (f_ax, 0), (f_ay, 0)]
    near_other, near_own = [(near, 0), (near_sib, 0)], [(near, 1), (near_sib, 1)]
    far_other = [(y_far_other, 0), (far_other_sib, 0)]

    def products(near, far, pieces, **kw):
        return share(near, far, [near_w[i] for i in pieces], [far_w[i] for i in pieces], half, **kw)

    (ready_1,) = products(near_other, far_other, range(2))
    part_1 = next_plane(ready_1)

    f_b, f_ac, n_bc = lax.optimization_barrier((f_b, f_ac, n_bc))
    near_w[7] = (n_bc, 0)
    y_far_own = far_plane(after(y_2, f_b))
    f_bx, f_by, f_bc = across(f_b), along(f_b), flip(f_b, "seq", seq_size, 6)
    far_w += [(f_ac, 0), (f_b, 0)]
    (ready_2,) = products(near_other, far_other, range(2, 5))
    part_2 = next_plane(after(ready_2, part_1))
    far_w += [(after(f_bx, y_far_own), 0), (f_by, 0), (f_bc, 0)]
    mine, other = products(near_other, far_other, range(5, 8), parts=2, cost=LONG)
    part_3 = next_plane(mine), next_cross(other)

    far_own_sib = core(after(y_far_own, mine))
    far_own = [(y_far_own, 0), (far_own_sib, 0)]
    own, cross = [], []
    for pieces, part in ((range(2), part_1), (range(2, 5), part_2), (range(5, 8), None)):
        mine, other = products(near_own, far_own, pieces, parts=2, add=part)
        other = core(other)
        own += [[(mine, n)] for n in range(len(pieces))]
        cross += [[(other, n)] for n in range(len(pieces))]
    for n in range(3):
        own[5 + n].append((part_3[0], n))
        cross[5 + n].append((part_3[1], n))
    spots = lambda s: jnp.stack([(me ^ s ^ (i % 4 * 2)) * 2 + i // 4 for i in range(8)])
    out = place(spots(0), own, half, None, all_cols, LONG, part_3[1:])
    return place(spots(1), cross, half, out, all_cols, SHORT)


def solution(mesh):
    in_specs = (
        P("seq", "ch"),
        P("seq", "ch"),
        P("seq", "ch"),
        P("ch", None),
        P("ch", None),
        P("ch", "seq"),
    )
    out_specs = P(("seq", "ch"), None)
    body = functools.partial(on_device, mesh.shape["seq"], mesh.shape["ch"])
    return jax.shard_map(
        body, mesh=mesh, in_specs=in_specs, out_specs=out_specs, check_vma=False
    )
```

time: 313 us -> 153 us (0.49)
  local copies, waits for them, and re-layouts: 105 us -> 8.08 us
  waiting for transfers between devices: 146 us -> 55.2 us
  Pallas kernels: 0 us -> 59 us
  matrix products: 29.7 us -> 0 us
  starting transfers between devices: 0.04 us -> 29 us
  blocking collectives: 13.7 us -> 0 us
  between operations: 13.6 us -> 0.24 us
  other arithmetic: 4.85 us -> 0.57 us
    reduce_scatter x1 -> x0, waiting for transfers between devices: 145 us -> none  [on_device(): lax.psum_scatter(jnp.dot(gated, weight_cols, preferred_element_type=jnp.f...]
    pallas_call x0 -> x12, Pallas kernels: none -> 59 us  [the longest x6 29.2 us: share(): pl.pallas_call(functools.partial(share_kernel, len(near), len(near_w), le...]
    ppermute x0 -> x24, waiting for transfers between devices: none -> 53.8 us  [the longest x23 53.8 us: flip(): return lax.ppermute(x, axis, [(i, i ^ bits) for i in range(size)])]
    reshape x2 -> x0, local copies, waits for them, and re-layouts: 39.4 us -> none  [the longest x1 36 us: band_matrix(): return tiled.reshape(group_count, block, 2 * block - 1)[:, :, block - 1:]]
    unnamed x11 -> x54, local copies, waits for them, and re-layouts: 39.1 us -> 5.66 us
    dot_general x4 -> x0, matrix products: 29.7 us -> none  [the longest x1 14.8 us: on_device(): jnp.dot(gated, weight_cols, preferred_element_type=jnp.float32)]
    ppermute x0 -> x24, starting transfers between devices: none -> 25.5 us  [the longest x23 23.7 us: flip(): return lax.ppermute(x, axis, [(i, i ^ bits) for i in range(size)])]
    all_gather x1 -> x0, blocking collectives: 13.7 us -> none  [on_device(): lax.all_gather(final_state[None].astype(jnp.bfloat16), 'seq', axis=0, til...]
  transfers between devices with their start and end apart: 2 -> 25, of which waited for: 1 -> 11; matrix products, arithmetic and copies ran while one was open for 40% -> 2% of each run, Pallas kernels for 0% -> 37%
where the time goes in v2:
time: 153 us; the launch traced here: 152 us
  Pallas kernels  59 us (39%)
  waiting for transfers between devices  55.2 us (36%)
  starting transfers between devices  29 us (19%)
  local copies, waits for them, and re-layouts  8.08 us (5%)
    ppermute x23, waiting for transfers between devices, flip(): return lax.ppermute(x, axis, [(i, i ^ bits) for i in range(size)])  53.8 us
    pallas_call x6, Pallas kernels, share(): pl.pallas_call(functools.partial(share_kernel, len(near), len(near_w), le...  29.2 us
    ppermute x23, starting transfers between devices, flip(): return lax.ppermute(x, axis, [(i, i ^ bits) for i in range(size)])  23.7 us
    pallas_call x1, Pallas kernels, local_conv(): pl.pallas_call(functools.partial(local_kernel, width), grid=(chans // TIL...  10.7 us
    pallas_call x2, Pallas kernels, gate(): pl.pallas_call(functools.partial(gate_kernel, modes, width, counts), grid...  8.15 us
    pallas_call x2, Pallas kernels, place(): pl.pallas_call(functools.partial(place_kernel, spots), grid_spec=pltpu.Pr...  6.01 us
    unnamed x54, local copies, waits for them, and re-layouts  5.66 us
    pallas_call x1, Pallas kernels, range_state(): pl.pallas_call(functools.partial(range_state_kernel, width), grid_spec=pl...  4.95 us
  transfers between devices with their start and end apart: 25, of which 11 were waited for; matrix products, arithmetic and copies ran while one was open for 2% of the time, Pallas kernels for 37%

profile of v2, /device:TPU:0, one launch (start us, length us, event | category | flops | bytes accessed | tf_op | source)
XLA Modules:
  0.0 152.2 jit_solution(13640208708550027083)
XLA Ops:
  0.0 2.9 %collective-permute-start = (bf16[1024,512]{1,0:T(8,128)(2,1)}, bf16[1024,512]{1,0:T(8,128)(2,1)S(1)}, u32[]{:S(2)}, u32[]{:S(2)}) collective-permute-start(bf16[1024,512]{1,0:T(8,128)(2,1)} %refs_6_.3), channel_id=1, source_target_pairs={{0,8},{4,12},{8,0},{12,4},{16,24},{20,28},{24,16},{28,20},{1,9},{5... | collective-permute-start | bytes 3145736 | tf_op jit(solution)/shard_map/ppermute | solution.py:307
  2.9 1.5 collective-permute-start.1
  4.5 1.1 slice.12
  5.6 2.7 %collective-permute-start.2 = (bf16[1024,256]{1,0:T(8,128)(2,1)S(1)}, bf16[1024,256]{1,0:T(8,128)(2,1)}, u32[]{:S(2)}, u32[]{:S(2)}) collective-permute-start(bf16[1024,256]{1,0:T(8,128)(2,1)S(1)} %slice.12), channel_id=1, source_target_pairs={{0,2},{1,3},{2,0},{3,1},{4,6},{5,7},{6,4},{7,5},{8,10},{9,11},{10,... | collective-permute-start | bytes 1572872 | tf_op jit(solution)/shard_map/ppermute | solution.py:307
  8.2 5.0 %range_state.1 = (bf16[1024,1024]{1,0:T(8,128)(2,1)}, bf16[8,16,1024]{2,1,0:T(8,128)(2,1)}) custom-call(s32[1]{0:T(128)} %bitcast.8.me_ref, bf16[1024,1024]{1,0:T(8,128)(2,1)} %k_ref.1, bf16[1024,1024]{1,0:T(8,128)(2,1)} %v_ref.1, f32[16,64]{1,0:T(8,128)} %bitcast.20), custom_call_target="tpu_custom_call" | custom-call | flops 1 | bytes 1 | tf_op jit(solution)/shard_map/range_state/pallas_call | solution.py:73
  13.2 3.5 %all-to-all-start = ((bf16[8,16,1024]{2,1,0:T(8,128)(2,1)}), bf16[8,16,1024]{2,1,0:T(8,128)(2,1)S(1)}, u32[]{:S(2)}, u32[]{:S(2)}) async-start(bf16[8,16,1024]{2,1,0:T(8,128)(2,1)} %get-tuple-element.42), calls=%async_computation | async-start | bytes 524288 | tf_op jit(solution)/shard_map/all_to_all | solution.py:327
  16.7 10.7 %local_conv.1 = (f32[1024,1024]{1,0:T(8,128)}, f32[2,1024]{1,0:T(2,128)}) custom-call(bf16[1024,1024]{1,0:T(8,128)(2,1)} %get-tuple-element.38.u_ref, f32[16,64]{1,0:T(8,128)} %bitcast.21, f32[16,64]{1,0:T(8,128)} %bitcast.22), custom_call_target="tpu_custom_call" | custom-call | flops 1 | bytes 1 | tf_op jit(solution)/shard_map/local_conv/pallas_call | solution.py:142
  27.4 0.6 broadcast_xor_fusion.place_ref
  28.0 1.1 collective-permute-done.1.refs_5_.refs_4_
  29.2 1.4 all-to-all-done.state_ref
  30.6 0.7 copy-done.7
  31.3 2.6 %gate.2 = bf16[256,1024]{1,0:T(8,128)(2,1)} custom-call(s32[1]{0:T(128)} %bitcast.11.place_ref, f32[1024,1024]{1,0:T(8,128)} %get-tuple-element.44.z_ref, bf16[1024,1024]{1,0:T(8,128)(2,1)} %q_ref.3, f32[2,1024]{1,0:T(2,128)} %get-tuple-element.41.rows_ref, bf16[8,16,1024]{2,1,0:T(8,128)(2,1)} %copy-done.7), custom_call_target="tpu_custom_call" | custom-call | flops 1 | bytes 1 | tf_op jit(solution)/shard_map/gate/pallas_call | solution.py:198
  33.9 0.9 collective-permute-start.5
  34.8 0.0 copy-start
  34.9 1.2 collective-permute-start.7
  36.1 0.9 collective-permute-start.6
  37.0 2.6 %collective-permute-start.4 = (bf16[256,1024]{1,0:T(8,128)(2,1)}, bf16[256,1024]{1,0:T(8,128)(2,1)S(1)}, u32[]{:S(2)}, u32[]{:S(2)}) collective-permute-start(bf16[256,1024]{1,0:T(8,128)(2,1)} %gate.2), channel_id=1, source_target_pairs={{0,2},{1,3},{2,0},{3,1},{4,6},{5,7},{6,4},{7,5},{8,10},{9,11},{10,... | collective-permute-start | bytes 1572872 | tf_op jit(solution)/shard_map/ppermute | solution.py:307
  39.5 5.5 %gate.3 = (bf16[512,1024]{1,0:T(8,128)(2,1)}, bf16[256,1024]{1,0:T(8,128)(2,1)}) custom-call(s32[3]{0:T(128)} %broadcast_xor_fusion.place_ref, f32[1024,1024]{1,0:T(8,128)} %get-tuple-element.44.z_ref, bf16[1024,1024]{1,0:T(8,128)(2,1)} %q_ref.3, f32[2,1024]{1,0:T(2,128)} %get-tuple-element.41.rows_ref, bf16[8,16,1024]{2,1,0:T(8,128)(2,1)} %copy-done.7), custom_call_target="tpu_custom_call" | custom-call | flops 1 | bytes 1 | tf_op jit(solution)/shard_map/gate/pallas_call | solution.py:198
  45.1 0.0 collective-permute-start.3
  45.1 4.7 %collective-permute-done.7.refs_5_ = bf16[1024,256]{1,0:T(8,128)(2,1)S(1)} collective-permute-done((bf16[1024,256]{1,0:T(8,128)(2,1)S(1)}, bf16[1024,256]{1,0:T(8,128)(2,1)S(1)}, u32[]{:S(2)}, u32[]{:S(2)}) %collective-permute-start.7) | collective-permute-done | bytes 524320 | tf_op jit(solution)/shard_map/ppermute | solution.py:307
  49.8 0.0 collective-permute-done.5.refs_7_
  49.8 9.4 %collective-permute-done.6.refs_7_ = bf16[1024,256]{1,0:T(8,128)(2,1)S(1)} collective-permute-done((bf16[1024,256]{1,0:T(8,128)(2,1)}, bf16[1024,256]{1,0:T(8,128)(2,1)S(1)}, u32[]{:S(2)}, u32[]{:S(2)}) %collective-permute-start.6) | collective-permute-done | bytes 524320 | tf_op jit(solution)/shard_map/ppermute | solution.py:307
  59.2 2.6 %collective-permute-done.4.refs_2_ = bf16[256,1024]{1,0:T(8,128)(2,1)S(1)} collective-permute-done((bf16[256,1024]{1,0:T(8,128)(2,1)}, bf16[256,1024]{1,0:T(8,128)(2,1)S(1)}, u32[]{:S(2)}, u32[]{:S(2)}) %collective-permute-start.4) | collective-permute-done | bytes 524320 | tf_op jit(solution)/shard_map/ppermute | solution.py:307
  61.8 1.9 %collective-permute-done.9.refs_3_ = bf16[256,1024]{1,0:T(8,128)(2,1)S(1)} collective-permute-done((bf16[256,1024]{1,0:T(8,128)(2,1)S(1)}, bf16[256,1024]{1,0:T(8,128)(2,1)S(1)}, u32[]{:S(2)}, u32[]{:S(2)}) %collective-permute-start.9) | collective-permute-done | bytes 524320 | tf_op jit(solution)/shard_map/ppermute | solution.py:307
  63.8 1.2 collective-permute-start.11
  65.0 1.5 collective-permute-start.10
  66.5 4.2 %share.7 = bf16[512,512]{1,0:T(8,128)(2,1)} custom-call(bf16[512,1024]{1,0:T(8,128)(2,1)} %get-tuple-element.45.refs_0_, bf16[512,1024]{1,0:T(8,128)(2,1)} %copy-done.1, bf16[256,1024]{1,0:T(8,128)(2,1)} %copy-done.12, bf16[256,1024]{1,0:T(8,128)(2,1)} %copy-done.13, bf16[1024,512]{1,0:T(8,128)(2,1)} %refs_6_.3, bf16[1024,512]{1,0:T(8,128)(2,1)} %copy-done.2, ...), custom_call_target="tpu_custom_call" | custom-call | flops 1 | bytes 1 | tf_op jit(solution)/shard_map/share/pallas_call | solution.py:237
  70.7 2.1 %collective-permute-start.17 = (bf16[512,512]{1,0:T(8,128)(2,1)}, bf16[512,512]{1,0:T(8,128)(2,1)}, u32[]{:S(2)}, u32[]{:S(2)}) collective-permute-start(bf16[512,512]{1,0:T(8,128)(2,1)} %share.7), channel_id=1, source_target_pairs={{0,1},{1,0},{2,3},{3,2},{4,5},{5,4},{6,7},{7,6},{8,9},{9,8},{10,11... | collective-permute-start | bytes 1572872 | tf_op jit(solution)/shard_map/ppermute | solution.py:307
  72.9 15.5 %collective-permute-done.8.refs_9_ = bf16[1024,256]{1,0:T(8,128)(2,1)S(1)} collective-permute-done((bf16[1024,256]{1,0:T(8,128)(2,1)S(1)}, bf16[1024,256]{1,0:T(8,128)(2,1)S(1)}, u32[]{:S(2)}, u32[]{:S(2)}) %collective-permute-start.8) | collective-permute-done | bytes 524320 | tf_op jit(solution)/shard_map/ppermute | solution.py:307
  88.4 0.0 collective-permute-done.10.refs_8_
  88.4 0.1 collective-permute-start.12
  88.5 1.2 collective-permute-start.13
  89.7 1.5 collective-permute-start.14
  91.2 0.8 collective-permute-start.15
  92.1 5.2 %share.9 = bf16[512,768]{1,0:T(8,128)(2,1)} custom-call(bf16[512,1024]{1,0:T(8,128)(2,1)} %get-tuple-element.45.refs_0_, bf16[512,1024]{1,0:T(8,128)(2,1)} %copy-done.1, bf16[256,1024]{1,0:T(8,128)(2,1)} %copy-done.12, bf16[256,1024]{1,0:T(8,128)(2,1)} %copy-done.13, bf16[1024,512]{1,0:T(8,128)(2,1)} %copy-done.3, bf16[1024,256]{1,0:T(8,128)(2,1)} %copy-done.8, ...), custom_call_target="tpu_custom_call" | custom-call | flops 1 | bytes 1 | tf_op jit(solution)/shard_map/share/pallas_call | solution.py:237
  97.2 0.0 collective-permute-done.17.refs_8_
  97.2 1.7 %collective-permute-start.19 = (bf16[512,768]{1,0:T(8,128)(2,1)}, bf16[512,768]{1,0:T(8,128)(2,1)S(1)}, u32[]{:S(2)}, u32[]{:S(2)}) collective-permute-start(bf16[512,768]{1,0:T(8,128)(2,1)} %share.9), channel_id=1, source_target_pairs={{0,1},{1,0},{2,3},{3,2},{4,5},{5,4},{6,7},{7,6},{8,9},{9,8},{10,11... | collective-permute-start | bytes 2359304 | tf_op jit(solution)/shard_map/ppermute | solution.py:307
  98.9 14.2 %collective-permute-done.12.refs_2_ = bf16[256,1024]{1,0:T(8,128)(2,1)S(1)} collective-permute-done((bf16[256,1024]{1,0:T(8,128)(2,1)S(1)}, bf16[256,1024]{1,0:T(8,128)(2,1)S(1)}, u32[]{:S(2)}, u32[]{:S(2)}) %collective-permute-start.12) | collective-permute-done | bytes 524320 | tf_op jit(solution)/shard_map/ppermute | solution.py:307
  113.1 0.1 collective-permute-done.14.refs_8_
  113.2 1.0 collective-permute-done.15.refs_9_
  114.2 0.8 copy-done.19
  114.9 5.1 %share.6 = (bf16[256,768]{1,0:T(8,128)(2,1)}, bf16[256,768]{1,0:T(8,128)(2,1)}) custom-call(bf16[512,1024]{1,0:T(8,128)(2,1)} %get-tuple-element.45.refs_0_, bf16[512,1024]{1,0:T(8,128)(2,1)} %copy-done.1, bf16[256,1024]{1,0:T(8,128)(2,1)} %copy-done.12, bf16[256,1024]{1,0:T(8,128)(2,1)} %copy-done.13, bf16[1024,512]{1,0:T(8,128)(2,1)} %copy-done.2, ...), custom_call_target="tpu_custom_call" | custom-call | flops 68719476736 | bytes 268435456 | tf_op jit(solution)/shard_map/share/pallas_call | solution.py:237
  120.0 0.0 collective-permute-start.16
  120.0 1.8 %collective-permute-start.22 = (bf16[256,768]{1,0:T(8,128)(2,1)}, bf16[256,768]{1,0:T(8,128)(2,1)S(1)}, u32[]{:S(2)}, u32[]{:S(2)}) collective-permute-start(bf16[256,768]{1,0:T(8,128)(2,1)} %get-tuple-element.67), channel_id=1, source_target_pairs={{0,5},{1,4},{2,7},{3,6},{4,1},{5,0},{6,3},{7,2},{8,13},{9,12},{10,... | collective-permute-start | bytes 1179656 | tf_op jit(solution)/shard_map/ppermute | solution.py:346
  121.9 0.3 collective-permute-start.23
  122.2 0.6 stack.71.place_ref
  122.8 0.6 stack.62.place_ref
  123.4 0.0 collective-permute-done.16.refs_3_
  123.4 0.8 copy-done.6
  124.2 5.1 %share.11 = (bf16[256,768]{1,0:T(8,128)(2,1)}, bf16[256,768]{1,0:T(8,128)(2,1)}) custom-call(bf16[512,1024]{1,0:T(8,128)(2,1)} %get-tuple-element.45.refs_0_, bf16[512,1024]{1,0:T(8,128)(2,1)} %copy-done.1, bf16[256,1024]{1,0:T(8,128)(2,1)} %copy-done.5, bf16[256,1024]{1,0:T(8,128)(2,1)} %copy-done.6, bf16[1024,512]{1,0:T(8,128)(2,1)} %copy-done.2, ...), custom_call_target="tpu_custom_call" | custom-call | flops 1 | bytes 1 | tf_op jit(solution)/shard_map/share/pallas_call | solution.py:237
  129.3 0.0 collective-permute-start.21
  129.3 0.9 copy-done.15
  130.2 5.4 %share.10 = (bf16[256,768]{1,0:T(8,128)(2,1)}, bf16[256,768]{1,0:T(8,128)(2,1)}) custom-call(bf16[512,1024]{1,0:T(8,128)(2,1)} %get-tuple-element.45.refs_0_, bf16[512,1024]{1,0:T(8,128)(2,1)} %copy-done.1, bf16[256,1024]{1,0:T(8,128)(2,1)} %copy-done.5, bf16[256,1024]{1,0:T(8,128)(2,1)} %copy-done.6, bf16[1024,512]{1,0:T(8,128)(2,1)} %copy-done.3, ...), custom_call_target="tpu_custom_call" | custom-call | flops 1 | bytes 1 | tf_op jit(solution)/shard_map/share/pallas_call | solution.py:237
  135.6 0.5 collective-permute-start.20
  136.1 4.3 %share.8 = (bf16[256,512]{1,0:T(8,128)(2,1)}, bf16[256,512]{1,0:T(8,128)(2,1)}) custom-call(bf16[512,1024]{1,0:T(8,128)(2,1)} %get-tuple-element.45.refs_0_, bf16[512,1024]{1,0:T(8,128)(2,1)} %copy-done.1, bf16[256,1024]{1,0:T(8,128)(2,1)} %copy-done.5, bf16[256,1024]{1,0:T(8,128)(2,1)} %copy-done.6, bf16[1024,512]{1,0:T(8,128)(2,1)} %refs_6_.3, ...), custom_call_target="tpu_custom_call" | custom-call | flops 1 | bytes 1 | tf_op jit(solution)/shard_map/share/pallas_call | solution.py:237
  140.4 0.0 collective-permute-start.18
  140.4 3.3 %collective-permute-done.23.refs_3_ = bf16[256,768]{1,0:T(8,128)(2,1)S(1)} collective-permute-done((bf16[256,768]{1,0:T(8,128)(2,1)}, bf16[256,768]{1,0:T(8,128)(2,1)S(1)}, u32[]{:S(2)}, u32[]{:S(2)}) %collective-permute-start.23) | collective-permute-done | bytes 393248 | tf_op jit(solution)/shard_map/ppermute | solution.py:307
  143.7 0.8 copy-done.25
  144.5 3.0 %place.2.refs_4_ = bf16[256,4096]{1,0:T(8,128)(2,1)} custom-call(s32[8]{0:T(128)} %stack.71.place_ref, bf16[256,512]{1,0:T(8,128)(2,1)} %get-tuple-element.68.refs_0_, bf16[256,768]{1,0:T(8,128)(2,1)} %get-tuple-element.69.refs_1_, bf16[256,768]{1,0:T(8,128)(2,1)} %get-tuple-element.70.refs_2_, bf16[256,768]{1,0:T(8,128)(2,1)} %copy-done.25, ...), custom_call_target="tpu_custom_call" | custom-call | flops 68719476736 | bytes 268435456 | tf_op jit(solution)/shard_map/place/pallas_call | solution.py:286
  147.5 0.0 collective-permute-done.18.refs_0_
  147.6 0.6 copy-done.23
  148.2 0.2 copy-done.21
  148.4 0.8 copy-done.22
  149.2 3.0 %place.3 = bf16[256,4096]{1,0:T(8,128)(2,1)} custom-call(s32[8]{0:T(128)} %stack.62.place_ref, bf16[256,512]{1,0:T(8,128)(2,1)} %copy-done.23, bf16[256,768]{1,0:T(8,128)(2,1)} %copy-done.22, bf16[256,768]{1,0:T(8,128)(2,1)} %copy-done.21, bf16[256,768]{1,0:T(8,128)(2,1)} %copy-done.20, bf16[256,4096]{1,0:T(8,128)(2,1)} %place.2.refs_4_), custom_call_target="tpu_custom_call", output_to_operand_aliasing={{}: (5, {})} | custom-call | flops 1 | bytes 1 | tf_op jit(solution)/shard_map/place/pallas_call | solution.py:286
  (59 shorter events, 0.2 us)
Async XLA Ops:
  0.0 28.0 %collective-permute-start = (bf16[1024,512]{1,0:T(8,128)(2,1)}, bf16[1024,512]{1,0:T(8,128)(2,1)S(1)}, u32[]{:S(2)}, u32[]{:S(2)}) collective-permute-start(bf16[1024,512]{1,0:T(8,128)(2,1)} %refs_6_.3), channel_id=1, source_target_pairs={{0,8},{4,12},{8,0},{12,4},{16,24},{20,28},{24,16},{28,20},{1,9},{5... | collective-permute-start | bytes 3145736 | tf_op jit(solution)/shard_map/ppermute | solution.py:307
  2.9 26.2 %collective-permute-start.1 = (bf16[1024,512]{1,0:T(8,128)(2,1)}, bf16[1024,512]{1,0:T(8,128)(2,1)S(1)}, u32[]{:S(2)}, u32[]{:S(2)}) collective-permute-start(bf16[1024,512]{1,0:T(8,128)(2,1)} %refs_6_.3), channel_id=1, source_target_pairs={{0,16},{4,20},{8,24},{12,28},{16,0},{20,4},{24,8},{28,12},{1,17},{... | collective-permute-start | bytes 3145736 | tf_op jit(solution)/shard_map/ppermute | solution.py:307
  5.6 28.3 %collective-permute-start.2 = (bf16[1024,256]{1,0:T(8,128)(2,1)S(1)}, bf16[1024,256]{1,0:T(8,128)(2,1)}, u32[]{:S(2)}, u32[]{:S(2)}) collective-permute-start(bf16[1024,256]{1,0:T(8,128)(2,1)S(1)} %slice.12), channel_id=1, source_target_pairs={{0,2},{1,3},{2,0},{3,1},{4,6},{5,7},{6,4},{7,5},{8,10},{9,11},{10,... | collective-permute-start | bytes 1572872 | tf_op jit(solution)/shard_map/ppermute | solution.py:307
  13.2 14.3 %copy-start.26 = (s32[3]{0:T(128)S(1)}, s32[3]{0:T(128)}, u32[]{:S(2)}) copy-start(s32[3]{0:T(128)} %constant.22.clone) | copy-start | bytes 40
  13.2 17.4 %all-to-all-start = ((bf16[8,16,1024]{2,1,0:T(8,128)(2,1)}), bf16[8,16,1024]{2,1,0:T(8,128)(2,1)S(1)}, u32[]{:S(2)}, u32[]{:S(2)}) async-start(bf16[8,16,1024]{2,1,0:T(8,128)(2,1)} %get-tuple-element.42), calls=%async_computation | async-start | bytes 524288 | tf_op jit(solution)/shard_map/all_to_all | solution.py:327
  28.0 6.8 %copy-start.2 = (bf16[1024,512]{1,0:T(8,128)(2,1)}, bf16[1024,512]{1,0:T(8,128)(2,1)S(1)}, u32[]{:S(2)}) copy-start(bf16[1024,512]{1,0:T(8,128)(2,1)S(1)} %collective-permute-done.refs_4_.refs_5_) | copy-start | bytes 3145732
  29.2 4.7 %copy-start.3 = (bf16[1024,512]{1,0:T(8,128)(2,1)}, bf16[1024,512]{1,0:T(8,128)(2,1)S(1)}, u32[]{:S(2)}) copy-start(bf16[1024,512]{1,0:T(8,128)(2,1)S(1)} %collective-permute-done.1.refs_5_.refs_4_) | copy-start | bytes 3145732
  30.6 0.7 copy-start.7
  33.9 15.9 %collective-permute-start.5 = (bf16[1024,256]{1,0:T(8,128)(2,1)}, bf16[1024,256]{1,0:T(8,128)(2,1)S(1)}, u32[]{:S(2)}, u32[]{:S(2)}) collective-permute-start(bf16[1024,256]{1,0:T(8,128)(2,1)} %collective-permute-done.2.refs_6_), channel_id=1, source_target_pairs={{0,8},{4,12},{8,0},{12,4},{16,24},{20,28},{24,16},{28,20},{1,9},{5... | collective-permute-start | bytes 1572872 | tf_op jit(solution)/shard_map/ppermute | solution.py:307
  34.8 10.3 %copy-start = (bf16[1024,512]{1,0:T(8,128)(2,1)S(1)}, bf16[1024,512]{1,0:T(8,128)(2,1)}, u32[]{:S(2)}) copy-start(bf16[1024,512]{1,0:T(8,128)(2,1)} %refs_6_.3) | copy-start | bytes 3145732
  34.8 28.9 %copy-start.4 = (bf16[1024,512]{1,0:T(8,128)(2,1)S(1)}, bf16[1024,512]{1,0:T(8,128)(2,1)}, u32[]{:S(2)}) copy-start(bf16[1024,512]{1,0:T(8,128)(2,1)} %copy-done.3) | copy-start | bytes 3145732
  34.9 14.9 %collective-permute-start.7 = (bf16[1024,256]{1,0:T(8,128)(2,1)S(1)}, bf16[1024,256]{1,0:T(8,128)(2,1)S(1)}, u32[]{:S(2)}, u32[]{:S(2)}) collective-permute-start(bf16[1024,256]{1,0:T(8,128)(2,1)S(1)} %slice.13), channel_id=1, source_target_pairs={{0,16},{4,20},{8,24},{12,28},{16,0},{20,4},{24,8},{28,12},{1,17},{... | collective-permute-start | bytes 1572872 | tf_op jit(solution)/shard_map/ppermute | solution.py:307
  36.1 23.1 %collective-permute-start.6 = (bf16[1024,256]{1,0:T(8,128)(2,1)}, bf16[1024,256]{1,0:T(8,128)(2,1)S(1)}, u32[]{:S(2)}, u32[]{:S(2)}) collective-permute-start(bf16[1024,256]{1,0:T(8,128)(2,1)} %collective-permute-done.2.refs_6_), channel_id=1, source_target_pairs={{0,16},{4,20},{8,24},{12,28},{16,0},{20,4},{24,8},{28,12},{1,17},{... | collective-permute-start | bytes 1572872 | tf_op jit(solution)/shard_map/ppermute | solution.py:307
  37.0 24.8 %collective-permute-start.4 = (bf16[256,1024]{1,0:T(8,128)(2,1)}, bf16[256,1024]{1,0:T(8,128)(2,1)S(1)}, u32[]{:S(2)}, u32[]{:S(2)}) collective-permute-start(bf16[256,1024]{1,0:T(8,128)(2,1)} %gate.2), channel_id=1, source_target_pairs={{0,2},{1,3},{2,0},{3,1},{4,6},{5,7},{6,4},{7,5},{8,10},{9,11},{10,... | collective-permute-start | bytes 1572872 | tf_op jit(solution)/shard_map/ppermute | solution.py:307
  45.1 18.6 %collective-permute-start.3 = (bf16[512,1024]{1,0:T(8,128)(2,1)}, bf16[512,1024]{1,0:T(8,128)(2,1)S(1)}, u32[]{:S(2)}, u32[]{:S(2)}) collective-permute-start(bf16[512,1024]{1,0:T(8,128)(2,1)} %get-tuple-element.45.refs_0_), channel_id=1, source_target_pairs={{0,4},{4,0},{8,12},{12,8},{16,20},{20,16},{24,28},{28,24},{1,5},{5... | collective-permute-start | bytes 3145736 | tf_op jit(solution)/shard_map/ppermute | solution.py:307
  49.8 42.3 %copy-start.8 = (bf16[1024,256]{1,0:T(8,128)(2,1)}, bf16[1024,256]{1,0:T(8,128)(2,1)S(1)}, u32[]{:S(2)}) copy-start(bf16[1024,256]{1,0:T(8,128)(2,1)S(1)} %collective-permute-done.7.refs_5_) | copy-start | bytes 1572868
  49.8 16.7 %copy-start.14 = (bf16[1024,256]{1,0:T(8,128)(2,1)}, bf16[1024,256]{1,0:T(8,128)(2,1)S(1)}, u32[]{:S(2)}) copy-start(bf16[1024,256]{1,0:T(8,128)(2,1)S(1)} %collective-permute-done.5.refs_7_) | copy-start | bytes 1572868
  59.2 32.8 %copy-start.9 = (bf16[1024,256]{1,0:T(8,128)(2,1)}, bf16[1024,256]{1,0:T(8,128)(2,1)S(1)}, u32[]{:S(2)}) copy-start(bf16[1024,256]{1,0:T(8,128)(2,1)S(1)} %collective-permute-done.6.refs_7_) | copy-start | bytes 1572868
  61.8 4.7 %copy-start.12 = (bf16[256,1024]{1,0:T(8,128)(2,1)}, bf16[256,1024]{1,0:T(8,128)(2,1)S(1)}, u32[]{:S(2)}) copy-start(bf16[256,1024]{1,0:T(8,128)(2,1)S(1)} %collective-permute-done.4.refs_2_) | copy-start | bytes 1572868
  61.8 1.9 %collective-permute-start.9 = (bf16[256,1024]{1,0:T(8,128)(2,1)S(1)}, bf16[256,1024]{1,0:T(8,128)(2,1)S(1)}, u32[]{:S(2)}, u32[]{:S(2)}) collective-permute-start(bf16[256,1024]{1,0:T(8,128)(2,1)S(1)} %collective-permute-done.4.refs_2_), channel_id=1, source_target_pairs={{0,4},{4,0},{8,12},{12,8},{16,20},{20,16},{24,28},{28,24},{1,5},{5... | collective-permute-start | bytes 1572872 | tf_op jit(solution)/shard_map/ppermute | solution.py:307
  61.8 26.6 %collective-permute-start.8 = (bf16[1024,256]{1,0:T(8,128)(2,1)S(1)}, bf16[1024,256]{1,0:T(8,128)(2,1)S(1)}, u32[]{:S(2)}, u32[]{:S(2)}) collective-permute-start(bf16[1024,256]{1,0:T(8,128)(2,1)S(1)} %slice.14), channel_id=1, source_target_pairs={{0,2},{1,3},{2,0},{3,1},{4,6},{5,7},{6,4},{7,5},{8,10},{9,11},{10,... | collective-permute-start | bytes 1572872 | tf_op jit(solution)/shard_map/ppermute | solution.py:307
  63.7 2.8 %copy-start.13 = (bf16[256,1024]{1,0:T(8,128)(2,1)}, bf16[256,1024]{1,0:T(8,128)(2,1)S(1)}, u32[]{:S(2)}) copy-start(bf16[256,1024]{1,0:T(8,128)(2,1)S(1)} %collective-permute-done.9.refs_3_) | copy-start | bytes 1572868
  63.7 2.8 %copy-start.1 = (bf16[512,1024]{1,0:T(8,128)(2,1)}, bf16[512,1024]{1,0:T(8,128)(2,1)S(1)}, u32[]{:S(2)}) copy-start(bf16[512,1024]{1,0:T(8,128)(2,1)S(1)} %collective-permute-done.3.refs_1_) | copy-start | bytes 3145732
  63.8 24.6 %copy-start.24 = (bf16[256,1024]{1,0:T(8,128)(2,1)S(1)}, bf16[256,1024]{1,0:T(8,128)(2,1)}, u32[]{:S(2)}) copy-start(bf16[256,1024]{1,0:T(8,128)(2,1)} %get-tuple-element.55) | copy-start | bytes 1572868
  63.8 24.6 %collective-permute-start.11 = (bf16[1024,256]{1,0:T(8,128)(2,1)S(1)}, bf16[1024,256]{1,0:T(8,128)(2,1)S(1)}, u32[]{:S(2)}, u32[]{:S(2)}) collective-permute-start(bf16[1024,256]{1,0:T(8,128)(2,1)S(1)} %slice.15), channel_id=1, source_target_pairs={{0,8},{4,12},{8,0},{12,4},{16,24},{20,28},{24,16},{28,20},{1,9},{5... | collective-permute-start | bytes 1572872 | tf_op jit(solution)/shard_map/ppermute | solution.py:307
  65.0 23.4 %collective-permute-start.10 = (bf16[1024,256]{1,0:T(8,128)(2,1)S(1)}, bf16[1024,256]{1,0:T(8,128)(2,1)S(1)}, u32[]{:S(2)}, u32[]{:S(2)}) collective-permute-start(bf16[1024,256]{1,0:T(8,128)(2,1)S(1)} %collective-permute-done.5.refs_7_), channel_id=1, source_target_pairs={{0,16},{4,20},{8,24},{12,28},{16,0},{20,4},{24,8},{28,12},{1,17},{... | collective-permute-start | bytes 1572872 | tf_op jit(solution)/shard_map/ppermute | solution.py:307
  70.7 26.5 %collective-permute-start.17 = (bf16[512,512]{1,0:T(8,128)(2,1)}, bf16[512,512]{1,0:T(8,128)(2,1)}, u32[]{:S(2)}, u32[]{:S(2)}) collective-permute-start(bf16[512,512]{1,0:T(8,128)(2,1)} %share.7), channel_id=1, source_target_pairs={{0,1},{1,0},{2,3},{3,2},{4,5},{5,4},{6,7},{7,6},{8,9},{9,8},{10,11... | collective-permute-start | bytes 1572872 | tf_op jit(solution)/shard_map/ppermute | solution.py:307
  88.4 3.7 %copy-start.10 = (bf16[1024,256]{1,0:T(8,128)(2,1)}, bf16[1024,256]{1,0:T(8,128)(2,1)S(1)}, u32[]{:S(2)}) copy-start(bf16[1024,256]{1,0:T(8,128)(2,1)S(1)} %collective-permute-done.8.refs_9_) | copy-start | bytes 1572868
  88.4 25.8 %copy-start.16 = (bf16[1024,256]{1,0:T(8,128)(2,1)}, bf16[1024,256]{1,0:T(8,128)(2,1)S(1)}, u32[]{:S(2)}) copy-start(bf16[1024,256]{1,0:T(8,128)(2,1)S(1)} %collective-permute-done.11.refs_6_) | copy-start | bytes 1572868
  88.4 3.7 %copy-start.11 = (bf16[1024,256]{1,0:T(8,128)(2,1)}, bf16[1024,256]{1,0:T(8,128)(2,1)S(1)}, u32[]{:S(2)}) copy-start(bf16[1024,256]{1,0:T(8,128)(2,1)S(1)} %collective-permute-done.10.refs_8_) | copy-start | bytes 1572868
  88.4 24.7 %collective-permute-start.12 = (bf16[256,1024]{1,0:T(8,128)(2,1)S(1)}, bf16[256,1024]{1,0:T(8,128)(2,1)S(1)}, u32[]{:S(2)}, u32[]{:S(2)}) collective-permute-start(bf16[256,1024]{1,0:T(8,128)(2,1)S(1)} %copy-done.24), channel_id=1, source_target_pairs={{0,2},{1,3},{2,0},{3,1},{4,6},{5,7},{6,4},{7,5},{8,10},{9,11},{10,... | collective-permute-start | bytes 1572872 | tf_op jit(solution)/shard_map/ppermute | solution.py:307
  88.5 24.6 %collective-permute-start.13 = (bf16[1024,256]{1,0:T(8,128)(2,1)S(1)}, bf16[1024,256]{1,0:T(8,128)(2,1)S(1)}, u32[]{:S(2)}, u32[]{:S(2)}) collective-permute-start(bf16[1024,256]{1,0:T(8,128)(2,1)S(1)} %collective-permute-done.8.refs_9_), channel_id=1, source_target_pairs={{0,8},{4,12},{8,0},{12,4},{16,24},{20,28},{24,16},{28,20},{1,9},{5... | collective-permute-start | bytes 1572872 | tf_op jit(solution)/shard_map/ppermute | solution.py:307
  89.7 23.5 %collective-permute-start.14 = (bf16[1024,256]{1,0:T(8,128)(2,1)S(1)}, bf16[1024,256]{1,0:T(8,128)(2,1)S(1)}, u32[]{:S(2)}, u32[]{:S(2)}) collective-permute-start(bf16[1024,256]{1,0:T(8,128)(2,1)S(1)} %collective-permute-done.8.refs_9_), channel_id=1, source_target_pairs={{0,16},{4,20},{8,24},{12,28},{16,0},{20,4},{24,8},{28,12},{1,17},{... | collective-permute-start | bytes 1572872 | tf_op jit(solution)/shard_map/ppermute | solution.py:307
  91.2 22.9 %collective-permute-start.15 = (bf16[1024,256]{1,0:T(8,128)(2,1)S(1)}, bf16[1024,256]{1,0:T(8,128)(2,1)S(1)}, u32[]{:S(2)}, u32[]{:S(2)}) collective-permute-start(bf16[1024,256]{1,0:T(8,128)(2,1)S(1)} %collective-permute-done.8.refs_9_), channel_id=1, source_target_pairs={{0,24},{4,28},{8,16},{12,20},{16,8},{20,12},{24,0},{28,4},{1,25},{... | collective-permute-start | bytes 1572872 | tf_op jit(solution)/shard_map/ppermute | solution.py:307
  97.2 32.0 %collective-permute-start.19 = (bf16[512,768]{1,0:T(8,128)(2,1)}, bf16[512,768]{1,0:T(8,128)(2,1)S(1)}, u32[]{:S(2)}, u32[]{:S(2)}) collective-permute-start(bf16[512,768]{1,0:T(8,128)(2,1)} %share.9), channel_id=1, source_target_pairs={{0,1},{1,0},{2,3},{3,2},{4,5},{5,4},{6,7},{7,6},{8,9},{9,8},{10,11... | collective-permute-start | bytes 2359304 | tf_op jit(solution)/shard_map/ppermute | solution.py:307
  113.1 6.9 %copy-start.5 = (bf16[256,1024]{1,0:T(8,128)(2,1)}, bf16[256,1024]{1,0:T(8,128)(2,1)S(1)}, u32[]{:S(2)}) copy-start(bf16[256,1024]{1,0:T(8,128)(2,1)S(1)} %collective-permute-done.12.refs_2_) | copy-start | bytes 1572868
  113.1 1.0 copy-start.17
  113.2 1.0 copy-start.18
  114.2 0.8 copy-start.19
  120.0 3.4 %collective-permute-start.16 = (bf16[256,1024]{1,0:T(8,128)(2,1)S(1)}, bf16[256,1024]{1,0:T(8,128)(2,1)S(1)}, u32[]{:S(2)}, u32[]{:S(2)}) collective-permute-start(bf16[256,1024]{1,0:T(8,128)(2,1)S(1)} %collective-permute-done.12.refs_2_), channel_id=1, source_target_pairs={{0,4},{4,0},{8,12},{12,8},{16,20},{20,16},{24,28},{28,24},{1,5},{5... | collective-permute-start | bytes 1572872 | tf_op jit(solution)/shard_map/ppermute | solution.py:307
  120.0 20.3 %collective-permute-start.22 = (bf16[256,768]{1,0:T(8,128)(2,1)}, bf16[256,768]{1,0:T(8,128)(2,1)S(1)}, u32[]{:S(2)}, u32[]{:S(2)}) collective-permute-start(bf16[256,768]{1,0:T(8,128)(2,1)} %get-tuple-element.67), channel_id=1, source_target_pairs={{0,5},{1,4},{2,7},{3,6},{4,1},{5,0},{6,3},{7,2},{8,13},{9,12},{10,... | collective-permute-start | bytes 1179656 | tf_op jit(solution)/shard_map/ppermute | solution.py:346
  121.9 21.9 %collective-permute-start.23 = (bf16[256,768]{1,0:T(8,128)(2,1)}, bf16[256,768]{1,0:T(8,128)(2,1)S(1)}, u32[]{:S(2)}, u32[]{:S(2)}) collective-permute-start(bf16[256,768]{1,0:T(8,128)(2,1)} %get-tuple-element.58), channel_id=1, source_target_pairs={{0,1},{1,0},{2,3},{3,2},{4,5},{5,4},{6,7},{7,6},{8,9},{9,8},{10,11... | collective-permute-start | bytes 1179656 | tf_op jit(solution)/shard_map/ppermute | solution.py:307
  123.4 0.8 copy-start.6
  129.3 18.3 %collective-permute-start.21 = (bf16[256,768]{1,0:T(8,128)(2,1)}, bf16[256,768]{1,0:T(8,128)(2,1)S(1)}, u32[]{:S(2)}, u32[]{:S(2)}) collective-permute-start(bf16[256,768]{1,0:T(8,128)(2,1)} %get-tuple-element.66), channel_id=1, source_target_pairs={{0,4},{4,0},{8,12},{12,8},{16,20},{20,16},{24,28},{28,24},{1,5},{5... | collective-permute-start | bytes 1179656 | tf_op jit(solution)/shard_map/ppermute | solution.py:307
  129.3 0.9 copy-start.15
  135.6 12.0 %collective-permute-start.20 = (bf16[256,768]{1,0:T(8,128)(2,1)}, bf16[256,768]{1,0:T(8,128)(2,1)S(1)}, u32[]{:S(2)}, u32[]{:S(2)}) collective-permute-start(bf16[256,768]{1,0:T(8,128)(2,1)} %get-tuple-element.65), channel_id=1, source_target_pairs={{0,4},{4,0},{8,12},{12,8},{16,20},{20,16},{24,28},{28,24},{1,5},{5... | collective-permute-start | bytes 1179656 | tf_op jit(solution)/shard_map/ppermute | solution.py:307
  140.4 7.2 %collective-permute-start.18 = (bf16[256,512]{1,0:T(8,128)(2,1)}, bf16[256,512]{1,0:T(8,128)(2,1)S(1)}, u32[]{:S(2)}, u32[]{:S(2)}) collective-permute-start(bf16[256,512]{1,0:T(8,128)(2,1)} %get-tuple-element.60), channel_id=1, source_target_pairs={{0,4},{4,0},{8,12},{12,8},{16,20},{20,16},{24,28},{28,24},{1,5},{5... | collective-permute-start | bytes 786440 | tf_op jit(solution)/shard_map/ppermute | solution.py:307
  140.4 3.4 %copy-start.20 = (bf16[256,768]{1,0:T(8,128)(2,1)}, bf16[256,768]{1,0:T(8,128)(2,1)S(1)}, u32[]{:S(2)}) copy-start(bf16[256,768]{1,0:T(8,128)(2,1)S(1)} %collective-permute-done.22.refs_4_.refs_3_) | copy-start | bytes 1179652
  143.7 0.8 copy-start.25
  147.5 0.7 copy-start.23
  147.6 0.8 copy-start.21
  148.4 0.8 copy-start.22

commit v3 on v2

--- a/solution.py
+++ b/solution.py
@@ -125,11 +125,11 @@
     readout = (res_row * jnp.exp(-rate_row * after.astype(F32))).astype(BF16)
     carried = dot32(readout, jnp.concatenate(starts, axis=1))
     z = dot32(taps_ref[...], split_ref[...])
-    z_ref[:SUB, :] = z[:, :TILE]
+    z_ref[:SUB, :] = z[:, :TILE].astype(BF16)
     for n in range(1, blocks):
         z_ref[n * SUB : (n + 1) * SUB, :] = (
             z[:, n * TILE : (n + 1) * TILE] + carried[:, (n - 1) * TILE : n * TILE]
-        )
+        ).astype(BF16)
 
 
 def local_conv(u, rates, residues, width):
@@ -145,7 +145,7 @@
         in_specs=[feat, table, table],
         out_specs=[feat, pl.BlockSpec((2, rows), lambda i: (0, i))],
         out_shape=[
-            jax.ShapeDtypeStruct((toks, chans), F32),
+            jax.ShapeDtypeStruct((toks, chans), BF16),
             jax.ShapeDtypeStruct((2, rates.size), F32),
         ],
         scratch_shapes=[
@@ -175,7 +175,7 @@
         ).astype(BF16)
         spread = jnp.concatenate([entering[:, lanes]] * (TILE // width), axis=0)
         spread = jnp.where(mask, spread, 0.0).astype(BF16)
-        z = z_ref[:, lanes] + dot32(readout, spread)
+        z = z_ref[:, lanes].astype(F32) + dot32(readout, spread)
         tiles.append((q_ref[:, lanes].astype(F32) * z).astype(BF16))
     at = 0
     for y_ref, count in y_refs:
@@ -210,42 +210,44 @@
     )(places, z, query_feat, rows, states)
 
 
-def share_kernel(sets, count, added, *refs):
+def share_kernel(sets, count, adds, *refs):
     near = jnp.concatenate([r[...] for r in refs[:sets]], axis=0)
     far = jnp.concatenate([r[...] for r in refs[sets : 2 * sets]], axis=0)
-    weights, outs = refs[2 * sets : 2 * sets + 2 * count], refs[2 * sets + 2 * count + added :]
-    rows = near.shape[0] // len(outs)
-    at = 0
-    for wn, wf in zip(weights[:count], weights[count:]):
-        cols = wn.shape[1]
+    weights = refs[2 * sets :][: 2 * count]
+    extra, outs = refs[2 * sets + 2 * count :][: len(adds)], refs[2 * sets + 2 * count + len(adds) :]
+    rows, cols = outs[0].shape[0], weights[0].shape[1]
+    added = {}
+    for ref, at in zip(extra, adds):
+        for n in range(ref.shape[1] // cols):
+            added[at + n] = ref, n * cols
+    for i, (wn, wf) in enumerate(zip(weights[:count], weights[count:])):
         total = dot32(near, wn[...]) + dot32(far, wf[...])
-        if added:
-            total = total + refs[-len(outs) - 1][:, at : at + cols].astype(F32)
+        if i in added:
+            ref, n = added[i]
+            total = total + ref[:, n : n + cols].astype(F32)
         total = total.astype(BF16)
-        for i, out in enumerate(outs):
-            out[:, at : at + cols] = total[i * rows : (i + 1) * rows]
-        at += cols
-
-
-def share(near, far, near_w, far_w, cols, parts=1, add=None, cost=SHORT):
+        for j, out in enumerate(outs):
+            out[:, i * cols : (i + 1) * cols] = total[j * rows : (j + 1) * rows]
+
+
+def share(near, far, near_w, far_w, cols, parts=1, adds=(), cost=SHORT):
     depth = near[0][0].shape[1]
     rows = lambda n: pl.BlockSpec((SUB, depth), lambda i: (n, 0))
     part = lambda col: pl.BlockSpec((depth, cols), lambda i: (0, col))
     whole = lambda *shape: pl.BlockSpec(shape, lambda i: (0, 0))
     height, total = len(near) * SUB, cols * len(near_w)
-    extra = [] if add is None else [add]
-    return pl.pallas_call(
-        functools.partial(share_kernel, len(near), len(near_w), len(extra)),
+    return pl.pallas_call(
+        functools.partial(share_kernel, len(near), len(near_w), [at for _, at in adds]),
         grid=(1,),
         in_specs=[rows(n) for _, n in near + far]
         + [part(col) for _, col in near_w + far_w]
-        + [whole(*e.shape) for e in extra],
+        + [whole(*a.shape) for a, _ in adds],
         out_specs=[whole(height // parts, total)] * parts,
         out_shape=[jax.ShapeDtypeStruct((height // parts, total), BF16)] * parts,
         compiler_params=pltpu.CompilerParams(vmem_limit_bytes=VMEM_BYTES),
         cost_estimate=cost,
         name="share",
-    )(*[a for a, _ in near + far + near_w + far_w], *extra)
+    )(*[a for a, _ in near + far + near_w + far_w], *[a for a, _ in adds])
 
 
 def place_kernel(spots, place_ref, *refs):
@@ -263,7 +265,7 @@
         copy.wait()
 
 
-def place(places, terms, cols, out, all_cols, cost, awaited=()):
+def place(places, terms, cols, all_cols):
     arrays, spots = [], []
     for group in terms:
         spot = []
@@ -276,13 +278,6 @@
         spots.append(spot)
     rows = arrays[0].shape[0]
     specs = [pl.BlockSpec(a.shape, lambda i, p: (0, 0)) for a in arrays]
-    alias = {}
-    arrays += awaited
-    specs += [pl.BlockSpec(memory_space=pl.ANY)] * len(awaited)
-    if out is not None:
-        alias = {1 + len(arrays): 0}
-        arrays.append(out)
-        specs.append(pl.BlockSpec(memory_space=pl.ANY))
     return pl.pallas_call(
         functools.partial(place_kernel, spots),
         grid_spec=pltpu.PrefetchScalarGridSpec(
@@ -296,11 +291,27 @@
             ],
         ),
         out_shape=jax.ShapeDtypeStruct((rows, all_cols), BF16),
-        input_output_aliases=alias,
-        compiler_params=pltpu.CompilerParams(vmem_limit_bytes=VMEM_BYTES),
-        cost_estimate=cost,
+        compiler_params=pltpu.CompilerParams(vmem_limit_bytes=63 << 20),
+        cost_estimate=SHORT,
         name="place",
     )(places, *arrays)
+
+
+def arrived_kernel(spots_ref, *refs):
+    for i in range(spots_ref.shape[0]):
+        refs[-1][i] = spots_ref[i]
+
+
+def arrived(spots, *arrays):
+    smem = pl.BlockSpec(memory_space=pltpu.SMEM)
+    return pl.pallas_call(
+        arrived_kernel,
+        in_specs=[smem] + [pl.BlockSpec(memory_space=pl.ANY)] * len(arrays),
+        out_specs=smem,
+        out_shape=jax.ShapeDtypeStruct(spots.shape, spots.dtype),
+        cost_estimate=LONG,
+        name="arrived",
+    )(spots, *arrays)
 
 
 def flip(x, axis, size, bits):
@@ -344,69 +355,72 @@
     core = lambda x: flip(x, "seq", seq_size, 1)
     pairs = [(s * ch_size + c, (s ^ 1) * ch_size + (c ^ 1)) for s in range(seq_size) for c in range(ch_size)]
     next_cross = lambda x: lax.ppermute(x, ("seq", "ch"), pairs)
-    across = lambda x: flip(x, "seq", seq_size, 2)
-    along = lambda x: flip(x, "seq", seq_size, 4)
+    sides = [(2, 4), (4, 2), (6, 6)]
+
+    def over(x, way):
+        return lax.ppermute(x, "seq", [(i, i ^ sides[way][i % 2]) for i in range(seq_size)])
 
     half = piece_cols // 2
     first, second = slice(0, half), slice(half, None)
 
     n_a = out_weight[:, first]
     f_a = far_plane(n_a)
-    n_x, n_y = across(out_weight), along(out_weight)
-    (y_3,) = gated((3,), (1,), n_x, n_y)
+    n_1 = over(out_weight, 0)
+    (y_3,) = gated((3,), (1,), n_1)
 
     y_far_other = far_plane(y_3)
     f_a = after(f_a, y_3)
-    f_ax, f_ay = across(f_a), along(f_a)
-    n_ac = along(after(n_x, f_a)[:, first])
-    near, y_2 = gated((1, 0, 2), (2, 1), n_x, n_y, f_a)
+    f_a1, f_a2 = over(f_a, 0), over(f_a, 1)
+    n_2 = over(after(out_weight, f_a), 1)
+    near, y_2 = gated((1, 0, 2), (2, 1), n_1, f_a)
     near_sib = core(near)
     n_b = after(out_weight, near)[:, second]
-    y_far_other, f_ax, f_ay, n_ac, n_b = lax.optimization_barrier(
-        (y_far_other, f_ax, f_ay, n_ac, n_b)
+    y_far_other, f_a1, f_a2, n_2, n_b = lax.optimization_barrier(
+        (y_far_other, f_a1, f_a2, n_2, n_b)
     )
 
     f_b = far_plane(n_b)
     far_other_sib = core(y_far_other)
-    f_ac = along(after(f_ax, far_other_sib))
-    n_bc = across(after(n_y, near_sib, far_other_sib)[:, second])
-    near_w = [(out_weight, 0), (n_x, 0), (n_y, 0), (n_ac, 0)]
-    near_w += [(out_weight, 1), (n_x, 1), (n_y, 1), (n_bc, 0)]
-    far_w = [(f_a, 0), (f_ax, 0), (f_ay, 0)]
+    n_3, f_a3 = over(after(n_1, far_other_sib), 1), over(after(f_a1, far_other_sib), 1)
+    near_w, far_w = [(out_weight, 0), (n_1, 0), (n_2, 0)], [(f_a, 0), (f_a1, 0), (f_a2, 0)]
     near_other, near_own = [(near, 0), (near_sib, 0)], [(near, 1), (near_sib, 1)]
     far_other = [(y_far_other, 0), (far_other_sib, 0)]
 
     def products(near, far, pieces, **kw):
         return share(near, far, [near_w[i] for i in pieces], [far_w[i] for i in pieces], half, **kw)
 
-    (ready_1,) = products(near_other, far_other, range(2))
+    (ready_1,) = products(near_other, far_other, range(3))
     part_1 = next_plane(ready_1)
 
-    f_b, f_ac, n_bc = lax.optimization_barrier((f_b, f_ac, n_bc))
-    near_w[7] = (n_bc, 0)
+    f_b, n_3, f_a3 = lax.optimization_barrier((f_b, n_3, f_a3))
+    near_w = [(n, h) for h in (0, 1) for n in (out_weight, n_1, n_2, n_3)]
     y_far_own = far_plane(after(y_2, f_b))
-    f_bx, f_by, f_bc = across(f_b), along(f_b), flip(f_b, "seq", seq_size, 6)
-    far_w += [(f_ac, 0), (f_b, 0)]
-    (ready_2,) = products(near_other, far_other, range(2, 5))
+    f_b1, f_b2, f_b3 = (over(f_b, way) for way in range(3))
+    far_w += [(f_a3, 0), (f_b, 0)]
+    (ready_2,) = products(near_other, far_other, range(3, 5))
     part_2 = next_plane(after(ready_2, part_1))
-    far_w += [(after(f_bx, y_far_own), 0), (f_by, 0), (f_bc, 0)]
+    far_w += [(after(f_b1, y_far_own), 0), (f_b2, 0), (f_b3, 0)]
     mine, other = products(near_other, far_other, range(5, 8), parts=2, cost=LONG)
     part_3 = next_plane(mine), next_cross(other)
 
     far_own_sib = core(after(y_far_own, mine))
-    far_own = [(y_far_own, 0), (far_own_sib, 0)]
-    own, cross = [], []
-    for pieces, part in ((range(2), part_1), (range(2, 5), part_2), (range(5, 8), None)):
-        mine, other = products(near_own, far_own, pieces, parts=2, add=part)
-        other = core(other)
-        own += [[(mine, n)] for n in range(len(pieces))]
-        cross += [[(other, n)] for n in range(len(pieces))]
+    far_own = [(after(y_far_own, part_2), 0), (far_own_sib, 0)]
+    mine, other = products(
+        near_own, far_own, range(8), parts=2, adds=[(part_1, 0), (part_2, 3)]
+    )
+    other = core(other)
+    own, cross = [[(mine, n)] for n in range(8)], [[(other, n)] for n in range(8)]
     for n in range(3):
         own[5 + n].append((part_3[0], n))
         cross[5 + n].append((part_3[1], n))
-    spots = lambda s: jnp.stack([(me ^ s ^ (i % 4 * 2)) * 2 + i // 4 for i in range(8)])
-    out = place(spots(0), own, half, None, all_cols, LONG, part_3[1:])
-    return place(spots(1), cross, half, out, all_cols, SHORT)
+
+    def spots(s):
+        at = me ^ s
+        chips = [0, jnp.where(at % 2 == 0, 2, 4), jnp.where(at % 2 == 0, 4, 2), 6]
+        return jnp.stack([(at ^ chips[i % 4]) * 2 + i // 4 for i in range(8)])
+
+    at = arrived(jnp.concatenate([spots(0), spots(1)]), *part_3)
+    return place(at, own + cross, half, all_cols)
 
 
 def solution(mesh):

time: 153 us -> 147 us (0.961)
  waiting for transfers between devices: 55.2 us -> 61.8 us
  Pallas kernels: 59 us -> 52.8 us
  starting transfers between devices: 29 us -> 23.7 us
    ppermute x23 -> x11, starting transfers between devices: 23.7 us -> 5.29 us  [flip(): return lax.ppermute(x, axis, [(i, i ^ bits) for i in range(size)])]
    ppermute x0 -> x9, waiting for transfers between devices: none -> 16.8 us  [over(): lax.ppermute(x, 'seq', [(i, i ^ sides[way][i % 2]) for i in range(seq_siz...]
    ppermute x0 -> x9, starting transfers between devices: none -> 12 us  [over(): lax.ppermute(x, 'seq', [(i, i ^ sides[way][i % 2]) for i in range(seq_siz...]
    ppermute x23 -> x11, waiting for transfers between devices: 53.8 us -> 45 us  [flip(): return lax.ppermute(x, axis, [(i, i ^ bits) for i in range(size)])]
    pallas_call x6 -> x5, Pallas kernels: 29.2 us -> 25.8 us  [the longest x4 24.6 us: share(): pl.pallas_call(functools.partial(share_kernel, len(near), len(near_w), [a...]
    pallas_call x2 -> x1, Pallas kernels: 6.01 us -> 3.86 us  [place(): pl.pallas_call(functools.partial(place_kernel, spots), grid_spec=pltpu.Pr...]
    unnamed x54 -> x44, local copies, waits for them, and re-layouts: 5.66 us -> 5.96 us
  transfers between devices with their start and end apart: 25 -> 22, of which waited for: 11 -> 8; matrix products, arithmetic and copies ran while one was open for 2% -> 2% of each run, Pallas kernels for 37% -> 33%
where the time goes in v3:
time: 147 us
  waiting for transfers between devices  61.8 us (42%)
  Pallas kernels  52.8 us (36%)
  starting transfers between devices  23.7 us (16%)
  local copies, waits for them, and re-layouts  7.77 us (5%)
    ppermute x11, waiting for transfers between devices, flip(): return lax.ppermute(x, axis, [(i, i ^ bits) for i in range(size)])  45 us
    pallas_call x4, Pallas kernels, share(): pl.pallas_call(functools.partial(share_kernel, len(near), len(near_w), [a...  24.6 us
    ppermute x9, waiting for transfers between devices, over(): lax.ppermute(x, 'seq', [(i, i ^ sides[way][i % 2]) for i in range(seq_siz...  16.8 us
    ppermute x9, starting transfers between devices, over(): lax.ppermute(x, 'seq', [(i, i ^ sides[way][i % 2]) for i in range(seq_siz...  12 us
    pallas_call x1, Pallas kernels, local_conv(): pl.pallas_call(functools.partial(local_kernel, width), grid=(chans // TIL...  10.5 us
    pallas_call x2, Pallas kernels, gate(): pl.pallas_call(functools.partial(gate_kernel, modes, width, counts), grid...  7.75 us
    unnamed x44, local copies, waits for them, and re-layouts  5.96 us
    ppermute x11, starting transfers between devices, flip(): return lax.ppermute(x, axis, [(i, i ^ bits) for i in range(size)])  5.29 us
  transfers between devices with their start and end apart: 22, of which 8 were waited for; matrix products, arithmetic and copies ran while one was open for 2% of the time, Pallas kernels for 33%

profile of v3, /device:TPU:0, one launch (start us, length us, event | category | flops | bytes accessed | tf_op | source)
XLA Modules:
  0.0 146.8 jit_solution(2842735812661611831)
XLA Ops:
  0.0 2.9 %collective-permute-start = (bf16[1024,512]{1,0:T(8,128)(2,1)}, bf16[1024,512]{1,0:T(8,128)(2,1)S(1)}, u32[]{:S(2)}, u32[]{:S(2)}) collective-permute-start(bf16[1024,512]{1,0:T(8,128)(2,1)} %refs_8_.1), channel_id=1, source_target_pairs={{0,8},{4,20},{8,0},{12,28},{16,24},{20,4},{24,16},{28,12},{1,9},{5... | collective-permute-start | bytes 3145736 | tf_op jit(solution)/shard_map/ppermute | solution.py:361
  2.9 1.1 slice.6
  4.1 2.7 %collective-permute-start.1 = (bf16[1024,256]{1,0:T(8,128)(2,1)S(1)}, bf16[1024,256]{1,0:T(8,128)(2,1)}, u32[]{:S(2)}, u32[]{:S(2)}) collective-permute-start(bf16[1024,256]{1,0:T(8,128)(2,1)S(1)} %slice.6), channel_id=1, source_target_pairs={{0,2},{1,3},{2,0},{3,1},{4,6},{5,7},{6,4},{7,5},{8,10},{9,11},{10,... | collective-permute-start | bytes 1572872 | tf_op jit(solution)/shard_map/ppermute | solution.py:318
  6.7 5.0 %range_state.1 = (bf16[1024,1024]{1,0:T(8,128)(2,1)}, bf16[8,16,1024]{2,1,0:T(8,128)(2,1)}) custom-call(s32[1]{0:T(128)} %bitcast.16.me_ref, bf16[1024,1024]{1,0:T(8,128)(2,1)} %k_ref.1, bf16[1024,1024]{1,0:T(8,128)(2,1)} %v_ref.1, f32[16,64]{1,0:T(8,128)} %bitcast.20), custom_call_target="tpu_custom_call" | custom-call | flops 1 | bytes 1 | tf_op jit(solution)/shard_map/range_state/pallas_call | solution.py:73
  11.7 3.4 %all-to-all-start = ((bf16[8,16,1024]{2,1,0:T(8,128)(2,1)}), bf16[8,16,1024]{2,1,0:T(8,128)(2,1)S(1)}, u32[]{:S(2)}, u32[]{:S(2)}) async-start(bf16[8,16,1024]{2,1,0:T(8,128)(2,1)} %get-tuple-element.39), calls=%async_computation | async-start | bytes 524288 | tf_op jit(solution)/shard_map/all_to_all | solution.py:338
  15.1 10.5 %local_conv.1 = (bf16[1024,1024]{1,0:T(8,128)(2,1)}, f32[2,1024]{1,0:T(2,128)}) custom-call(bf16[1024,1024]{1,0:T(8,128)(2,1)} %get-tuple-element.35.u_ref, f32[16,64]{1,0:T(8,128)} %bitcast.21, f32[16,64]{1,0:T(8,128)} %bitcast.22), custom_call_target="tpu_custom_call" | custom-call | flops 1 | bytes 1 | tf_op jit(solution)/shard_map/local_conv/pallas_call | solution.py:142
  25.6 0.0 collective-permute-done.refs_4_.refs_5_.refs_9_
  25.6 0.0 all-to-all-done.state_ref
  25.6 0.7 copy-done.5
  26.3 2.6 %gate.2 = bf16[256,1024]{1,0:T(8,128)(2,1)} custom-call(s32[1]{0:T(128)} %bitcast.19.place_ref, bf16[1024,1024]{1,0:T(8,128)(2,1)} %get-tuple-element.41.z_ref, bf16[1024,1024]{1,0:T(8,128)(2,1)} %q_ref.3, f32[2,1024]{1,0:T(2,128)} %get-tuple-element.38.rows_ref, bf16[8,16,1024]{2,1,0:T(8,128)(2,1)} %copy-done.5), custom_call_target="tpu_custom_call" | custom-call | flops 1 | bytes 1 | tf_op jit(solution)/shard_map/gate/pallas_call | solution.py:198
  28.9 0.9 collective-permute-done.1.refs_7_.refs_12_
  29.8 1.0 collective-permute-start.6
  30.8 1.0 collective-permute-start.5
  31.8 1.5 %collective-permute-start.4 = (bf16[1024,256]{1,0:T(8,128)(2,1)}, bf16[1024,256]{1,0:T(8,128)(2,1)S(1)}, u32[]{:S(2)}, u32[]{:S(2)}) collective-permute-start(bf16[1024,256]{1,0:T(8,128)(2,1)} %collective-permute-done.1.refs_7_.refs_12_), channel_id=1, source_target_pairs={{0,8},{4,20},{8,0},{12,28},{16,24},{20,4},{24,16},{28,12},{1,9},{5... | collective-permute-start | bytes 1572872 | tf_op jit(solution)/shard_map/ppermute | solution.py:361
  33.3 0.0 collective-permute-start.3
  33.3 0.5 broadcast_xor_fusion.place_ref
  33.8 5.2 %gate.3 = (bf16[512,1024]{1,0:T(8,128)(2,1)}, bf16[256,1024]{1,0:T(8,128)(2,1)}) custom-call(s32[3]{0:T(128)} %broadcast_xor_fusion.place_ref, bf16[1024,1024]{1,0:T(8,128)(2,1)} %get-tuple-element.41.z_ref, bf16[1024,1024]{1,0:T(8,128)(2,1)} %q_ref.3, f32[2,1024]{1,0:T(2,128)} %get-tuple-element.38.rows_ref, bf16[8,16,1024]{2,1,0:T(8,128)(2,1)} %copy-done.5), custom_call_target="tpu_custom_call" | custom-call | flops 1 | bytes 1 | tf_op jit(solution)/shard_map/gate/pallas_call | solution.py:198
  39.1 16.8 %collective-permute-done.5.refs_9_.refs_14_ = bf16[1024,256]{1,0:T(8,128)(2,1)S(1)} collective-permute-done((bf16[1024,256]{1,0:T(8,128)(2,1)}, bf16[1024,256]{1,0:T(8,128)(2,1)S(1)}, u32[]{:S(2)}, u32[]{:S(2)}) %collective-permute-start.5) | collective-permute-done | bytes 524320 | tf_op jit(solution)/shard_map/ppermute | solution.py:361
  55.8 0.0 collective-permute-done.4.refs_8_.refs_13_
  55.8 2.5 %collective-permute-done.3.refs_2_ = bf16[256,1024]{1,0:T(8,128)(2,1)S(1)} collective-permute-done((bf16[256,1024]{1,0:T(8,128)(2,1)}, bf16[256,1024]{1,0:T(8,128)(2,1)S(1)}, u32[]{:S(2)}, u32[]{:S(2)}) %collective-permute-start.3) | collective-permute-done | bytes 524320 | tf_op jit(solution)/shard_map/ppermute | solution.py:318
  58.3 0.0 collective-permute-done.6.refs_5_.refs_6_.refs_10_
  58.3 0.1 collective-permute-start.7
  58.4 0.5 collective-permute-start.2
  58.9 1.4 collective-permute-done.7.refs_3_
  60.3 0.6 collective-permute-start.9
  60.9 0.0 collective-permute-start.8
  60.9 1.4 collective-permute-start.10
  62.3 0.0 collective-permute-done.2.refs_1_
  62.4 1.0 copy-done.3
  63.4 5.2 %share.6 = bf16[512,768]{1,0:T(8,128)(2,1)} custom-call(bf16[512,1024]{1,0:T(8,128)(2,1)} %get-tuple-element.42.refs_0_, bf16[512,1024]{1,0:T(8,128)(2,1)} %copy-done.3, bf16[256,1024]{1,0:T(8,128)(2,1)} %copy-done.10, bf16[256,1024]{1,0:T(8,128)(2,1)} %copy-done.11, bf16[1024,512]{1,0:T(8,128)(2,1)} %refs_8_.1, bf16[1024,512]{1,0:T(8,128)(2,1)} %copy-done.1, ...), custom_call_target="tpu_custom_call" | custom-call | flops 1 | bytes 1 | tf_op jit(solution)/shard_map/share/pallas_call | solution.py:239
  68.5 1.8 %collective-permute-start.17 = (bf16[512,768]{1,0:T(8,128)(2,1)}, bf16[512,768]{1,0:T(8,128)(2,1)S(1)}, u32[]{:S(2)}, u32[]{:S(2)}) collective-permute-start(bf16[512,768]{1,0:T(8,128)(2,1)} %share.6), channel_id=1, source_target_pairs={{0,1},{1,0},{2,3},{3,2},{4,5},{5,4},{6,7},{7,6},{8,9},{9,8},{10,11... | collective-permute-start | bytes 2359304 | tf_op jit(solution)/shard_map/ppermute | solution.py:318
  70.3 16.0 %collective-permute-done.8.refs_7_.refs_16_ = bf16[1024,256]{1,0:T(8,128)(2,1)S(1)} collective-permute-done((bf16[1024,256]{1,0:T(8,128)(2,1)S(1)}, bf16[1024,256]{1,0:T(8,128)(2,1)S(1)}, u32[]{:S(2)}, u32[]{:S(2)}) %collective-permute-start.8) | collective-permute-done | bytes 524320 | tf_op jit(solution)/shard_map/ppermute | solution.py:318
  86.3 0.0 collective-permute-done.10.refs_6_.refs_15_
  86.3 0.0 collective-permute-done.9.refs_6_.refs_4_.refs_7_.refs_11_
  86.3 0.1 collective-permute-start.12
  86.4 0.6 collective-permute-start.11
  87.0 1.9 %collective-permute-start.14 = (bf16[1024,256]{1,0:T(8,128)(2,1)S(1)}, bf16[1024,256]{1,0:T(8,128)(2,1)S(1)}, u32[]{:S(2)}, u32[]{:S(2)}) collective-permute-start(bf16[1024,256]{1,0:T(8,128)(2,1)S(1)} %collective-permute-done.8.refs_7_.refs_16_), channel_id=1, source_target_pairs={{0,24},{4,28},{8,16},{12,20},{16,8},{20,12},{24,0},{28,4},{1,25},{... | collective-permute-start | bytes 1572872 | tf_op jit(solution)/shard_map/ppermute | solution.py:361
  88.9 1.0 collective-permute-start.13
  90.0 4.2 %share.5 = bf16[512,512]{1,0:T(8,128)(2,1)} custom-call(bf16[512,1024]{1,0:T(8,128)(2,1)} %get-tuple-element.42.refs_0_, bf16[512,1024]{1,0:T(8,128)(2,1)} %copy-done.3, bf16[256,1024]{1,0:T(8,128)(2,1)} %copy-done.10, bf16[256,1024]{1,0:T(8,128)(2,1)} %copy-done.11, bf16[1024,512]{1,0:T(8,128)(2,1)} %copy-done.4, bf16[1024,512]{1,0:T(8,128)(2,1)} %refs_8_.1, ...), custom_call_target="tpu_custom_call" | custom-call | flops 1 | bytes 1 | tf_op jit(solution)/shard_map/share/pallas_call | solution.py:239
  94.2 6.7 %collective-permute-done.17.refs_20_ = bf16[512,768]{1,0:T(8,128)(2,1)S(1)} collective-permute-done((bf16[512,768]{1,0:T(8,128)(2,1)}, bf16[512,768]{1,0:T(8,128)(2,1)S(1)}, u32[]{:S(2)}, u32[]{:S(2)}) %collective-permute-start.17) | collective-permute-done | bytes 786464 | tf_op jit(solution)/shard_map/ppermute | solution.py:318
  100.9 0.0 collective-permute-start.18
  100.9 11.8 %collective-permute-done.12.refs_2_ = bf16[256,1024]{1,0:T(8,128)(2,1)S(1)} collective-permute-done((bf16[256,1024]{1,0:T(8,128)(2,1)}, bf16[256,1024]{1,0:T(8,128)(2,1)S(1)}, u32[]{:S(2)}, u32[]{:S(2)}) %collective-permute-start.12) | collective-permute-done | bytes 524320 | tf_op jit(solution)/shard_map/ppermute | solution.py:318
  112.8 0.0 collective-permute-done.11.refs_7_.refs_17_
  112.8 0.0 collective-permute-done.14.refs_9_.refs_19_
  112.8 0.0 collective-permute-done.13.refs_8_.refs_18_
  112.8 0.8 copy-done.14
  113.6 0.2 copy-done.15
  113.8 0.8 copy-done.16
  114.6 5.1 %share.4 = (bf16[256,768]{1,0:T(8,128)(2,1)}, bf16[256,768]{1,0:T(8,128)(2,1)}) custom-call(bf16[512,1024]{1,0:T(8,128)(2,1)} %get-tuple-element.42.refs_0_, bf16[512,1024]{1,0:T(8,128)(2,1)} %copy-done.3, bf16[256,1024]{1,0:T(8,128)(2,1)} %copy-done.10, bf16[256,1024]{1,0:T(8,128)(2,1)} %copy-done.11, bf16[1024,512]{1,0:T(8,128)(2,1)} %copy-done.1, ...), custom_call_target="tpu_custom_call" | custom-call | flops 68719476736 | bytes 268435456 | tf_op jit(solution)/shard_map/share/pallas_call | solution.py:239
  119.7 0.1 collective-permute-start.19
  119.7 2.9 %collective-permute-start.16 = (bf16[256,768]{1,0:T(8,128)(2,1)}, bf16[256,768]{1,0:T(8,128)(2,1)S(1)}, u32[]{:S(2)}, u32[]{:S(2)}) collective-permute-start(bf16[256,768]{1,0:T(8,128)(2,1)} %get-tuple-element.57), channel_id=1, source_target_pairs={{0,5},{1,4},{2,7},{3,6},{4,1},{5,0},{6,3},{7,2},{8,13},{9,12},{10,... | collective-permute-start | bytes 1179656 | tf_op jit(solution)/shard_map/ppermute | solution.py:357
  122.6 0.0 collective-permute-start.15
  122.7 0.7 concatenate.3.spots_ref
  123.4 0.0 collective-permute-done.18.refs_21_
  123.4 0.0 collective-permute-done.19.refs_3_
  123.4 0.8 copy-done.17
  124.2 0.8 copy-done.18
  125.0 10.1 %share.7 = (bf16[256,2048]{1,0:T(8,128)(2,1)}, bf16[256,2048]{1,0:T(8,128)(2,1)}) custom-call(bf16[512,1024]{1,0:T(8,128)(2,1)} %get-tuple-element.42.refs_0_, bf16[512,1024]{1,0:T(8,128)(2,1)} %copy-done.3, bf16[256,1024]{1,0:T(8,128)(2,1)} %copy-done.13, bf16[256,1024]{1,0:T(8,128)(2,1)} %copy-done.18, bf16[1024,512]{1,0:T(8,128)(2,1)} %refs_8_.1, ...), custom_call_target="tpu_custom_call" | custom-call | flops 1 | bytes 1 | tf_op jit(solution)/shard_map/share/pallas_call | solution.py:239
  135.2 0.1 collective-permute-start.20
  135.2 0.0 collective-permute-done.16.refs_1_.refs_3_
  135.2 5.7 %collective-permute-done.15.refs_0_.refs_1_ = bf16[256,768]{1,0:T(8,128)(2,1)S(1)} collective-permute-done((bf16[256,768]{1,0:T(8,128)(2,1)}, bf16[256,768]{1,0:T(8,128)(2,1)S(1)}, u32[]{:S(2)}, u32[]{:S(2)}) %collective-permute-start.15) | collective-permute-done | bytes 393248 | tf_op jit(solution)/shard_map/ppermute | solution.py:318
  140.9 0.7 copy-done.20
  141.7 1.2 arrived.1.place_ref
  142.9 3.9 %place.1 = bf16[256,4096]{1,0:T(8,128)(2,1)} custom-call(s32[16]{0:T(128)} %arrived.1.place_ref, bf16[256,2048]{1,0:T(8,128)(2,1)} %get-tuple-element.63.refs_0_, bf16[256,768]{1,0:T(8,128)(2,1)} %copy-done.20, bf16[256,2048]{1,0:T(8,128)(2,1)} %collective-permute-done.20.refs_2_, bf16[256,768]{1,0:T(8,128)(2,1)} %copy-done.19), custom_call_target="tpu_custom_call" | custom-call | flops 1 | bytes 1 | tf_op jit(solution)/shard_map/place/pallas_call | solution.py:281
  (38 shorter events, 0.1 us)
Async XLA Ops:
  0.0 25.6 %collective-permute-start = (bf16[1024,512]{1,0:T(8,128)(2,1)}, bf16[1024,512]{1,0:T(8,128)(2,1)S(1)}, u32[]{:S(2)}, u32[]{:S(2)}) collective-permute-start(bf16[1024,512]{1,0:T(8,128)(2,1)} %refs_8_.1), channel_id=1, source_target_pairs={{0,8},{4,20},{8,0},{12,28},{16,24},{20,4},{24,16},{28,12},{1,9},{5... | collective-permute-start | bytes 3145736 | tf_op jit(solution)/shard_map/ppermute | solution.py:361
  4.1 25.7 %collective-permute-start.1 = (bf16[1024,256]{1,0:T(8,128)(2,1)S(1)}, bf16[1024,256]{1,0:T(8,128)(2,1)}, u32[]{:S(2)}, u32[]{:S(2)}) collective-permute-start(bf16[1024,256]{1,0:T(8,128)(2,1)S(1)} %slice.6), channel_id=1, source_target_pairs={{0,2},{1,3},{2,0},{3,1},{4,6},{5,7},{6,4},{7,5},{8,10},{9,11},{10,... | collective-permute-start | bytes 1572872 | tf_op jit(solution)/shard_map/ppermute | solution.py:318
  11.7 13.9 %all-to-all-start = ((bf16[8,16,1024]{2,1,0:T(8,128)(2,1)}), bf16[8,16,1024]{2,1,0:T(8,128)(2,1)S(1)}, u32[]{:S(2)}, u32[]{:S(2)}) async-start(bf16[8,16,1024]{2,1,0:T(8,128)(2,1)} %get-tuple-element.39), calls=%async_computation | async-start | bytes 524288 | tf_op jit(solution)/shard_map/all_to_all | solution.py:338
  25.6 34.7 %copy-start.1 = (bf16[1024,512]{1,0:T(8,128)(2,1)}, bf16[1024,512]{1,0:T(8,128)(2,1)S(1)}, u32[]{:S(2)}) copy-start(bf16[1024,512]{1,0:T(8,128)(2,1)S(1)} %collective-permute-done.refs_4_.refs_5_.refs_9_) | copy-start | bytes 3145732
  25.6 0.7 copy-start.5
  26.3 3.5 %copy-start = (bf16[1024,512]{1,0:T(8,128)(2,1)S(1)}, bf16[1024,512]{1,0:T(8,128)(2,1)}, u32[]{:S(2)}) copy-start(bf16[1024,512]{1,0:T(8,128)(2,1)} %refs_8_.1) | copy-start | bytes 3145732
  26.3 7.0 %copy-start.21 = (s32[3]{0:T(128)S(1)}, s32[3]{0:T(128)}, u32[]{:S(2)}) copy-start(s32[3]{0:T(128)} %constant.41.clone) | copy-start | bytes 40
  29.8 28.6 %collective-permute-start.6 = (bf16[1024,512]{1,0:T(8,128)(2,1)S(1)}, bf16[1024,512]{1,0:T(8,128)(2,1)S(1)}, u32[]{:S(2)}, u32[]{:S(2)}) collective-permute-start(bf16[1024,512]{1,0:T(8,128)(2,1)S(1)} %copy-done), channel_id=1, source_target_pairs={{0,16},{4,12},{8,24},{12,4},{16,0},{20,28},{24,8},{28,20},{1,17},{... | collective-permute-start | bytes 3145736 | tf_op jit(solution)/shard_map/ppermute | solution.py:361
  30.8 25.0 %collective-permute-start.5 = (bf16[1024,256]{1,0:T(8,128)(2,1)}, bf16[1024,256]{1,0:T(8,128)(2,1)S(1)}, u32[]{:S(2)}, u32[]{:S(2)}) collective-permute-start(bf16[1024,256]{1,0:T(8,128)(2,1)} %collective-permute-done.1.refs_7_.refs_12_), channel_id=1, source_target_pairs={{0,16},{4,12},{8,24},{12,4},{16,0},{20,28},{24,8},{28,20},{1,17},{... | collective-permute-start | bytes 1572872 | tf_op jit(solution)/shard_map/ppermute | solution.py:361
  31.8 24.0 %collective-permute-start.4 = (bf16[1024,256]{1,0:T(8,128)(2,1)}, bf16[1024,256]{1,0:T(8,128)(2,1)S(1)}, u32[]{:S(2)}, u32[]{:S(2)}) collective-permute-start(bf16[1024,256]{1,0:T(8,128)(2,1)} %collective-permute-done.1.refs_7_.refs_12_), channel_id=1, source_target_pairs={{0,8},{4,20},{8,0},{12,28},{16,24},{20,4},{24,16},{28,12},{1,9},{5... | collective-permute-start | bytes 1572872 | tf_op jit(solution)/shard_map/ppermute | solution.py:361
  33.3 25.0 %collective-permute-start.3 = (bf16[256,1024]{1,0:T(8,128)(2,1)}, bf16[256,1024]{1,0:T(8,128)(2,1)S(1)}, u32[]{:S(2)}, u32[]{:S(2)}) collective-permute-start(bf16[256,1024]{1,0:T(8,128)(2,1)} %gate.2), channel_id=1, source_target_pairs={{0,2},{1,3},{2,0},{3,1},{4,6},{5,7},{6,4},{7,5},{8,10},{9,11},{10,... | collective-permute-start | bytes 1572872 | tf_op jit(solution)/shard_map/ppermute | solution.py:318
  55.8 6.5 %copy-start.6 = (bf16[1024,256]{1,0:T(8,128)(2,1)}, bf16[1024,256]{1,0:T(8,128)(2,1)S(1)}, u32[]{:S(2)}) copy-start(bf16[1024,256]{1,0:T(8,128)(2,1)S(1)} %collective-permute-done.5.refs_9_.refs_14_) | copy-start | bytes 1572868
  55.8 6.5 %copy-start.7 = (bf16[1024,256]{1,0:T(8,128)(2,1)}, bf16[1024,256]{1,0:T(8,128)(2,1)S(1)}, u32[]{:S(2)}) copy-start(bf16[1024,256]{1,0:T(8,128)(2,1)S(1)} %collective-permute-done.4.refs_8_.refs_13_) | copy-start | bytes 1572868
  58.3 4.0 %copy-start.10 = (bf16[256,1024]{1,0:T(8,128)(2,1)}, bf16[256,1024]{1,0:T(8,128)(2,1)S(1)}, u32[]{:S(2)}) copy-start(bf16[256,1024]{1,0:T(8,128)(2,1)S(1)} %collective-permute-done.3.refs_2_) | copy-start | bytes 1572868
  58.3 4.0 %copy-start.2 = (bf16[1024,512]{1,0:T(8,128)(2,1)}, bf16[1024,512]{1,0:T(8,128)(2,1)S(1)}, u32[]{:S(2)}) copy-start(bf16[1024,512]{1,0:T(8,128)(2,1)S(1)} %collective-permute-done.6.refs_5_.refs_6_.refs_10_) | copy-start | bytes 3145732
  58.3 2.0 %collective-permute-start.7 = (bf16[256,1024]{1,0:T(8,128)(2,1)S(1)}, bf16[256,1024]{1,0:T(8,128)(2,1)S(1)}, u32[]{:S(2)}, u32[]{:S(2)}) collective-permute-start(bf16[256,1024]{1,0:T(8,128)(2,1)S(1)} %collective-permute-done.3.refs_2_), channel_id=1, source_target_pairs={{0,4},{4,0},{8,12},{12,8},{16,20},{20,16},{24,28},{28,24},{1,5},{5... | collective-permute-start | bytes 1572872 | tf_op jit(solution)/shard_map/ppermute | solution.py:318
  58.4 3.9 %collective-permute-start.2 = (bf16[512,1024]{1,0:T(8,128)(2,1)}, bf16[512,1024]{1,0:T(8,128)(2,1)S(1)}, u32[]{:S(2)}, u32[]{:S(2)}) collective-permute-start(bf16[512,1024]{1,0:T(8,128)(2,1)} %get-tuple-element.42.refs_0_), channel_id=1, source_target_pairs={{0,4},{4,0},{8,12},{12,8},{16,20},{20,16},{24,28},{28,24},{1,5},{5... | collective-permute-start | bytes 3145736 | tf_op jit(solution)/shard_map/ppermute | solution.py:318
  60.3 2.1 %copy-start.11 = (bf16[256,1024]{1,0:T(8,128)(2,1)}, bf16[256,1024]{1,0:T(8,128)(2,1)S(1)}, u32[]{:S(2)}) copy-start(bf16[256,1024]{1,0:T(8,128)(2,1)S(1)} %collective-permute-done.7.refs_3_) | copy-start | bytes 1572868
  60.3 26.0 %collective-permute-start.9 = (bf16[1024,512]{1,0:T(8,128)(2,1)S(1)}, bf16[1024,512]{1,0:T(8,128)(2,1)S(1)}, u32[]{:S(2)}, u32[]{:S(2)}) collective-permute-start(bf16[1024,512]{1,0:T(8,128)(2,1)S(1)} %collective-permute-done.refs_4_.refs_5_.refs_9_), channel_id=1, source_target_pairs={{0,16},{4,12},{8,24},{12,4},{16,0},{20,28},{24,8},{28,20},{1,17},{... | collective-permute-start | bytes 3145736 | tf_op jit(solution)/shard_map/ppermute | solution.py:361
  60.9 25.4 %collective-permute-start.8 = (bf16[1024,256]{1,0:T(8,128)(2,1)S(1)}, bf16[1024,256]{1,0:T(8,128)(2,1)S(1)}, u32[]{:S(2)}, u32[]{:S(2)}) collective-permute-start(bf16[1024,256]{1,0:T(8,128)(2,1)S(1)} %slice.7), channel_id=1, source_target_pairs={{0,2},{1,3},{2,0},{3,1},{4,6},{5,7},{6,4},{7,5},{8,10},{9,11},{10,... | collective-permute-start | bytes 1572872 | tf_op jit(solution)/shard_map/ppermute | solution.py:318
  60.9 25.4 %collective-permute-start.10 = (bf16[1024,256]{1,0:T(8,128)(2,1)S(1)}, bf16[1024,256]{1,0:T(8,128)(2,1)S(1)}, u32[]{:S(2)}, u32[]{:S(2)}) collective-permute-start(bf16[1024,256]{1,0:T(8,128)(2,1)S(1)} %collective-permute-done.4.refs_8_.refs_13_), channel_id=1, source_target_pairs={{0,16},{4,12},{8,24},{12,4},{16,0},{20,28},{24,8},{28,20},{1,17},{... | collective-permute-start | bytes 1572872 | tf_op jit(solution)/shard_map/ppermute | solution.py:361
  62.4 1.0 copy-start.3
  68.5 32.4 %collective-permute-start.17 = (bf16[512,768]{1,0:T(8,128)(2,1)}, bf16[512,768]{1,0:T(8,128)(2,1)S(1)}, u32[]{:S(2)}, u32[]{:S(2)}) collective-permute-start(bf16[512,768]{1,0:T(8,128)(2,1)} %share.6), channel_id=1, source_target_pairs={{0,1},{1,0},{2,3},{3,2},{4,5},{5,4},{6,7},{7,6},{8,9},{9,8},{10,11... | collective-permute-start | bytes 2359304 | tf_op jit(solution)/shard_map/ppermute | solution.py:318
  86.3 3.7 %copy-start.8 = (bf16[1024,256]{1,0:T(8,128)(2,1)}, bf16[1024,256]{1,0:T(8,128)(2,1)S(1)}, u32[]{:S(2)}) copy-start(bf16[1024,256]{1,0:T(8,128)(2,1)S(1)} %collective-permute-done.8.refs_7_.refs_16_) | copy-start | bytes 1572868
  86.3 3.7 %copy-start.9 = (bf16[1024,256]{1,0:T(8,128)(2,1)}, bf16[1024,256]{1,0:T(8,128)(2,1)S(1)}, u32[]{:S(2)}) copy-start(bf16[1024,256]{1,0:T(8,128)(2,1)S(1)} %collective-permute-done.10.refs_6_.refs_15_) | copy-start | bytes 1572868
  86.3 3.7 %copy-start.4 = (bf16[1024,512]{1,0:T(8,128)(2,1)}, bf16[1024,512]{1,0:T(8,128)(2,1)S(1)}, u32[]{:S(2)}) copy-start(bf16[1024,512]{1,0:T(8,128)(2,1)S(1)} %collective-permute-done.9.refs_6_.refs_4_.refs_7_.refs_11_) | copy-start | bytes 3145732
  86.3 26.4 %collective-permute-start.12 = (bf16[256,1024]{1,0:T(8,128)(2,1)}, bf16[256,1024]{1,0:T(8,128)(2,1)S(1)}, u32[]{:S(2)}, u32[]{:S(2)}) collective-permute-start(bf16[256,1024]{1,0:T(8,128)(2,1)} %get-tuple-element.54), channel_id=1, source_target_pairs={{0,2},{1,3},{2,0},{3,1},{4,6},{5,7},{6,4},{7,5},{8,10},{9,11},{10,... | collective-permute-start | bytes 1572872 | tf_op jit(solution)/shard_map/ppermute | solution.py:318
  86.4 26.4 %collective-permute-start.11 = (bf16[1024,256]{1,0:T(8,128)(2,1)S(1)}, bf16[1024,256]{1,0:T(8,128)(2,1)S(1)}, u32[]{:S(2)}, u32[]{:S(2)}) collective-permute-start(bf16[1024,256]{1,0:T(8,128)(2,1)S(1)} %collective-permute-done.8.refs_7_.refs_16_), channel_id=1, source_target_pairs={{0,8},{4,20},{8,0},{12,28},{16,24},{20,4},{24,16},{28,12},{1,9},{5... | collective-permute-start | bytes 1572872 | tf_op jit(solution)/shard_map/ppermute | solution.py:361
  87.0 25.7 %collective-permute-start.14 = (bf16[1024,256]{1,0:T(8,128)(2,1)S(1)}, bf16[1024,256]{1,0:T(8,128)(2,1)S(1)}, u32[]{:S(2)}, u32[]{:S(2)}) collective-permute-start(bf16[1024,256]{1,0:T(8,128)(2,1)S(1)} %collective-permute-done.8.refs_7_.refs_16_), channel_id=1, source_target_pairs={{0,24},{4,28},{8,16},{12,20},{16,8},{20,12},{24,0},{28,4},{1,25},{... | collective-permute-start | bytes 1572872 | tf_op jit(solution)/shard_map/ppermute | solution.py:361
  88.9 23.9 %collective-permute-start.13 = (bf16[1024,256]{1,0:T(8,128)(2,1)S(1)}, bf16[1024,256]{1,0:T(8,128)(2,1)S(1)}, u32[]{:S(2)}, u32[]{:S(2)}) collective-permute-start(bf16[1024,256]{1,0:T(8,128)(2,1)S(1)} %collective-permute-done.8.refs_7_.refs_16_), channel_id=1, source_target_pairs={{0,16},{4,12},{8,24},{12,4},{16,0},{20,28},{24,8},{28,20},{1,17},{... | collective-permute-start | bytes 1572872 | tf_op jit(solution)/shard_map/ppermute | solution.py:361
  100.9 18.7 %copy-start.12 = (bf16[512,768]{1,0:T(8,128)(2,1)}, bf16[512,768]{1,0:T(8,128)(2,1)S(1)}, u32[]{:S(2)}) copy-start(bf16[512,768]{1,0:T(8,128)(2,1)S(1)} %collective-permute-done.17.refs_20_) | copy-start | bytes 2359300
  100.9 22.4 %collective-permute-start.18 = (bf16[512,512]{1,0:T(8,128)(2,1)}, bf16[512,512]{1,0:T(8,128)(2,1)S(1)}, u32[]{:S(2)}, u32[]{:S(2)}) collective-permute-start(bf16[512,512]{1,0:T(8,128)(2,1)} %share.5), channel_id=1, source_target_pairs={{0,1},{1,0},{2,3},{3,2},{4,5},{5,4},{6,7},{7,6},{8,9},{9,8},{10,11... | collective-permute-start | bytes 1572872 | tf_op jit(solution)/shard_map/ppermute | solution.py:318
  112.8 6.9 %copy-start.13 = (bf16[256,1024]{1,0:T(8,128)(2,1)}, bf16[256,1024]{1,0:T(8,128)(2,1)S(1)}, u32[]{:S(2)}) copy-start(bf16[256,1024]{1,0:T(8,128)(2,1)S(1)} %collective-permute-done.12.refs_2_) | copy-start | bytes 1572868
  112.8 0.8 copy-start.14
  112.8 1.0 copy-start.15
  113.8 0.8 copy-start.16
  119.7 3.7 %collective-permute-start.19 = (bf16[256,1024]{1,0:T(8,128)(2,1)S(1)}, bf16[256,1024]{1,0:T(8,128)(2,1)S(1)}, u32[]{:S(2)}, u32[]{:S(2)}) collective-permute-start(bf16[256,1024]{1,0:T(8,128)(2,1)S(1)} %collective-permute-done.12.refs_2_), channel_id=1, source_target_pairs={{0,4},{4,0},{8,12},{12,8},{16,20},{20,16},{24,28},{28,24},{1,5},{5... | collective-permute-start | bytes 1572872 | tf_op jit(solution)/shard_map/ppermute | solution.py:318
  119.7 15.5 %collective-permute-start.16 = (bf16[256,768]{1,0:T(8,128)(2,1)}, bf16[256,768]{1,0:T(8,128)(2,1)S(1)}, u32[]{:S(2)}, u32[]{:S(2)}) collective-permute-start(bf16[256,768]{1,0:T(8,128)(2,1)} %get-tuple-element.57), channel_id=1, source_target_pairs={{0,5},{1,4},{2,7},{3,6},{4,1},{5,0},{6,3},{7,2},{8,13},{9,12},{10,... | collective-permute-start | bytes 1179656 | tf_op jit(solution)/shard_map/ppermute | solution.py:357
  122.6 18.3 %collective-permute-start.15 = (bf16[256,768]{1,0:T(8,128)(2,1)}, bf16[256,768]{1,0:T(8,128)(2,1)S(1)}, u32[]{:S(2)}, u32[]{:S(2)}) collective-permute-start(bf16[256,768]{1,0:T(8,128)(2,1)} %get-tuple-element.56), channel_id=1, source_target_pairs={{0,1},{1,0},{2,3},{3,2},{4,5},{5,4},{6,7},{7,6},{8,9},{9,8},{10,11... | collective-permute-start | bytes 1179656 | tf_op jit(solution)/shard_map/ppermute | solution.py:318
  123.4 0.8 copy-start.17
  124.2 0.8 copy-start.18
  135.2 7.7 %collective-permute-start.20 = (bf16[256,2048]{1,0:T(8,128)(2,1)}, bf16[256,2048]{1,0:T(8,128)(2,1)}, u32[]{:S(2)}, u32[]{:S(2)}) collective-permute-start(bf16[256,2048]{1,0:T(8,128)(2,1)} %get-tuple-element.64), channel_id=1, source_target_pairs={{0,4},{4,0},{8,12},{12,8},{16,20},{20,16},{24,28},{28,24},{1,5},{5... | collective-permute-start | bytes 3145736 | tf_op jit(solution)/shard_map/ppermute | solution.py:318
  135.2 5.7 %copy-start.19 = (bf16[256,768]{1,0:T(8,128)(2,1)}, bf16[256,768]{1,0:T(8,128)(2,1)S(1)}, u32[]{:S(2)}) copy-start(bf16[256,768]{1,0:T(8,128)(2,1)S(1)} %collective-permute-done.16.refs_1_.refs_3_) | copy-start | bytes 1179652
  140.9 0.8 copy-start.20

commit v4 on v3

--- a/solution.py
+++ b/solution.py
@@ -244,7 +244,7 @@
         + [whole(*a.shape) for a, _ in adds],
         out_specs=[whole(height // parts, total)] * parts,
         out_shape=[jax.ShapeDtypeStruct((height // parts, total), BF16)] * parts,
-        compiler_params=pltpu.CompilerParams(vmem_limit_bytes=VMEM_BYTES),
+        compiler_params=pltpu.CompilerParams(vmem_limit_bytes=63 << 20),
         cost_estimate=cost,
         name="share",
     )(*[a for a, _ in near + far + near_w + far_w], *[a for a, _ in adds])
@@ -265,7 +265,7 @@
         copy.wait()
 
 
-def place(places, terms, cols, all_cols):
+def place(places, terms, cols, all_cols, out=None):
     arrays, spots = [], []
     for group in terms:
         spot = []
@@ -278,6 +278,11 @@
         spots.append(spot)
     rows = arrays[0].shape[0]
     specs = [pl.BlockSpec(a.shape, lambda i, p: (0, 0)) for a in arrays]
+    alias = {}
+    if out is not None:
+        alias = {1 + len(arrays): 0}
+        arrays.append(out)
+        specs.append(pl.BlockSpec(memory_space=pl.ANY))
     return pl.pallas_call(
         functools.partial(place_kernel, spots),
         grid_spec=pltpu.PrefetchScalarGridSpec(
@@ -291,6 +296,7 @@
             ],
         ),
         out_shape=jax.ShapeDtypeStruct((rows, all_cols), BF16),
+        input_output_aliases=alias,
         compiler_params=pltpu.CompilerParams(vmem_limit_bytes=63 << 20),
         cost_estimate=SHORT,
         name="place",
@@ -372,16 +378,16 @@
     f_a = after(f_a, y_3)
     f_a1, f_a2 = over(f_a, 0), over(f_a, 1)
     n_2 = over(after(out_weight, f_a), 1)
-    near, y_2 = gated((1, 0, 2), (2, 1), n_1, f_a)
+    n_b = after(out_weight, y_3)[:, second]
+    near, y_2 = gated((1, 0, 2), (2, 1), n_1, f_a, n_b)
     near_sib = core(near)
-    n_b = after(out_weight, near)[:, second]
     y_far_other, f_a1, f_a2, n_2, n_b = lax.optimization_barrier(
         (y_far_other, f_a1, f_a2, n_2, n_b)
     )
 
     f_b = far_plane(n_b)
     far_other_sib = core(y_far_other)
-    n_3, f_a3 = over(after(n_1, far_other_sib), 1), over(after(f_a1, far_other_sib), 1)
+    n_3, f_a3 = over(after(n_1, y_far_other), 1), over(after(f_a1, y_far_other), 1)
     near_w, far_w = [(out_weight, 0), (n_1, 0), (n_2, 0)], [(f_a, 0), (f_a1, 0), (f_a2, 0)]
     near_other, near_own = [(near, 0), (near_sib, 0)], [(near, 1), (near_sib, 1)]
     far_other = [(y_far_other, 0), (far_other_sib, 0)]
@@ -419,8 +425,9 @@
         chips = [0, jnp.where(at % 2 == 0, 2, 4), jnp.where(at % 2 == 0, 4, 2), 6]
         return jnp.stack([(at ^ chips[i % 4]) * 2 + i // 4 for i in range(8)])
 
-    at = arrived(jnp.concatenate([spots(0), spots(1)]), *part_3)
-    return place(at, own + cross, half, all_cols)
+    early = place(spots(0)[:5], own[:5], half, all_cols)
+    at = arrived(jnp.concatenate([spots(0)[5:], spots(1)]), *part_3, early)
+    return place(at, own[5:] + cross, half, all_cols, early)
 
 
 def solution(mesh):

time: 147 us -> 145 us (0.986)
  Pallas kernels: 52.8 us -> 55.4 us
  local copies, waits for them, and re-layouts: 7.77 us -> 5.73 us
  waiting for transfers between devices: 61.8 us -> 60.1 us
    ppermute x11, waiting for transfers between devices: 45 us -> 29.5 us  [flip(): return lax.ppermute(x, axis, [(i, i ^ bits) for i in range(size)])]
    ppermute x9, waiting for transfers between devices: 16.8 us -> 27.6 us  [over(): lax.ppermute(x, 'seq', [(i, i ^ sides[way][i % 2]) for i in range(seq_siz...]
    unnamed x44 -> x20, local copies, waits for them, and re-layouts: 5.96 us -> 2.56 us
    ppermute x1, waiting for transfers between devices: 0.01 us -> 3.07 us  [on_device(): next_cross = lambda x: lax.ppermute(x, ('seq', 'ch'), pairs)]
    ppermute x1, starting transfers between devices: 2.91 us -> 0.15 us  [on_device(): next_cross = lambda x: lax.ppermute(x, ('seq', 'ch'), pairs)]
    pallas_call x1 -> x2, Pallas kernels: 3.86 us -> 6.39 us  [place(): pl.pallas_call(functools.partial(place_kernel, spots), grid_spec=pltpu.Pr...]
    ppermute x11, starting transfers between devices: 5.29 us -> 6.97 us  [flip(): return lax.ppermute(x, axis, [(i, i ^ bits) for i in range(size)])]
  transfers between devices with their start and end apart: 22 -> 22, of which waited for: 8 -> 12; matrix products, arithmetic and copies ran while one was open for 2% -> 3% of each run, Pallas kernels for 33% -> 36%
where the time goes in v4:
time: 145 us; the launch traced here: 144 us
  waiting for transfers between devices  60.1 us (41%)
  Pallas kernels  55.4 us (38%)
  starting transfers between devices  22.6 us (16%)
  local copies, waits for them, and re-layouts  5.73 us (4%)
    ppermute x11, waiting for transfers between devices, flip(): return lax.ppermute(x, axis, [(i, i ^ bits) for i in range(size)])  29.5 us
    ppermute x9, waiting for transfers between devices, over(): lax.ppermute(x, 'seq', [(i, i ^ sides[way][i % 2]) for i in range(seq_siz...  27.6 us
    pallas_call x4, Pallas kernels, share(): pl.pallas_call(functools.partial(share_kernel, len(near), len(near_w), [a...  24.6 us
    ppermute x9, starting transfers between devices, over(): lax.ppermute(x, 'seq', [(i, i ^ sides[way][i % 2]) for i in range(seq_siz...  12 us
    pallas_call x1, Pallas kernels, local_conv(): pl.pallas_call(functools.partial(local_kernel, width), grid=(chans // TIL...  10.5 us
    pallas_call x2, Pallas kernels, gate(): pl.pallas_call(functools.partial(gate_kernel, modes, width, counts), grid...  7.75 us
    ppermute x11, starting transfers between devices, flip(): return lax.ppermute(x, axis, [(i, i ^ bits) for i in range(size)])  6.97 us
    pallas_call x2, Pallas kernels, place(): pl.pallas_call(functools.partial(place_kernel, spots), grid_spec=pltpu.Pr...  6.39 us
  transfers between devices with their start and end apart: 22, of which 12 were waited for; matrix products, arithmetic and copies ran while one was open for 3% of the time, Pallas kernels for 36%

profile of v4, /device:TPU:0, one launch (start us, length us, event | category | flops | bytes accessed | tf_op | source)
XLA Modules:
  0.0 144.5 jit_solution(13627401972279564127)
XLA Ops:
  0.0 2.9 %collective-permute-start = (bf16[1024,512]{1,0:T(8,128)(2,1)}, bf16[1024,512]{1,0:T(8,128)(2,1)}, u32[]{:S(2)}, u32[]{:S(2)}) collective-permute-start(bf16[1024,512]{1,0:T(8,128)(2,1)} %refs_8_.1), channel_id=1, source_target_pairs={{0,8},{4,20},{8,0},{12,28},{16,24},{20,4},{24,16},{28,12},{1,9},{5... | collective-permute-start | bytes 3145736 | tf_op jit(solution)/shard_map/ppermute | solution.py:367
  2.9 1.1 slice.6
  4.1 2.7 %collective-permute-start.1 = (bf16[1024,256]{1,0:T(8,128)(2,1)S(1)}, bf16[1024,256]{1,0:T(8,128)(2,1)S(1)}, u32[]{:S(2)}, u32[]{:S(2)}) collective-permute-start(bf16[1024,256]{1,0:T(8,128)(2,1)S(1)} %slice.6), channel_id=1, source_target_pairs={{0,2},{1,3},{2,0},{3,1},{4,6},{5,7},{6,4},{7,5},{8,10},{9,11},{10,... | collective-permute-start | bytes 1572872 | tf_op jit(solution)/shard_map/ppermute | solution.py:324
  6.7 5.0 %range_state.1 = (bf16[1024,1024]{1,0:T(8,128)(2,1)}, bf16[8,16,1024]{2,1,0:T(8,128)(2,1)}) custom-call(s32[1]{0:T(128)} %bitcast.11.me_ref, bf16[1024,1024]{1,0:T(8,128)(2,1)} %k_ref.1, bf16[1024,1024]{1,0:T(8,128)(2,1)} %v_ref.1, f32[16,64]{1,0:T(8,128)} %bitcast.20), custom_call_target="tpu_custom_call" | custom-call | flops 1 | bytes 1 | tf_op jit(solution)/shard_map/range_state/pallas_call | solution.py:73
  11.7 3.4 %all-to-all-start = ((bf16[8,16,1024]{2,1,0:T(8,128)(2,1)}), bf16[8,16,1024]{2,1,0:T(8,128)(2,1)S(1)}, u32[]{:S(2)}, u32[]{:S(2)}) async-start(bf16[8,16,1024]{2,1,0:T(8,128)(2,1)} %get-tuple-element.39), calls=%async_computation | async-start | bytes 524288 | tf_op jit(solution)/shard_map/all_to_all | solution.py:344
  15.1 10.5 %local_conv.1 = (bf16[1024,1024]{1,0:T(8,128)(2,1)}, f32[2,1024]{1,0:T(2,128)}) custom-call(bf16[1024,1024]{1,0:T(8,128)(2,1)} %get-tuple-element.35.u_ref, f32[16,64]{1,0:T(8,128)} %bitcast.21, f32[16,64]{1,0:T(8,128)} %bitcast.22), custom_call_target="tpu_custom_call" | custom-call | flops 1 | bytes 1 | tf_op jit(solution)/shard_map/local_conv/pallas_call | solution.py:142
  25.6 0.0 collective-permute-done.refs_4_.refs_5_.refs_9_
  25.6 0.0 all-to-all-done.state_ref
  25.6 0.7 copy-done.2
  26.3 2.5 %gate.2 = bf16[256,1024]{1,0:T(8,128)(2,1)} custom-call(s32[1]{0:T(128)} %bitcast.14.place_ref, bf16[1024,1024]{1,0:T(8,128)(2,1)} %get-tuple-element.42.z_ref, bf16[1024,1024]{1,0:T(8,128)(2,1)} %q_ref.3, f32[2,1024]{1,0:T(2,128)} %get-tuple-element.38.rows_ref, bf16[8,16,1024]{2,1,0:T(8,128)(2,1)} %copy-done.2), custom_call_target="tpu_custom_call" | custom-call | flops 1 | bytes 1 | tf_op jit(solution)/shard_map/gate/pallas_call | solution.py:198
  28.8 0.8 collective-permute-done.1.refs_7_.refs_12_
  29.7 1.1 collective-permute-start.6
  30.8 1.5 %collective-permute-start.4 = (bf16[1024,256]{1,0:T(8,128)(2,1)S(1)}, bf16[1024,256]{1,0:T(8,128)(2,1)}, u32[]{:S(2)}, u32[]{:S(2)}) collective-permute-start(bf16[1024,256]{1,0:T(8,128)(2,1)S(1)} %collective-permute-done.1.refs_7_.refs_12_), channel_id=1, source_target_pairs={{0,8},{4,20},{8,0},{12,28},{16,24},{20,4},{24,16},{28,12},{1,9},{5... | collective-permute-start | bytes 1572872 | tf_op jit(solution)/shard_map/ppermute | solution.py:367
  32.3 0.9 collective-permute-start.5
  33.2 0.0 collective-permute-start.3
  33.2 0.6 broadcast_xor_fusion.place_ref
  33.8 0.8 slice.7
  34.6 5.2 %gate.3 = (bf16[512,1024]{1,0:T(8,128)(2,1)}, bf16[256,1024]{1,0:T(8,128)(2,1)}) custom-call(s32[3]{0:T(128)} %broadcast_xor_fusion.place_ref, bf16[1024,1024]{1,0:T(8,128)(2,1)} %get-tuple-element.42.z_ref, bf16[1024,1024]{1,0:T(8,128)(2,1)} %q_ref.3, f32[2,1024]{1,0:T(2,128)} %get-tuple-element.38.rows_ref, bf16[8,16,1024]{2,1,0:T(8,128)(2,1)} %copy-done.2), custom_call_target="tpu_custom_call" | custom-call | flops 1 | bytes 1 | tf_op jit(solution)/shard_map/gate/pallas_call | solution.py:198
  39.8 0.0 collective-permute-start.2
  39.8 5.9 %collective-permute-done.4.refs_8_.refs_13_ = bf16[1024,256]{1,0:T(8,128)(2,1)} collective-permute-done((bf16[1024,256]{1,0:T(8,128)(2,1)S(1)}, bf16[1024,256]{1,0:T(8,128)(2,1)}, u32[]{:S(2)}, u32[]{:S(2)}) %collective-permute-start.4) | collective-permute-done | bytes 524320 | tf_op jit(solution)/shard_map/ppermute | solution.py:367
  45.8 9.9 %collective-permute-done.5.refs_9_.refs_14_ = bf16[1024,256]{1,0:T(8,128)(2,1)S(1)} collective-permute-done((bf16[1024,256]{1,0:T(8,128)(2,1)S(1)}, bf16[1024,256]{1,0:T(8,128)(2,1)S(1)}, u32[]{:S(2)}, u32[]{:S(2)}) %collective-permute-start.5) | collective-permute-done | bytes 524320 | tf_op jit(solution)/shard_map/ppermute | solution.py:367
  55.7 2.6 %collective-permute-done.3.refs_2_ = bf16[256,1024]{1,0:T(8,128)(2,1)S(1)} collective-permute-done((bf16[256,1024]{1,0:T(8,128)(2,1)}, bf16[256,1024]{1,0:T(8,128)(2,1)S(1)}, u32[]{:S(2)}, u32[]{:S(2)}) %collective-permute-start.3) | collective-permute-done | bytes 524320 | tf_op jit(solution)/shard_map/ppermute | solution.py:324
  58.3 0.0 collective-permute-done.6.refs_5_.refs_6_.refs_10_
  58.3 1.0 copy-done.1
  59.3 0.5 collective-permute-start.9
  59.9 0.0 copy-done.4
  59.9 0.0 collective-permute-start.7
  59.9 1.5 %collective-permute-start.10 = (bf16[1024,256]{1,0:T(8,128)(2,1)}, bf16[1024,256]{1,0:T(8,128)(2,1)S(1)}, u32[]{:S(2)}, u32[]{:S(2)}) collective-permute-start(bf16[1024,256]{1,0:T(8,128)(2,1)} %collective-permute-done.4.refs_8_.refs_13_), channel_id=1, source_target_pairs={{0,16},{4,12},{8,24},{12,4},{16,0},{20,28},{24,8},{28,20},{1,17},{... | collective-permute-start | bytes 1572872 | tf_op jit(solution)/shard_map/ppermute | solution.py:367
  61.4 0.0 collective-permute-start.8
  61.4 0.0 collective-permute-done.2.refs_1_
  61.4 0.5 collective-permute-done.7.refs_3_
  61.9 5.2 %share.6 = bf16[512,768]{1,0:T(8,128)(2,1)} custom-call(bf16[512,1024]{1,0:T(8,128)(2,1)} %get-tuple-element.43.refs_0_, bf16[512,1024]{1,0:T(8,128)(2,1)} %collective-permute-done.2.refs_1_, bf16[256,1024]{1,0:T(8,128)(2,1)} %copy-done.6, bf16[256,1024]{1,0:T(8,128)(2,1)} %collective-permute-done.7.refs_3_, bf16[1024,512]{1,0:T(8,128)(2,1)} %refs_8_.1, ...), custom_call_target="tpu_custom_call" | custom-call | flops 1 | bytes 1 | tf_op jit(solution)/shard_map/share/pallas_call | solution.py:239
  67.1 1.3 collective-permute-start.17
  68.4 11.6 %collective-permute-done.10.refs_6_.refs_15_ = bf16[1024,256]{1,0:T(8,128)(2,1)S(1)} collective-permute-done((bf16[1024,256]{1,0:T(8,128)(2,1)}, bf16[1024,256]{1,0:T(8,128)(2,1)S(1)}, u32[]{:S(2)}, u32[]{:S(2)}) %collective-permute-start.10) | collective-permute-done | bytes 524320 | tf_op jit(solution)/shard_map/ppermute | solution.py:367
  80.0 6.8 %collective-permute-done.8.refs_7_.refs_16_ = bf16[1024,256]{1,0:T(8,128)(2,1)} collective-permute-done((bf16[1024,256]{1,0:T(8,128)(2,1)}, bf16[1024,256]{1,0:T(8,128)(2,1)}, u32[]{:S(2)}, u32[]{:S(2)}) %collective-permute-start.8) | collective-permute-done | bytes 524320 | tf_op jit(solution)/shard_map/ppermute | solution.py:324
  86.7 0.0 collective-permute-done.9.refs_6_.refs_4_.refs_7_.refs_11_
  86.7 0.0 collective-permute-start.12
  86.7 0.8 collective-permute-start.11
  87.5 1.1 collective-permute-start.13
  88.6 1.6 %collective-permute-start.14 = (bf16[1024,256]{1,0:T(8,128)(2,1)}, bf16[1024,256]{1,0:T(8,128)(2,1)}, u32[]{:S(2)}, u32[]{:S(2)}) collective-permute-start(bf16[1024,256]{1,0:T(8,128)(2,1)} %collective-permute-done.8.refs_7_.refs_16_), channel_id=1, source_target_pairs={{0,24},{4,28},{8,16},{12,20},{16,8},{20,12},{24,0},{28,4},{1,25},{... | collective-permute-start | bytes 1572872 | tf_op jit(solution)/shard_map/ppermute | solution.py:367
  90.2 4.2 %share.5 = bf16[512,512]{1,0:T(8,128)(2,1)} custom-call(bf16[512,1024]{1,0:T(8,128)(2,1)} %get-tuple-element.43.refs_0_, bf16[512,1024]{1,0:T(8,128)(2,1)} %collective-permute-done.2.refs_1_, bf16[256,1024]{1,0:T(8,128)(2,1)} %copy-done.6, bf16[256,1024]{1,0:T(8,128)(2,1)} %collective-permute-done.7.refs_3_, ...), custom_call_target="tpu_custom_call" | custom-call | flops 1 | bytes 1 | tf_op jit(solution)/shard_map/share/pallas_call | solution.py:239
  94.4 5.5 %collective-permute-done.17.refs_20_ = bf16[512,768]{1,0:T(8,128)(2,1)} collective-permute-done((bf16[512,768]{1,0:T(8,128)(2,1)}, bf16[512,768]{1,0:T(8,128)(2,1)}, u32[]{:S(2)}, u32[]{:S(2)}) %collective-permute-start.17) | collective-permute-done | bytes 786464 | tf_op jit(solution)/shard_map/ppermute | solution.py:324
  99.9 0.0 collective-permute-start.18
  99.9 13.2 %collective-permute-done.12.refs_2_ = bf16[256,1024]{1,0:T(8,128)(2,1)} collective-permute-done((bf16[256,1024]{1,0:T(8,128)(2,1)}, bf16[256,1024]{1,0:T(8,128)(2,1)}, u32[]{:S(2)}, u32[]{:S(2)}) %collective-permute-start.12) | collective-permute-done | bytes 524320 | tf_op jit(solution)/shard_map/ppermute | solution.py:324
  113.1 0.0 collective-permute-done.11.refs_7_.refs_17_
  113.1 0.0 collective-permute-done.13.refs_8_.refs_18_
  113.2 0.1 collective-permute-done.14.refs_9_.refs_19_
  113.3 5.1 %share.4 = (bf16[256,768]{1,0:T(8,128)(2,1)}, bf16[256,768]{1,0:T(8,128)(2,1)}) custom-call(bf16[512,1024]{1,0:T(8,128)(2,1)} %get-tuple-element.43.refs_0_, bf16[512,1024]{1,0:T(8,128)(2,1)} %collective-permute-done.2.refs_1_, bf16[256,1024]{1,0:T(8,128)(2,1)} %copy-done.6, bf16[256,1024]{1,0:T(8,128)(2,1)} %collective-permute-done.7.refs_3_, ...), custom_call_target="tpu_custom_call" | custom-call | flops 68719476736 | bytes 268435456 | tf_op jit(solution)/shard_map/share/pallas_call | solution.py:239
  118.4 0.0 collective-permute-start.19
  118.4 2.9 %collective-permute-start.15 = (bf16[256,768]{1,0:T(8,128)(2,1)}, bf16[256,768]{1,0:T(8,128)(2,1)S(1)}, u32[]{:S(2)}, u32[]{:S(2)}) collective-permute-start(bf16[256,768]{1,0:T(8,128)(2,1)} %get-tuple-element.56), channel_id=1, source_target_pairs={{0,1},{1,0},{2,3},{3,2},{4,5},{5,4},{6,7},{7,6},{8,9},{9,8},{10,11... | collective-permute-start | bytes 1179656 | tf_op jit(solution)/shard_map/ppermute | solution.py:324
  121.3 0.1 collective-permute-start.16
  121.4 0.6 stack.67.place_ref
  122.0 0.6 concatenate.3.spots_ref
  122.7 0.1 collective-permute-done.18.refs_21_
  122.7 0.0 collective-permute-done.19.refs_3_
  122.7 0.8 copy-done.7
  123.6 10.2 %share.7 = (bf16[256,2048]{1,0:T(8,128)(2,1)}, bf16[256,2048]{1,0:T(8,128)(2,1)}) custom-call(bf16[512,1024]{1,0:T(8,128)(2,1)} %get-tuple-element.43.refs_0_, bf16[512,1024]{1,0:T(8,128)(2,1)} %collective-permute-done.2.refs_1_, bf16[256,1024]{1,0:T(8,128)(2,1)} %collective-permute-done.12.refs_2_, bf16[256,1024]{1,0:T(8,128)(2,1)} %collective-permute-done.19.refs_3_, ...), custom_call_target="tpu_custom_call" | custom-call | flops 1 | bytes 1 | tf_op jit(solution)/shard_map/share/pallas_call | solution.py:239
  133.7 0.1 collective-permute-start.20
  133.8 2.8 %place.2.refs_2_.refs_4_ = bf16[256,4096]{1,0:T(8,128)(2,1)} custom-call(s32[5]{0:T(128)} %stack.67.place_ref, bf16[256,2048]{1,0:T(8,128)(2,1)} %get-tuple-element.63.refs_0_), custom_call_target="tpu_custom_call" | custom-call | flops 1 | bytes 1 | tf_op jit(solution)/shard_map/place/pallas_call | solution.py:286
  136.5 0.0 collective-permute-done.15.refs_0_.refs_1_
  136.6 3.1 %collective-permute-done.16.refs_1_.refs_3_ = bf16[256,768]{1,0:T(8,128)(2,1)} collective-permute-done((bf16[256,768]{1,0:T(8,128)(2,1)}, bf16[256,768]{1,0:T(8,128)(2,1)}, u32[]{:S(2)}, u32[]{:S(2)}) %collective-permute-start.16) | collective-permute-done | bytes 393248 | tf_op jit(solution)/shard_map/ppermute | solution.py:363
  139.6 1.2 arrived.1.place_ref
  140.8 0.0 collective-permute-done.20.refs_2_
  140.8 3.6 %place.3 = bf16[256,4096]{1,0:T(8,128)(2,1)} custom-call(s32[11]{0:T(128)} %arrived.1.place_ref, bf16[256,2048]{1,0:T(8,128)(2,1)} %get-tuple-element.63.refs_0_, bf16[256,768]{1,0:T(8,128)(2,1)} %copy-done.8, bf16[256,2048]{1,0:T(8,128)(2,1)} %collective-permute-done.20.refs_2_, ...), custom_call_target="tpu_custom_call", output_to_operand_aliasing={{}: (5, {})} | custom-call | flops 1 | bytes 1 | tf_op jit(solution)/shard_map/place/pallas_call | solution.py:286
  (16 shorter events, 0.0 us)
Async XLA Ops:
  0.0 25.6 %collective-permute-start = (bf16[1024,512]{1,0:T(8,128)(2,1)}, bf16[1024,512]{1,0:T(8,128)(2,1)}, u32[]{:S(2)}, u32[]{:S(2)}) collective-permute-start(bf16[1024,512]{1,0:T(8,128)(2,1)} %refs_8_.1), channel_id=1, source_target_pairs={{0,8},{4,20},{8,0},{12,28},{16,24},{20,4},{24,16},{28,12},{1,9},{5... | collective-permute-start | bytes 3145736 | tf_op jit(solution)/shard_map/ppermute | solution.py:367
  4.1 25.6 %collective-permute-start.1 = (bf16[1024,256]{1,0:T(8,128)(2,1)S(1)}, bf16[1024,256]{1,0:T(8,128)(2,1)S(1)}, u32[]{:S(2)}, u32[]{:S(2)}) collective-permute-start(bf16[1024,256]{1,0:T(8,128)(2,1)S(1)} %slice.6), channel_id=1, source_target_pairs={{0,2},{1,3},{2,0},{3,1},{4,6},{5,7},{6,4},{7,5},{8,10},{9,11},{10,... | collective-permute-start | bytes 1572872 | tf_op jit(solution)/shard_map/ppermute | solution.py:324
  11.7 13.9 %all-to-all-start = ((bf16[8,16,1024]{2,1,0:T(8,128)(2,1)}), bf16[8,16,1024]{2,1,0:T(8,128)(2,1)S(1)}, u32[]{:S(2)}, u32[]{:S(2)}) async-start(bf16[8,16,1024]{2,1,0:T(8,128)(2,1)} %get-tuple-element.39), calls=%async_computation | async-start | bytes 524288 | tf_op jit(solution)/shard_map/all_to_all | solution.py:344
  25.6 0.7 copy-start.2
  26.3 3.4 %copy-start = (bf16[1024,512]{1,0:T(8,128)(2,1)S(1)}, bf16[1024,512]{1,0:T(8,128)(2,1)}, u32[]{:S(2)}) copy-start(bf16[1024,512]{1,0:T(8,128)(2,1)} %refs_8_.1) | copy-start | bytes 3145732
  26.3 6.9 %copy-start.9 = (s32[3]{0:T(128)S(1)}, s32[3]{0:T(128)}, u32[]{:S(2)}) copy-start(s32[3]{0:T(128)} %constant.45.clone) | copy-start | bytes 40
  29.7 10.2 %copy-start.3 = (bf16[1024,256]{1,0:T(8,128)(2,1)}, bf16[1024,256]{1,0:T(8,128)(2,1)S(1)}, u32[]{:S(2)}) copy-start(bf16[1024,256]{1,0:T(8,128)(2,1)S(1)} %collective-permute-done.1.refs_7_.refs_12_) | copy-start | bytes 1572868
  29.7 28.7 %collective-permute-start.6 = (bf16[1024,512]{1,0:T(8,128)(2,1)S(1)}, bf16[1024,512]{1,0:T(8,128)(2,1)S(1)}, u32[]{:S(2)}, u32[]{:S(2)}) collective-permute-start(bf16[1024,512]{1,0:T(8,128)(2,1)S(1)} %copy-done), channel_id=1, source_target_pairs={{0,16},{4,12},{8,24},{12,4},{16,0},{20,28},{24,8},{28,20},{1,17},{... | collective-permute-start | bytes 3145736 | tf_op jit(solution)/shard_map/ppermute | solution.py:367
  30.8 15.0 %collective-permute-start.4 = (bf16[1024,256]{1,0:T(8,128)(2,1)S(1)}, bf16[1024,256]{1,0:T(8,128)(2,1)}, u32[]{:S(2)}, u32[]{:S(2)}) collective-permute-start(bf16[1024,256]{1,0:T(8,128)(2,1)S(1)} %collective-permute-done.1.refs_7_.refs_12_), channel_id=1, source_target_pairs={{0,8},{4,20},{8,0},{12,28},{16,24},{20,4},{24,16},{28,12},{1,9},{5... | collective-permute-start | bytes 1572872 | tf_op jit(solution)/shard_map/ppermute | solution.py:367
  32.3 23.4 %collective-permute-start.5 = (bf16[1024,256]{1,0:T(8,128)(2,1)S(1)}, bf16[1024,256]{1,0:T(8,128)(2,1)S(1)}, u32[]{:S(2)}, u32[]{:S(2)}) collective-permute-start(bf16[1024,256]{1,0:T(8,128)(2,1)S(1)} %collective-permute-done.1.refs_7_.refs_12_), channel_id=1, source_target_pairs={{0,16},{4,12},{8,24},{12,4},{16,0},{20,28},{24,8},{28,20},{1,17},{... | collective-permute-start | bytes 1572872 | tf_op jit(solution)/shard_map/ppermute | solution.py:367
  33.2 25.2 %collective-permute-start.3 = (bf16[256,1024]{1,0:T(8,128)(2,1)}, bf16[256,1024]{1,0:T(8,128)(2,1)S(1)}, u32[]{:S(2)}, u32[]{:S(2)}) collective-permute-start(bf16[256,1024]{1,0:T(8,128)(2,1)} %gate.2), channel_id=1, source_target_pairs={{0,2},{1,3},{2,0},{3,1},{4,6},{5,7},{6,4},{7,5},{8,10},{9,11},{10,... | collective-permute-start | bytes 1572872 | tf_op jit(solution)/shard_map/ppermute | solution.py:324
  39.8 21.6 %collective-permute-start.2 = (bf16[512,1024]{1,0:T(8,128)(2,1)}, bf16[512,1024]{1,0:T(8,128)(2,1)}, u32[]{:S(2)}, u32[]{:S(2)}) collective-permute-start(bf16[512,1024]{1,0:T(8,128)(2,1)} %get-tuple-element.43.refs_0_), channel_id=1, source_target_pairs={{0,4},{4,0},{8,12},{12,8},{16,20},{20,16},{24,28},{28,24},{1,5},{5... | collective-permute-start | bytes 3145736 | tf_op jit(solution)/shard_map/ppermute | solution.py:324
  55.7 4.2 %copy-start.4 = (bf16[1024,256]{1,0:T(8,128)(2,1)}, bf16[1024,256]{1,0:T(8,128)(2,1)S(1)}, u32[]{:S(2)}) copy-start(bf16[1024,256]{1,0:T(8,128)(2,1)S(1)} %collective-permute-done.5.refs_9_.refs_14_) | copy-start | bytes 1572868
  58.3 1.5 %copy-start.6 = (bf16[256,1024]{1,0:T(8,128)(2,1)}, bf16[256,1024]{1,0:T(8,128)(2,1)S(1)}, u32[]{:S(2)}) copy-start(bf16[256,1024]{1,0:T(8,128)(2,1)S(1)} %collective-permute-done.3.refs_2_) | copy-start | bytes 1572868
  58.3 1.0 copy-start.1
  59.3 27.4 %collective-permute-start.9 = (bf16[1024,512]{1,0:T(8,128)(2,1)}, bf16[1024,512]{1,0:T(8,128)(2,1)}, u32[]{:S(2)}, u32[]{:S(2)}) collective-permute-start(bf16[1024,512]{1,0:T(8,128)(2,1)} %collective-permute-done.refs_4_.refs_5_.refs_9_), channel_id=1, source_target_pairs={{0,16},{4,12},{8,24},{12,4},{16,0},{20,28},{24,8},{28,20},{1,17},{... | collective-permute-start | bytes 3145736 | tf_op jit(solution)/shard_map/ppermute | solution.py:367
  59.9 2.0 %collective-permute-start.7 = (bf16[256,1024]{1,0:T(8,128)(2,1)S(1)}, bf16[256,1024]{1,0:T(8,128)(2,1)}, u32[]{:S(2)}, u32[]{:S(2)}) collective-permute-start(bf16[256,1024]{1,0:T(8,128)(2,1)S(1)} %collective-permute-done.3.refs_2_), channel_id=1, source_target_pairs={{0,4},{4,0},{8,12},{12,8},{16,20},{20,16},{24,28},{28,24},{1,5},{5... | collective-permute-start | bytes 1572872 | tf_op jit(solution)/shard_map/ppermute | solution.py:324
  59.9 20.1 %collective-permute-start.10 = (bf16[1024,256]{1,0:T(8,128)(2,1)}, bf16[1024,256]{1,0:T(8,128)(2,1)S(1)}, u32[]{:S(2)}, u32[]{:S(2)}) collective-permute-start(bf16[1024,256]{1,0:T(8,128)(2,1)} %collective-permute-done.4.refs_8_.refs_13_), channel_id=1, source_target_pairs={{0,16},{4,12},{8,24},{12,4},{16,0},{20,28},{24,8},{28,20},{1,17},{... | collective-permute-start | bytes 1572872 | tf_op jit(solution)/shard_map/ppermute | solution.py:367
  61.4 25.3 %collective-permute-start.8 = (bf16[1024,256]{1,0:T(8,128)(2,1)}, bf16[1024,256]{1,0:T(8,128)(2,1)}, u32[]{:S(2)}, u32[]{:S(2)}) collective-permute-start(bf16[1024,256]{1,0:T(8,128)(2,1)} %slice.7), channel_id=1, source_target_pairs={{0,2},{1,3},{2,0},{3,1},{4,6},{5,7},{6,4},{7,5},{8,10},{9,11},{10,... | collective-permute-start | bytes 1572872 | tf_op jit(solution)/shard_map/ppermute | solution.py:324
  67.1 32.8 %collective-permute-start.17 = (bf16[512,768]{1,0:T(8,128)(2,1)}, bf16[512,768]{1,0:T(8,128)(2,1)}, u32[]{:S(2)}, u32[]{:S(2)}) collective-permute-start(bf16[512,768]{1,0:T(8,128)(2,1)} %share.6), channel_id=1, source_target_pairs={{0,1},{1,0},{2,3},{3,2},{4,5},{5,4},{6,7},{7,6},{8,9},{9,8},{10,11... | collective-permute-start | bytes 2359304 | tf_op jit(solution)/shard_map/ppermute | solution.py:324
  80.0 10.3 %copy-start.5 = (bf16[1024,256]{1,0:T(8,128)(2,1)}, bf16[1024,256]{1,0:T(8,128)(2,1)S(1)}, u32[]{:S(2)}) copy-start(bf16[1024,256]{1,0:T(8,128)(2,1)S(1)} %collective-permute-done.10.refs_6_.refs_15_) | copy-start | bytes 1572868
  86.7 26.4 %collective-permute-start.12 = (bf16[256,1024]{1,0:T(8,128)(2,1)}, bf16[256,1024]{1,0:T(8,128)(2,1)}, u32[]{:S(2)}, u32[]{:S(2)}) collective-permute-start(bf16[256,1024]{1,0:T(8,128)(2,1)} %get-tuple-element.54), channel_id=1, source_target_pairs={{0,2},{1,3},{2,0},{3,1},{4,6},{5,7},{6,4},{7,5},{8,10},{9,11},{10,... | collective-permute-start | bytes 1572872 | tf_op jit(solution)/shard_map/ppermute | solution.py:324
  86.7 26.4 %collective-permute-start.11 = (bf16[1024,256]{1,0:T(8,128)(2,1)}, bf16[1024,256]{1,0:T(8,128)(2,1)}, u32[]{:S(2)}, u32[]{:S(2)}) collective-permute-start(bf16[1024,256]{1,0:T(8,128)(2,1)} %collective-permute-done.8.refs_7_.refs_16_), channel_id=1, source_target_pairs={{0,8},{4,20},{8,0},{12,28},{16,24},{20,4},{24,16},{28,12},{1,9},{5... | collective-permute-start | bytes 1572872 | tf_op jit(solution)/shard_map/ppermute | solution.py:367
  87.5 25.6 %collective-permute-start.13 = (bf16[1024,256]{1,0:T(8,128)(2,1)}, bf16[1024,256]{1,0:T(8,128)(2,1)}, u32[]{:S(2)}, u32[]{:S(2)}) collective-permute-start(bf16[1024,256]{1,0:T(8,128)(2,1)} %collective-permute-done.8.refs_7_.refs_16_), channel_id=1, source_target_pairs={{0,16},{4,12},{8,24},{12,4},{16,0},{20,28},{24,8},{28,20},{1,17},{... | collective-permute-start | bytes 1572872 | tf_op jit(solution)/shard_map/ppermute | solution.py:367
  88.6 24.7 %collective-permute-start.14 = (bf16[1024,256]{1,0:T(8,128)(2,1)}, bf16[1024,256]{1,0:T(8,128)(2,1)}, u32[]{:S(2)}, u32[]{:S(2)}) collective-permute-start(bf16[1024,256]{1,0:T(8,128)(2,1)} %collective-permute-done.8.refs_7_.refs_16_), channel_id=1, source_target_pairs={{0,24},{4,28},{8,16},{12,20},{16,8},{20,12},{24,0},{28,4},{1,25},{... | collective-permute-start | bytes 1572872 | tf_op jit(solution)/shard_map/ppermute | solution.py:367
  99.9 22.8 %collective-permute-start.18 = (bf16[512,512]{1,0:T(8,128)(2,1)}, bf16[512,512]{1,0:T(8,128)(2,1)S(1)}, u32[]{:S(2)}, u32[]{:S(2)}) collective-permute-start(bf16[512,512]{1,0:T(8,128)(2,1)} %share.5), channel_id=1, source_target_pairs={{0,1},{1,0},{2,3},{3,2},{4,5},{5,4},{6,7},{7,6},{8,9},{9,8},{10,11... | collective-permute-start | bytes 1572872 | tf_op jit(solution)/shard_map/ppermute | solution.py:324
  118.4 4.3 %collective-permute-start.19 = (bf16[256,1024]{1,0:T(8,128)(2,1)}, bf16[256,1024]{1,0:T(8,128)(2,1)}, u32[]{:S(2)}, u32[]{:S(2)}) collective-permute-start(bf16[256,1024]{1,0:T(8,128)(2,1)} %collective-permute-done.12.refs_2_), channel_id=1, source_target_pairs={{0,4},{4,0},{8,12},{12,8},{16,20},{20,16},{24,28},{28,24},{1,5},{5... | collective-permute-start | bytes 1572872 | tf_op jit(solution)/shard_map/ppermute | solution.py:324
  118.4 18.2 %collective-permute-start.15 = (bf16[256,768]{1,0:T(8,128)(2,1)}, bf16[256,768]{1,0:T(8,128)(2,1)S(1)}, u32[]{:S(2)}, u32[]{:S(2)}) collective-permute-start(bf16[256,768]{1,0:T(8,128)(2,1)} %get-tuple-element.56), channel_id=1, source_target_pairs={{0,1},{1,0},{2,3},{3,2},{4,5},{5,4},{6,7},{7,6},{8,9},{9,8},{10,11... | collective-permute-start | bytes 1179656 | tf_op jit(solution)/shard_map/ppermute | solution.py:324
  121.3 18.3 %collective-permute-start.16 = (bf16[256,768]{1,0:T(8,128)(2,1)}, bf16[256,768]{1,0:T(8,128)(2,1)}, u32[]{:S(2)}, u32[]{:S(2)}) collective-permute-start(bf16[256,768]{1,0:T(8,128)(2,1)} %get-tuple-element.57), channel_id=1, source_target_pairs={{0,5},{1,4},{2,7},{3,6},{4,1},{5,0},{6,3},{7,2},{8,13},{9,12},{10,... | collective-permute-start | bytes 1179656 | tf_op jit(solution)/shard_map/ppermute | solution.py:363
  122.7 0.8 copy-start.7
  133.7 7.1 %collective-permute-start.20 = (bf16[256,2048]{1,0:T(8,128)(2,1)}, bf16[256,2048]{1,0:T(8,128)(2,1)}, u32[]{:S(2)}, u32[]{:S(2)}) collective-permute-start(bf16[256,2048]{1,0:T(8,128)(2,1)} %get-tuple-element.64), channel_id=1, source_target_pairs={{0,4},{4,0},{8,12},{12,8},{16,20},{20,16},{24,28},{28,24},{1,5},{5... | collective-permute-start | bytes 3145736 | tf_op jit(solution)/shard_map/ppermute | solution.py:324
  136.5 3.1 %copy-start.8 = (bf16[256,768]{1,0:T(8,128)(2,1)}, bf16[256,768]{1,0:T(8,128)(2,1)S(1)}, u32[]{:S(2)}) copy-start(bf16[256,768]{1,0:T(8,128)(2,1)S(1)} %collective-permute-done.15.refs_0_.refs_1_) | copy-start | bytes 1179652

commit v5 on v4

--- a/solution.py
+++ b/solution.py
@@ -44,7 +44,7 @@
 
 
 def range_state_kernel(width, me_ref, k_ref, v_ref, rate_ref, u_ref, f_ref):
-    u = (k_ref[...].astype(F32) * v_ref[...].astype(F32)).astype(BF16)
+    u = k_ref[...] * v_ref[...]
     u_ref[...] = u
     toks, cols = u.shape
     modes = rate_ref.shape[0]
@@ -88,10 +88,10 @@
     )(me, key_feat, value_feat, rates)
 
 
-def local_kernel(width, u_ref, rate_ref, res_ref, z_ref, rows_ref, taps_ref, split_ref):
+def local_tile(width, tile, u_ref, rate_ref, res_ref, z_ref, rows_ref, taps_ref, split_ref):
     modes, groups = rate_ref.shape[0], TILE // width
     rows = groups * modes
-    rate, res = (as_column(r[...], pl.program_id(0) * groups, groups) for r in (rate_ref, res_ref))
+    rate, res = (as_column(r[...], tile * groups, groups) for r in (rate_ref, res_ref))
     rate_row, res_row = as_row(rate), as_row(res)
     rows_ref[0:1, :] = rate_row
     rows_ref[1:2, :] = res_row
@@ -132,25 +132,36 @@
         ).astype(BF16)
 
 
+def local_kernel(width, u_ref, rate_ref, res_ref, z_ref, rows_ref, taps_ref, split_ref):
+    tiles = u_ref.shape[1] // TILE
+    per_tile = rows_ref.shape[1] // tiles
+    for t in range(tiles):
+        lanes = pl.ds(t * TILE, TILE)
+        local_tile(
+            width, pl.program_id(0) * tiles + t, u_ref.at[:, lanes], rate_ref, res_ref, z_ref.at[:, lanes],
+            rows_ref.at[:, pl.ds(t * per_tile, per_tile)], taps_ref.at[t], split_ref.at[t],
+        )
+
+
 def local_conv(u, rates, residues, width):
     toks, chans = u.shape
     modes = rates.shape[0]
     groups = TILE // width
-    rows = groups * modes
+    rows, tiles = groups * modes, 2
     table = pl.BlockSpec(rates.shape, lambda i: (0, 0))
-    feat = pl.BlockSpec((toks, TILE), lambda i: (0, i))
+    feat = pl.BlockSpec((toks, tiles * TILE), lambda i: (0, i))
     return pl.pallas_call(
         functools.partial(local_kernel, width),
-        grid=(chans // TILE,),
+        grid=(chans // TILE // tiles,),
         in_specs=[feat, table, table],
-        out_specs=[feat, pl.BlockSpec((2, rows), lambda i: (0, i))],
+        out_specs=[feat, pl.BlockSpec((2, tiles * rows), lambda i: (0, i))],
         out_shape=[
             jax.ShapeDtypeStruct((toks, chans), BF16),
             jax.ShapeDtypeStruct((2, rates.size), F32),
         ],
         scratch_shapes=[
-            pltpu.VMEM((SUB, groups * SUB), BF16),
-            pltpu.VMEM((groups * SUB, toks // SUB * TILE), BF16),
+            pltpu.VMEM((tiles, SUB, groups * SUB), BF16),
+            pltpu.VMEM((tiles, groups * SUB, toks // SUB * TILE), BF16),
         ],
         compiler_params=pltpu.CompilerParams(vmem_limit_bytes=VMEM_BYTES),
         cost_estimate=SHORT,
@@ -374,20 +385,20 @@
     n_1 = over(out_weight, 0)
     (y_3,) = gated((3,), (1,), n_1)
 
-    y_far_other = far_plane(y_3)
+    y_far_other = far_plane(after(y_3, f_a))
     f_a = after(f_a, y_3)
     f_a1, f_a2 = over(f_a, 0), over(f_a, 1)
     n_2 = over(after(out_weight, f_a), 1)
     n_b = after(out_weight, y_3)[:, second]
     near, y_2 = gated((1, 0, 2), (2, 1), n_1, f_a, n_b)
     near_sib = core(near)
-    y_far_other, f_a1, f_a2, n_2, n_b = lax.optimization_barrier(
-        (y_far_other, f_a1, f_a2, n_2, n_b)
-    )
+    there = arrived(me.reshape(1), y_far_other)
+    f_a1, f_a2, n_2, _ = lax.optimization_barrier((f_a1, f_a2, n_2, there))
+    n_b = after(n_b, y_far_other)
 
     f_b = far_plane(n_b)
     far_other_sib = core(y_far_other)
-    n_3, f_a3 = over(after(n_1, y_far_other), 1), over(after(f_a1, y_far_other), 1)
+    n_3, f_a3 = over(after(n_1, there), 1), over(after(f_a1, there), 1)
     near_w, far_w = [(out_weight, 0), (n_1, 0), (n_2, 0)], [(f_a, 0), (f_a1, 0), (f_a2, 0)]
     near_other, near_own = [(near, 0), (near_sib, 0)], [(near, 1), (near_sib, 1)]
     far_other = [(y_far_other, 0), (far_other_sib, 0)]

time: 145 us -> 142 us (0.979)
  waiting for transfers between devices: 60.1 us -> 57.1 us
    ppermute x9, waiting for transfers between devices: 27.6 us -> 0.02 us  [over(): lax.ppermute(x, 'seq', [(i, i ^ sides[way][i % 2]) for i in range(seq_siz...]
    ppermute x11, waiting for transfers between devices: 29.5 us -> 54.1 us  [flip(): return lax.ppermute(x, axis, [(i, i ^ bits) for i in range(size)])]
  transfers between devices with their start and end apart: 22 -> 22, of which waited for: 12 -> 8; matrix products, arithmetic and copies ran while one was open for 3% -> 3% of each run, Pallas kernels for 36% -> 36%
where the time goes in v5:
time: 142 us; the launch traced here: 141 us
  waiting for transfers between devices  57.1 us (40%)
  Pallas kernels  54.3 us (38%)
  starting transfers between devices  23.2 us (16%)
  local copies, waits for them, and re-layouts  5.92 us (4%)
    ppermute x11, waiting for transfers between devices, flip(): return lax.ppermute(x, axis, [(i, i ^ bits) for i in range(size)])  54.1 us
    pallas_call x4, Pallas kernels, share(): pl.pallas_call(functools.partial(share_kernel, len(near), len(near_w), [a...  24.6 us
    ppermute x9, starting transfers between devices, over(): lax.ppermute(x, 'seq', [(i, i ^ sides[way][i % 2]) for i in range(seq_siz...  12 us
    pallas_call x1, Pallas kernels, local_conv(): pl.pallas_call(functools.partial(local_kernel, width), grid=(chans // TIL...  9.61 us
    pallas_call x2, Pallas kernels, gate(): pl.pallas_call(functools.partial(gate_kernel, modes, width, counts), grid...  7.81 us
    ppermute x11, starting transfers between devices, flip(): return lax.ppermute(x, axis, [(i, i ^ bits) for i in range(size)])  7.64 us
    pallas_call x2, Pallas kernels, place(): pl.pallas_call(functools.partial(place_kernel, spots), grid_spec=pltpu.Pr...  6.39 us
    pallas_call x1, Pallas kernels, range_state(): pl.pallas_call(functools.partial(range_state_kernel, width), grid_spec=pl...  4.77 us
  transfers between devices with their start and end apart: 22, of which 8 were waited for; matrix products, arithmetic and copies ran while one was open for 3% of the time, Pallas kernels for 36%

profile of v5, /device:TPU:0, one launch (start us, length us, event | category | flops | bytes accessed | tf_op | source)
XLA Modules:
  0.0 141.3 jit_solution(17061714265642736687)
XLA Ops:
  0.0 2.9 %collective-permute-start = (bf16[1024,512]{1,0:T(8,128)(2,1)}, bf16[1024,512]{1,0:T(8,128)(2,1)}, u32[]{:S(2)}, u32[]{:S(2)}) collective-permute-start(bf16[1024,512]{1,0:T(8,128)(2,1)} %refs_8_.1), channel_id=1, source_target_pairs={{0,8},{4,20},{8,0},{12,28},{16,24},{20,4},{24,16},{28,12},{1,9},{5... | collective-permute-start | bytes 3145736 | tf_op jit(solution)/shard_map/ppermute | solution.py:378
  2.9 1.1 slice.6
  4.1 2.7 %collective-permute-start.1 = (bf16[1024,256]{1,0:T(8,128)(2,1)S(1)}, bf16[1024,256]{1,0:T(8,128)(2,1)S(1)}, u32[]{:S(2)}, u32[]{:S(2)}) collective-permute-start(bf16[1024,256]{1,0:T(8,128)(2,1)S(1)} %slice.6), channel_id=1, source_target_pairs={{0,2},{1,3},{2,0},{3,1},{4,6},{5,7},{6,4},{7,5},{8,10},{9,11},{10,... | collective-permute-start | bytes 1572872 | tf_op jit(solution)/shard_map/ppermute | solution.py:335
  6.7 4.8 %range_state.1 = (bf16[1024,1024]{1,0:T(8,128)(2,1)}, bf16[8,16,1024]{2,1,0:T(8,128)(2,1)}) custom-call(s32[1]{0:T(128)} %bitcast.11.me_ref, bf16[1024,1024]{1,0:T(8,128)(2,1)} %k_ref.1, bf16[1024,1024]{1,0:T(8,128)(2,1)} %v_ref.1, f32[16,64]{1,0:T(8,128)} %bitcast.20), custom_call_target="tpu_custom_call" | custom-call | flops 1 | bytes 1 | tf_op jit(solution)/shard_map/range_state/pallas_call | solution.py:73
  11.5 3.4 %all-to-all-start = ((bf16[8,16,1024]{2,1,0:T(8,128)(2,1)}), bf16[8,16,1024]{2,1,0:T(8,128)(2,1)S(1)}, u32[]{:S(2)}, u32[]{:S(2)}) async-start(bf16[8,16,1024]{2,1,0:T(8,128)(2,1)} %get-tuple-element.39), calls=%async_computation | async-start | bytes 524288 | tf_op jit(solution)/shard_map/all_to_all | solution.py:355
  14.9 9.6 %local_conv.1 = (bf16[1024,1024]{1,0:T(8,128)(2,1)}, f32[2,1024]{1,0:T(2,128)}) custom-call(bf16[1024,1024]{1,0:T(8,128)(2,1)} %get-tuple-element.35.u_ref, f32[16,64]{1,0:T(8,128)} %bitcast.21, f32[16,64]{1,0:T(8,128)} %bitcast.22), custom_call_target="tpu_custom_call" | custom-call | flops 1 | bytes 1 | tf_op jit(solution)/shard_map/local_conv/pallas_call | solution.py:153
  24.5 0.0 collective-permute-done.refs_4_.refs_5_.refs_9_
  24.5 0.0 all-to-all-done.state_ref
  24.5 0.7 copy-done.2
  25.2 2.6 %gate.2 = bf16[256,1024]{1,0:T(8,128)(2,1)} custom-call(s32[1]{0:T(128)} %bitcast.14.place_ref, bf16[1024,1024]{1,0:T(8,128)(2,1)} %get-tuple-element.42.z_ref, bf16[1024,1024]{1,0:T(8,128)(2,1)} %q_ref.3, f32[2,1024]{1,0:T(2,128)} %get-tuple-element.38.rows_ref, bf16[8,16,1024]{2,1,0:T(8,128)(2,1)} %copy-done.2), custom_call_target="tpu_custom_call" | custom-call | flops 1 | bytes 1 | tf_op jit(solution)/shard_map/gate/pallas_call | solution.py:209
  27.8 1.9 %collective-permute-done.1.refs_7_.refs_12_ = bf16[1024,256]{1,0:T(8,128)(2,1)S(1)} collective-permute-done((bf16[1024,256]{1,0:T(8,128)(2,1)S(1)}, bf16[1024,256]{1,0:T(8,128)(2,1)S(1)}, u32[]{:S(2)}, u32[]{:S(2)}) %collective-permute-start.1) | collective-permute-done | bytes 524320 | tf_op jit(solution)/shard_map/ppermute | solution.py:335
  29.7 0.0 collective-permute-start.3
  29.7 0.6 broadcast_xor_fusion.place_ref
  30.2 1.5 %collective-permute-start.5 = (bf16[1024,256]{1,0:T(8,128)(2,1)S(1)}, bf16[1024,256]{1,0:T(8,128)(2,1)}, u32[]{:S(2)}, u32[]{:S(2)}) collective-permute-start(bf16[1024,256]{1,0:T(8,128)(2,1)S(1)} %collective-permute-done.1.refs_7_.refs_12_), channel_id=1, source_target_pairs={{0,8},{4,20},{8,0},{12,28},{16,24},{20,4},{24,16},{28,12},{1,9},{5... | collective-permute-start | bytes 1572872 | tf_op jit(solution)/shard_map/ppermute | solution.py:378
  31.7 0.5 collective-permute-start.6
  32.3 1.5 %collective-permute-start.7 = (bf16[1024,512]{1,0:T(8,128)(2,1)S(1)}, bf16[1024,512]{1,0:T(8,128)(2,1)S(1)}, u32[]{:S(2)}, u32[]{:S(2)}) collective-permute-start(bf16[1024,512]{1,0:T(8,128)(2,1)S(1)} %copy-done), channel_id=1, source_target_pairs={{0,16},{4,12},{8,24},{12,4},{16,0},{20,28},{24,8},{28,20},{1,17},{... | collective-permute-start | bytes 3145736 | tf_op jit(solution)/shard_map/ppermute | solution.py:378
  33.8 0.9 slice.7
  34.6 5.2 %gate.3 = (bf16[512,1024]{1,0:T(8,128)(2,1)}, bf16[256,1024]{1,0:T(8,128)(2,1)}) custom-call(s32[3]{0:T(128)} %broadcast_xor_fusion.place_ref, bf16[1024,1024]{1,0:T(8,128)(2,1)} %get-tuple-element.42.z_ref, bf16[1024,1024]{1,0:T(8,128)(2,1)} %q_ref.3, f32[2,1024]{1,0:T(2,128)} %get-tuple-element.38.rows_ref, bf16[8,16,1024]{2,1,0:T(8,128)(2,1)} %copy-done.2), custom_call_target="tpu_custom_call" | custom-call | flops 1 | bytes 1 | tf_op jit(solution)/shard_map/gate/pallas_call | solution.py:209
  39.9 0.0 copy-done.3
  39.9 0.0 collective-permute-start.2
  39.9 14.9 %collective-permute-done.3.refs_2_ = bf16[256,1024]{1,0:T(8,128)(2,1)S(1)} collective-permute-done((bf16[256,1024]{1,0:T(8,128)(2,1)}, bf16[256,1024]{1,0:T(8,128)(2,1)S(1)}, u32[]{:S(2)}, u32[]{:S(2)}) %collective-permute-start.3) | collective-permute-done | bytes 524320 | tf_op jit(solution)/shard_map/ppermute | solution.py:335
  54.8 1.3 collective-permute-start.9
  56.1 0.0 collective-permute-done.5.refs_8_.refs_13_
  56.1 0.2 collective-permute-start.4
  56.2 0.0 collective-permute-done.6.refs_9_.refs_14_
  56.2 0.0 collective-permute-start.8
  56.3 0.0 collective-permute-done.7.refs_5_.refs_6_.refs_10_
  56.3 1.1 copy-done.1
  57.3 0.7 collective-permute-start.10
  58.0 0.0 collective-permute-done.2.refs_1_
  58.0 0.1 collective-permute-done.4.refs_3_
  58.1 5.1 %share.6 = bf16[512,768]{1,0:T(8,128)(2,1)} custom-call(bf16[512,1024]{1,0:T(8,128)(2,1)} %get-tuple-element.43.refs_0_, bf16[512,1024]{1,0:T(8,128)(2,1)} %collective-permute-done.2.refs_1_, bf16[256,1024]{1,0:T(8,128)(2,1)} %copy-done.6, bf16[256,1024]{1,0:T(8,128)(2,1)} %collective-permute-done.4.refs_3_, bf16[1024,512]{1,0:T(8,128)(2,1)} %refs_8_.1, ...), custom_call_target="tpu_custom_call" | custom-call | flops 1 | bytes 1 | tf_op jit(solution)/shard_map/share/pallas_call | solution.py:250
  63.3 2.5 %collective-permute-start.17 = (bf16[512,768]{1,0:T(8,128)(2,1)}, bf16[512,768]{1,0:T(8,128)(2,1)}, u32[]{:S(2)}, u32[]{:S(2)}) collective-permute-start(bf16[512,768]{1,0:T(8,128)(2,1)} %share.6), channel_id=1, source_target_pairs={{0,1},{1,0},{2,3},{3,2},{4,5},{5,4},{6,7},{7,6},{8,9},{9,8},{10,11... | collective-permute-start | bytes 2359304 | tf_op jit(solution)/shard_map/ppermute | solution.py:335
  65.7 16.3 %collective-permute-done.8.refs_7_.refs_16_ = bf16[1024,256]{1,0:T(8,128)(2,1)S(1)} collective-permute-done((bf16[1024,256]{1,0:T(8,128)(2,1)}, bf16[1024,256]{1,0:T(8,128)(2,1)S(1)}, u32[]{:S(2)}, u32[]{:S(2)}) %collective-permute-start.8) | collective-permute-done | bytes 524320 | tf_op jit(solution)/shard_map/ppermute | solution.py:335
  82.0 0.0 collective-permute-done.10.refs_6_.refs_15_
  82.0 0.0 collective-permute-done.9.refs_6_.refs_4_.refs_7_.refs_11_
  82.0 0.1 collective-permute-start.12
  82.1 1.0 collective-permute-start.11
  83.1 1.8 %collective-permute-start.13 = (bf16[1024,256]{1,0:T(8,128)(2,1)S(1)}, bf16[1024,256]{1,0:T(8,128)(2,1)}, u32[]{:S(2)}, u32[]{:S(2)}) collective-permute-start(bf16[1024,256]{1,0:T(8,128)(2,1)S(1)} %collective-permute-done.8.refs_7_.refs_16_), channel_id=1, source_target_pairs={{0,16},{4,12},{8,24},{12,4},{16,0},{20,28},{24,8},{28,20},{1,17},{... | collective-permute-start | bytes 1572872 | tf_op jit(solution)/shard_map/ppermute | solution.py:378
  84.9 0.8 collective-permute-start.14
  85.6 4.2 %share.5 = bf16[512,512]{1,0:T(8,128)(2,1)} custom-call(bf16[512,1024]{1,0:T(8,128)(2,1)} %get-tuple-element.43.refs_0_, bf16[512,1024]{1,0:T(8,128)(2,1)} %collective-permute-done.2.refs_1_, bf16[256,1024]{1,0:T(8,128)(2,1)} %copy-done.6, bf16[256,1024]{1,0:T(8,128)(2,1)} %collective-permute-done.4.refs_3_, ...), custom_call_target="tpu_custom_call" | custom-call | flops 1 | bytes 1 | tf_op jit(solution)/shard_map/share/pallas_call | solution.py:250
  89.8 7.2 %collective-permute-done.17.refs_20_ = bf16[512,768]{1,0:T(8,128)(2,1)} collective-permute-done((bf16[512,768]{1,0:T(8,128)(2,1)}, bf16[512,768]{1,0:T(8,128)(2,1)}, u32[]{:S(2)}, u32[]{:S(2)}) %collective-permute-start.17) | collective-permute-done | bytes 786464 | tf_op jit(solution)/shard_map/ppermute | solution.py:335
  97.0 0.0 collective-permute-start.18
  97.0 11.5 %collective-permute-done.12.refs_2_ = bf16[256,1024]{1,0:T(8,128)(2,1)} collective-permute-done((bf16[256,1024]{1,0:T(8,128)(2,1)}, bf16[256,1024]{1,0:T(8,128)(2,1)}, u32[]{:S(2)}, u32[]{:S(2)}) %collective-permute-start.12) | collective-permute-done | bytes 524320 | tf_op jit(solution)/shard_map/ppermute | solution.py:335
  108.5 0.0 collective-permute-done.11.refs_7_.refs_17_
  108.5 0.0 collective-permute-done.13.refs_8_.refs_18_
  108.5 0.0 collective-permute-done.14.refs_9_.refs_19_
  108.5 5.1 %share.4 = (bf16[256,768]{1,0:T(8,128)(2,1)}, bf16[256,768]{1,0:T(8,128)(2,1)}) custom-call(bf16[512,1024]{1,0:T(8,128)(2,1)} %get-tuple-element.43.refs_0_, bf16[512,1024]{1,0:T(8,128)(2,1)} %collective-permute-done.2.refs_1_, bf16[256,1024]{1,0:T(8,128)(2,1)} %copy-done.6, bf16[256,1024]{1,0:T(8,128)(2,1)} %collective-permute-done.4.refs_3_, ...), custom_call_target="tpu_custom_call" | custom-call | flops 68719476736 | bytes 268435456 | tf_op jit(solution)/shard_map/share/pallas_call | solution.py:250
  113.6 0.0 collective-permute-start.19
  113.6 2.2 %collective-permute-start.15 = (bf16[256,768]{1,0:T(8,128)(2,1)}, bf16[256,768]{1,0:T(8,128)(2,1)S(1)}, u32[]{:S(2)}, u32[]{:S(2)}) collective-permute-start(bf16[256,768]{1,0:T(8,128)(2,1)} %get-tuple-element.56), channel_id=1, source_target_pairs={{0,1},{1,0},{2,3},{3,2},{4,5},{5,4},{6,7},{7,6},{8,9},{9,8},{10,11... | collective-permute-start | bytes 1179656 | tf_op jit(solution)/shard_map/ppermute | solution.py:335
  115.8 0.1 collective-permute-start.16
  116.0 0.7 stack.67.place_ref
  116.7 0.7 concatenate.3.spots_ref
  117.3 2.3 %collective-permute-done.18.refs_21_ = bf16[512,512]{1,0:T(8,128)(2,1)} collective-permute-done((bf16[512,512]{1,0:T(8,128)(2,1)}, bf16[512,512]{1,0:T(8,128)(2,1)}, u32[]{:S(2)}, u32[]{:S(2)}) %collective-permute-start.18) | collective-permute-done | bytes 524320 | tf_op jit(solution)/shard_map/ppermute | solution.py:335
  119.7 0.0 collective-permute-done.19.refs_3_
  119.7 0.8 copy-done.7
  120.5 10.1 %share.7 = (bf16[256,2048]{1,0:T(8,128)(2,1)}, bf16[256,2048]{1,0:T(8,128)(2,1)}) custom-call(bf16[512,1024]{1,0:T(8,128)(2,1)} %get-tuple-element.43.refs_0_, bf16[512,1024]{1,0:T(8,128)(2,1)} %collective-permute-done.2.refs_1_, bf16[256,1024]{1,0:T(8,128)(2,1)} %collective-permute-done.12.refs_2_, bf16[256,1024]{1,0:T(8,128)(2,1)} %copy-done.7, ...), custom_call_target="tpu_custom_call" | custom-call | flops 1 | bytes 1 | tf_op jit(solution)/shard_map/share/pallas_call | solution.py:250
  130.6 0.0 collective-permute-start.20
  130.6 2.8 %place.2.refs_2_.refs_4_ = bf16[256,4096]{1,0:T(8,128)(2,1)} custom-call(s32[5]{0:T(128)} %stack.67.place_ref, bf16[256,2048]{1,0:T(8,128)(2,1)} %get-tuple-element.63.refs_0_), custom_call_target="tpu_custom_call" | custom-call | flops 1 | bytes 1 | tf_op jit(solution)/shard_map/place/pallas_call | solution.py:297
  133.4 0.0 collective-permute-done.15.refs_0_.refs_1_
  133.4 3.0 %collective-permute-done.16.refs_1_.refs_3_ = bf16[256,768]{1,0:T(8,128)(2,1)} collective-permute-done((bf16[256,768]{1,0:T(8,128)(2,1)}, bf16[256,768]{1,0:T(8,128)(2,1)}, u32[]{:S(2)}, u32[]{:S(2)}) %collective-permute-start.16) | collective-permute-done | bytes 393248 | tf_op jit(solution)/shard_map/ppermute | solution.py:374
  136.4 1.2 arrived.2.place_ref
  137.6 0.0 collective-permute-done.20.refs_2_
  137.6 3.6 %place.3 = bf16[256,4096]{1,0:T(8,128)(2,1)} custom-call(s32[11]{0:T(128)} %arrived.2.place_ref, bf16[256,2048]{1,0:T(8,128)(2,1)} %get-tuple-element.63.refs_0_, bf16[256,768]{1,0:T(8,128)(2,1)} %copy-done.8, bf16[256,2048]{1,0:T(8,128)(2,1)} %collective-permute-done.20.refs_2_, ...), custom_call_target="tpu_custom_call", output_to_operand_aliasing={{}: (5, {})} | custom-call | flops 1 | bytes 1 | tf_op jit(solution)/shard_map/place/pallas_call | solution.py:297
  (16 shorter events, 0.0 us)
Async XLA Ops:
  0.0 24.5 %collective-permute-start = (bf16[1024,512]{1,0:T(8,128)(2,1)}, bf16[1024,512]{1,0:T(8,128)(2,1)}, u32[]{:S(2)}, u32[]{:S(2)}) collective-permute-start(bf16[1024,512]{1,0:T(8,128)(2,1)} %refs_8_.1), channel_id=1, source_target_pairs={{0,8},{4,20},{8,0},{12,28},{16,24},{20,4},{24,16},{28,12},{1,9},{5... | collective-permute-start | bytes 3145736 | tf_op jit(solution)/shard_map/ppermute | solution.py:378
  4.1 25.6 %collective-permute-start.1 = (bf16[1024,256]{1,0:T(8,128)(2,1)S(1)}, bf16[1024,256]{1,0:T(8,128)(2,1)S(1)}, u32[]{:S(2)}, u32[]{:S(2)}) collective-permute-start(bf16[1024,256]{1,0:T(8,128)(2,1)S(1)} %slice.6), channel_id=1, source_target_pairs={{0,2},{1,3},{2,0},{3,1},{4,6},{5,7},{6,4},{7,5},{8,10},{9,11},{10,... | collective-permute-start | bytes 1572872 | tf_op jit(solution)/shard_map/ppermute | solution.py:335
  11.5 13.0 %all-to-all-start = ((bf16[8,16,1024]{2,1,0:T(8,128)(2,1)}), bf16[8,16,1024]{2,1,0:T(8,128)(2,1)S(1)}, u32[]{:S(2)}, u32[]{:S(2)}) async-start(bf16[8,16,1024]{2,1,0:T(8,128)(2,1)} %get-tuple-element.39), calls=%async_computation | async-start | bytes 524288 | tf_op jit(solution)/shard_map/all_to_all | solution.py:355
  24.5 0.7 copy-start.2
  25.2 4.4 %copy-start.9 = (s32[3]{0:T(128)S(1)}, s32[3]{0:T(128)}, u32[]{:S(2)}) copy-start(s32[3]{0:T(128)} %constant.45.clone) | copy-start | bytes 40
  25.2 7.0 %copy-start = (bf16[1024,512]{1,0:T(8,128)(2,1)S(1)}, bf16[1024,512]{1,0:T(8,128)(2,1)}, u32[]{:S(2)}) copy-start(bf16[1024,512]{1,0:T(8,128)(2,1)} %refs_8_.1) | copy-start | bytes 3145732
  29.7 10.2 %copy-start.3 = (bf16[1024,256]{1,0:T(8,128)(2,1)}, bf16[1024,256]{1,0:T(8,128)(2,1)S(1)}, u32[]{:S(2)}) copy-start(bf16[1024,256]{1,0:T(8,128)(2,1)S(1)} %collective-permute-done.1.refs_7_.refs_12_) | copy-start | bytes 1572868
  29.7 25.1 %collective-permute-start.3 = (bf16[256,1024]{1,0:T(8,128)(2,1)}, bf16[256,1024]{1,0:T(8,128)(2,1)S(1)}, u32[]{:S(2)}, u32[]{:S(2)}) collective-permute-start(bf16[256,1024]{1,0:T(8,128)(2,1)} %gate.2), channel_id=1, source_target_pairs={{0,2},{1,3},{2,0},{3,1},{4,6},{5,7},{6,4},{7,5},{8,10},{9,11},{10,... | collective-permute-start | bytes 1572872 | tf_op jit(solution)/shard_map/ppermute | solution.py:335
  30.2 25.8 %collective-permute-start.5 = (bf16[1024,256]{1,0:T(8,128)(2,1)S(1)}, bf16[1024,256]{1,0:T(8,128)(2,1)}, u32[]{:S(2)}, u32[]{:S(2)}) collective-permute-start(bf16[1024,256]{1,0:T(8,128)(2,1)S(1)} %collective-permute-done.1.refs_7_.refs_12_), channel_id=1, source_target_pairs={{0,8},{4,20},{8,0},{12,28},{16,24},{20,4},{24,16},{28,12},{1,9},{5... | collective-permute-start | bytes 1572872 | tf_op jit(solution)/shard_map/ppermute | solution.py:378
  31.7 24.5 %collective-permute-start.6 = (bf16[1024,256]{1,0:T(8,128)(2,1)S(1)}, bf16[1024,256]{1,0:T(8,128)(2,1)S(1)}, u32[]{:S(2)}, u32[]{:S(2)}) collective-permute-start(bf16[1024,256]{1,0:T(8,128)(2,1)S(1)} %collective-permute-done.1.refs_7_.refs_12_), channel_id=1, source_target_pairs={{0,16},{4,12},{8,24},{12,4},{16,0},{20,28},{24,8},{28,20},{1,17},{... | collective-permute-start | bytes 1572872 | tf_op jit(solution)/shard_map/ppermute | solution.py:378
  32.3 24.0 %collective-permute-start.7 = (bf16[1024,512]{1,0:T(8,128)(2,1)S(1)}, bf16[1024,512]{1,0:T(8,128)(2,1)S(1)}, u32[]{:S(2)}, u32[]{:S(2)}) collective-permute-start(bf16[1024,512]{1,0:T(8,128)(2,1)S(1)} %copy-done), channel_id=1, source_target_pairs={{0,16},{4,12},{8,24},{12,4},{16,0},{20,28},{24,8},{28,20},{1,17},{... | collective-permute-start | bytes 3145736 | tf_op jit(solution)/shard_map/ppermute | solution.py:378
  39.9 18.2 %collective-permute-start.2 = (bf16[512,1024]{1,0:T(8,128)(2,1)}, bf16[512,1024]{1,0:T(8,128)(2,1)}, u32[]{:S(2)}, u32[]{:S(2)}) collective-permute-start(bf16[512,1024]{1,0:T(8,128)(2,1)} %get-tuple-element.43.refs_0_), channel_id=1, source_target_pairs={{0,4},{4,0},{8,12},{12,8},{16,20},{20,16},{24,28},{28,24},{1,5},{5... | collective-permute-start | bytes 3145736 | tf_op jit(solution)/shard_map/ppermute | solution.py:335
  54.8 3.2 %copy-start.6 = (bf16[256,1024]{1,0:T(8,128)(2,1)}, bf16[256,1024]{1,0:T(8,128)(2,1)S(1)}, u32[]{:S(2)}) copy-start(bf16[256,1024]{1,0:T(8,128)(2,1)S(1)} %collective-permute-done.3.refs_2_) | copy-start | bytes 1572868
  54.8 27.2 %collective-permute-start.9 = (bf16[1024,512]{1,0:T(8,128)(2,1)}, bf16[1024,512]{1,0:T(8,128)(2,1)}, u32[]{:S(2)}, u32[]{:S(2)}) collective-permute-start(bf16[1024,512]{1,0:T(8,128)(2,1)} %collective-permute-done.refs_4_.refs_5_.refs_9_), channel_id=1, source_target_pairs={{0,16},{4,12},{8,24},{12,4},{16,0},{20,28},{24,8},{28,20},{1,17},{... | collective-permute-start | bytes 3145736 | tf_op jit(solution)/shard_map/ppermute | solution.py:378
  56.1 2.0 %collective-permute-start.4 = (bf16[256,1024]{1,0:T(8,128)(2,1)S(1)}, bf16[256,1024]{1,0:T(8,128)(2,1)}, u32[]{:S(2)}, u32[]{:S(2)}) collective-permute-start(bf16[256,1024]{1,0:T(8,128)(2,1)S(1)} %collective-permute-done.3.refs_2_), channel_id=1, source_target_pairs={{0,4},{4,0},{8,12},{12,8},{16,20},{20,16},{24,28},{28,24},{1,5},{5... | collective-permute-start | bytes 1572872 | tf_op jit(solution)/shard_map/ppermute | solution.py:335
  56.2 1.8 %copy-start.4 = (bf16[1024,256]{1,0:T(8,128)(2,1)}, bf16[1024,256]{1,0:T(8,128)(2,1)S(1)}, u32[]{:S(2)}) copy-start(bf16[1024,256]{1,0:T(8,128)(2,1)S(1)} %collective-permute-done.6.refs_9_.refs_14_) | copy-start | bytes 1572868
  56.2 25.8 %collective-permute-start.8 = (bf16[1024,256]{1,0:T(8,128)(2,1)}, bf16[1024,256]{1,0:T(8,128)(2,1)S(1)}, u32[]{:S(2)}, u32[]{:S(2)}) collective-permute-start(bf16[1024,256]{1,0:T(8,128)(2,1)} %slice.7), channel_id=1, source_target_pairs={{0,2},{1,3},{2,0},{3,1},{4,6},{5,7},{6,4},{7,5},{8,10},{9,11},{10,... | collective-permute-start | bytes 1572872 | tf_op jit(solution)/shard_map/ppermute | solution.py:335
  56.3 1.1 copy-start.1
  57.3 24.7 %collective-permute-start.10 = (bf16[1024,256]{1,0:T(8,128)(2,1)}, bf16[1024,256]{1,0:T(8,128)(2,1)}, u32[]{:S(2)}, u32[]{:S(2)}) collective-permute-start(bf16[1024,256]{1,0:T(8,128)(2,1)} %collective-permute-done.5.refs_8_.refs_13_), channel_id=1, source_target_pairs={{0,16},{4,12},{8,24},{12,4},{16,0},{20,28},{24,8},{28,20},{1,17},{... | collective-permute-start | bytes 1572872 | tf_op jit(solution)/shard_map/ppermute | solution.py:378
  63.3 33.8 %collective-permute-start.17 = (bf16[512,768]{1,0:T(8,128)(2,1)}, bf16[512,768]{1,0:T(8,128)(2,1)}, u32[]{:S(2)}, u32[]{:S(2)}) collective-permute-start(bf16[512,768]{1,0:T(8,128)(2,1)} %share.6), channel_id=1, source_target_pairs={{0,1},{1,0},{2,3},{3,2},{4,5},{5,4},{6,7},{7,6},{8,9},{9,8},{10,11... | collective-permute-start | bytes 2359304 | tf_op jit(solution)/shard_map/ppermute | solution.py:335
  82.0 3.6 %copy-start.5 = (bf16[1024,256]{1,0:T(8,128)(2,1)}, bf16[1024,256]{1,0:T(8,128)(2,1)S(1)}, u32[]{:S(2)}) copy-start(bf16[1024,256]{1,0:T(8,128)(2,1)S(1)} %collective-permute-done.8.refs_7_.refs_16_) | copy-start | bytes 1572868
  82.0 26.5 %collective-permute-start.12 = (bf16[256,1024]{1,0:T(8,128)(2,1)}, bf16[256,1024]{1,0:T(8,128)(2,1)}, u32[]{:S(2)}, u32[]{:S(2)}) collective-permute-start(bf16[256,1024]{1,0:T(8,128)(2,1)} %get-tuple-element.54), channel_id=1, source_target_pairs={{0,2},{1,3},{2,0},{3,1},{4,6},{5,7},{6,4},{7,5},{8,10},{9,11},{10,... | collective-permute-start | bytes 1572872 | tf_op jit(solution)/shard_map/ppermute | solution.py:335
  82.1 26.4 %collective-permute-start.11 = (bf16[1024,256]{1,0:T(8,128)(2,1)S(1)}, bf16[1024,256]{1,0:T(8,128)(2,1)}, u32[]{:S(2)}, u32[]{:S(2)}) collective-permute-start(bf16[1024,256]{1,0:T(8,128)(2,1)S(1)} %collective-permute-done.8.refs_7_.refs_16_), channel_id=1, source_target_pairs={{0,8},{4,20},{8,0},{12,28},{16,24},{20,4},{24,16},{28,12},{1,9},{5... | collective-permute-start | bytes 1572872 | tf_op jit(solution)/shard_map/ppermute | solution.py:378
  83.1 25.4 %collective-permute-start.13 = (bf16[1024,256]{1,0:T(8,128)(2,1)S(1)}, bf16[1024,256]{1,0:T(8,128)(2,1)}, u32[]{:S(2)}, u32[]{:S(2)}) collective-permute-start(bf16[1024,256]{1,0:T(8,128)(2,1)S(1)} %collective-permute-done.8.refs_7_.refs_16_), channel_id=1, source_target_pairs={{0,16},{4,12},{8,24},{12,4},{16,0},{20,28},{24,8},{28,20},{1,17},{... | collective-permute-start | bytes 1572872 | tf_op jit(solution)/shard_map/ppermute | solution.py:378
  84.9 23.6 %collective-permute-start.14 = (bf16[1024,256]{1,0:T(8,128)(2,1)S(1)}, bf16[1024,256]{1,0:T(8,128)(2,1)}, u32[]{:S(2)}, u32[]{:S(2)}) collective-permute-start(bf16[1024,256]{1,0:T(8,128)(2,1)S(1)} %collective-permute-done.8.refs_7_.refs_16_), channel_id=1, source_target_pairs={{0,24},{4,28},{8,16},{12,20},{16,8},{20,12},{24,0},{28,4},{1,25},{... | collective-permute-start | bytes 1572872 | tf_op jit(solution)/shard_map/ppermute | solution.py:378
  97.0 22.6 %collective-permute-start.18 = (bf16[512,512]{1,0:T(8,128)(2,1)}, bf16[512,512]{1,0:T(8,128)(2,1)}, u32[]{:S(2)}, u32[]{:S(2)}) collective-permute-start(bf16[512,512]{1,0:T(8,128)(2,1)} %share.5), channel_id=1, source_target_pairs={{0,1},{1,0},{2,3},{3,2},{4,5},{5,4},{6,7},{7,6},{8,9},{9,8},{10,11... | collective-permute-start | bytes 1572872 | tf_op jit(solution)/shard_map/ppermute | solution.py:335
  113.6 6.0 %collective-permute-start.19 = (bf16[256,1024]{1,0:T(8,128)(2,1)}, bf16[256,1024]{1,0:T(8,128)(2,1)S(1)}, u32[]{:S(2)}, u32[]{:S(2)}) collective-permute-start(bf16[256,1024]{1,0:T(8,128)(2,1)} %collective-permute-done.12.refs_2_), channel_id=1, source_target_pairs={{0,4},{4,0},{8,12},{12,8},{16,20},{20,16},{24,28},{28,24},{1,5},{5... | collective-permute-start | bytes 1572872 | tf_op jit(solution)/shard_map/ppermute | solution.py:335
  113.6 19.8 %collective-permute-start.15 = (bf16[256,768]{1,0:T(8,128)(2,1)}, bf16[256,768]{1,0:T(8,128)(2,1)S(1)}, u32[]{:S(2)}, u32[]{:S(2)}) collective-permute-start(bf16[256,768]{1,0:T(8,128)(2,1)} %get-tuple-element.56), channel_id=1, source_target_pairs={{0,1},{1,0},{2,3},{3,2},{4,5},{5,4},{6,7},{7,6},{8,9},{9,8},{10,11... | collective-permute-start | bytes 1179656 | tf_op jit(solution)/shard_map/ppermute | solution.py:335
  115.8 20.6 %collective-permute-start.16 = (bf16[256,768]{1,0:T(8,128)(2,1)}, bf16[256,768]{1,0:T(8,128)(2,1)}, u32[]{:S(2)}, u32[]{:S(2)}) collective-permute-start(bf16[256,768]{1,0:T(8,128)(2,1)} %get-tuple-element.57), channel_id=1, source_target_pairs={{0,5},{1,4},{2,7},{3,6},{4,1},{5,0},{6,3},{7,2},{8,13},{9,12},{10,... | collective-permute-start | bytes 1179656 | tf_op jit(solution)/shard_map/ppermute | solution.py:374
  119.7 0.8 copy-start.7
  130.6 7.0 %collective-permute-start.20 = (bf16[256,2048]{1,0:T(8,128)(2,1)}, bf16[256,2048]{1,0:T(8,128)(2,1)}, u32[]{:S(2)}, u32[]{:S(2)}) collective-permute-start(bf16[256,2048]{1,0:T(8,128)(2,1)} %get-tuple-element.64), channel_id=1, source_target_pairs={{0,4},{4,0},{8,12},{12,8},{16,20},{20,16},{24,28},{28,24},{1,5},{5... | collective-permute-start | bytes 3145736 | tf_op jit(solution)/shard_map/ppermute | solution.py:335
  133.4 3.0 %copy-start.8 = (bf16[256,768]{1,0:T(8,128)(2,1)}, bf16[256,768]{1,0:T(8,128)(2,1)S(1)}, u32[]{:S(2)}) copy-start(bf16[256,768]{1,0:T(8,128)(2,1)S(1)} %collective-permute-done.15.refs_0_.refs_1_) | copy-start | bytes 1179652

commit v6 on v5

--- a/solution.py
+++ b/solution.py
@@ -68,7 +68,7 @@
 def range_state(me, key_feat, value_feat, rates, seq_size, width):
     toks, chans = key_feat.shape
     modes = rates.shape[0]
-    step = 256
+    step = 512
     feat = pl.BlockSpec((toks, step), lambda i, p: (0, i))
     return pl.pallas_call(
         functools.partial(range_state_kernel, width),
@@ -215,7 +215,7 @@
             out_specs=[result(sum(counts[:n]), count) for n, count in enumerate(counts)],
         ),
         out_shape=[jax.ShapeDtypeStruct((n * SUB, chans), BF16) for n in counts],
-        compiler_params=pltpu.CompilerParams(vmem_limit_bytes=VMEM_BYTES),
+        compiler_params=pltpu.CompilerParams(vmem_limit_bytes=VMEM_BYTES if sum(counts) == 1 else 63 << 20),
         cost_estimate=SHORT,
         name="gate",
     )(places, z, query_feat, rows, states)

time: 142 us -> 142 us (level)
    ppermute x11, waiting for transfers between devices: 54.1 us -> 55.6 us  [flip(): return lax.ppermute(x, axis, [(i, i ^ bits) for i in range(size)])]
where the time goes in v6:
time: 142 us; the launch traced here: 141 us
  waiting for transfers between devices  58.5 us (41%)
  Pallas kernels  54.2 us (38%)
  starting transfers between devices  22 us (15%)
  local copies, waits for them, and re-layouts  5.91 us (4%)
    ppermute x11, waiting for transfers between devices, flip(): return lax.ppermute(x, axis, [(i, i ^ bits) for i in range(size)])  55.6 us
    pallas_call x4, Pallas kernels, share(): pl.pallas_call(functools.partial(share_kernel, len(near), len(near_w), [a...  24.6 us
    ppermute x9, starting transfers between devices, over(): lax.ppermute(x, 'seq', [(i, i ^ sides[way][i % 2]) for i in range(seq_siz...  12 us
    pallas_call x1, Pallas kernels, local_conv(): pl.pallas_call(functools.partial(local_kernel, width), grid=(chans // TIL...  9.67 us
    pallas_call x2, Pallas kernels, gate(): pl.pallas_call(functools.partial(gate_kernel, modes, width, counts), grid...  7.71 us
    ppermute x11, starting transfers between devices, flip(): return lax.ppermute(x, axis, [(i, i ^ bits) for i in range(size)])  6.43 us
    pallas_call x2, Pallas kernels, place(): pl.pallas_call(functools.partial(place_kernel, spots), grid_spec=pltpu.Pr...  6.4 us
    pallas_call x1, Pallas kernels, range_state(): pl.pallas_call(functools.partial(range_state_kernel, width), grid_spec=pl...  4.66 us
  transfers between devices with their start and end apart: 22, of which 8 were waited for; matrix products, arithmetic and copies ran while one was open for 3% of the time, Pallas kernels for 36%

profile of v6, /device:TPU:0, one launch (start us, length us, event | category | flops | bytes accessed | tf_op | source)
XLA Modules:
  0.0 141.3 jit_solution(1438984207966045719)
XLA Ops:
  0.0 2.9 %collective-permute-start = (bf16[1024,512]{1,0:T(8,128)(2,1)}, bf16[1024,512]{1,0:T(8,128)(2,1)S(1)}, u32[]{:S(2)}, u32[]{:S(2)}) collective-permute-start(bf16[1024,512]{1,0:T(8,128)(2,1)} %refs_8_.1), channel_id=1, source_target_pairs={{0,8},{4,20},{8,0},{12,28},{16,24},{20,4},{24,16},{28,12},{1,9},{5... | collective-permute-start | bytes 3145736 | tf_op jit(solution)/shard_map/ppermute | solution.py:378
  2.9 1.1 slice.6
  4.1 2.7 %collective-permute-start.1 = (bf16[1024,256]{1,0:T(8,128)(2,1)S(1)}, bf16[1024,256]{1,0:T(8,128)(2,1)S(1)}, u32[]{:S(2)}, u32[]{:S(2)}) collective-permute-start(bf16[1024,256]{1,0:T(8,128)(2,1)S(1)} %slice.6), channel_id=1, source_target_pairs={{0,2},{1,3},{2,0},{3,1},{4,6},{5,7},{6,4},{7,5},{8,10},{9,11},{10,... | collective-permute-start | bytes 1572872 | tf_op jit(solution)/shard_map/ppermute | solution.py:335
  6.7 4.7 %range_state.1 = (bf16[1024,1024]{1,0:T(8,128)(2,1)}, bf16[8,16,1024]{2,1,0:T(8,128)(2,1)}) custom-call(s32[1]{0:T(128)} %bitcast.11.me_ref, bf16[1024,1024]{1,0:T(8,128)(2,1)} %k_ref.1, bf16[1024,1024]{1,0:T(8,128)(2,1)} %v_ref.1, f32[16,64]{1,0:T(8,128)} %bitcast.20), custom_call_target="tpu_custom_call" | custom-call | flops 1 | bytes 1 | tf_op jit(solution)/shard_map/range_state/pallas_call | solution.py:73
  11.4 3.4 %all-to-all-start = ((bf16[8,16,1024]{2,1,0:T(8,128)(2,1)}), bf16[8,16,1024]{2,1,0:T(8,128)(2,1)S(1)}, u32[]{:S(2)}, u32[]{:S(2)}) async-start(bf16[8,16,1024]{2,1,0:T(8,128)(2,1)} %get-tuple-element.39), calls=%async_computation | async-start | bytes 524288 | tf_op jit(solution)/shard_map/all_to_all | solution.py:355
  14.8 9.7 %local_conv.1 = (bf16[1024,1024]{1,0:T(8,128)(2,1)}, f32[2,1024]{1,0:T(2,128)}) custom-call(bf16[1024,1024]{1,0:T(8,128)(2,1)} %get-tuple-element.35.u_ref, f32[16,64]{1,0:T(8,128)} %bitcast.21, f32[16,64]{1,0:T(8,128)} %bitcast.22), custom_call_target="tpu_custom_call" | custom-call | flops 1 | bytes 1 | tf_op jit(solution)/shard_map/local_conv/pallas_call | solution.py:153
  24.4 0.0 collective-permute-done.refs_4_.refs_5_.refs_9_
  24.5 0.0 all-to-all-done.state_ref
  24.5 0.0 copy-start.1
  24.5 0.7 copy-done.1
  25.2 2.5 %gate.2 = bf16[256,1024]{1,0:T(8,128)(2,1)} custom-call(s32[1]{0:T(128)} %bitcast.14.place_ref, bf16[1024,1024]{1,0:T(8,128)(2,1)} %get-tuple-element.42.z_ref, bf16[1024,1024]{1,0:T(8,128)(2,1)} %q_ref.3, f32[2,1024]{1,0:T(2,128)} %get-tuple-element.38.rows_ref, bf16[8,16,1024]{2,1,0:T(8,128)(2,1)} %copy-done.1), custom_call_target="tpu_custom_call" | custom-call | flops 1 | bytes 1 | tf_op jit(solution)/shard_map/gate/pallas_call | solution.py:209
  27.7 0.0 copy-done
  27.7 2.0 %collective-permute-done.1.refs_7_.refs_12_ = bf16[1024,256]{1,0:T(8,128)(2,1)S(1)} collective-permute-done((bf16[1024,256]{1,0:T(8,128)(2,1)S(1)}, bf16[1024,256]{1,0:T(8,128)(2,1)S(1)}, u32[]{:S(2)}, u32[]{:S(2)}) %collective-permute-start.1) | collective-permute-done | bytes 524320 | tf_op jit(solution)/shard_map/ppermute | solution.py:335
  29.7 0.0 collective-permute-start.3
  29.7 0.6 broadcast_xor_fusion.place_ref
  30.3 1.5 %collective-permute-start.5 = (bf16[1024,256]{1,0:T(8,128)(2,1)S(1)}, bf16[1024,256]{1,0:T(8,128)(2,1)}, u32[]{:S(2)}, u32[]{:S(2)}) collective-permute-start(bf16[1024,256]{1,0:T(8,128)(2,1)S(1)} %collective-permute-done.1.refs_7_.refs_12_), channel_id=1, source_target_pairs={{0,8},{4,20},{8,0},{12,28},{16,24},{20,4},{24,16},{28,12},{1,9},{5... | collective-permute-start | bytes 1572872 | tf_op jit(solution)/shard_map/ppermute | solution.py:378
  31.8 0.5 collective-permute-start.6
  32.3 1.5 %collective-permute-start.7 = (bf16[1024,512]{1,0:T(8,128)(2,1)}, bf16[1024,512]{1,0:T(8,128)(2,1)}, u32[]{:S(2)}, u32[]{:S(2)}) collective-permute-start(bf16[1024,512]{1,0:T(8,128)(2,1)} %refs_8_.1), channel_id=1, source_target_pairs={{0,16},{4,12},{8,24},{12,4},{16,0},{20,28},{24,8},{28,20},{1,17},{... | collective-permute-start | bytes 3145736 | tf_op jit(solution)/shard_map/ppermute | solution.py:378
  33.8 2.0 %slice.7 = bf16[1024,256]{1,0:T(8,128)(2,1)} slice(bf16[1024,512]{1,0:T(8,128)(2,1)} %refs_8_.1), slice={[0:1024], [256:512]} | slice | bytes 1048576 | tf_op jit(solution)/shard_map/slice | solution.py:392
  35.8 5.2 %gate.3 = (bf16[512,1024]{1,0:T(8,128)(2,1)}, bf16[256,1024]{1,0:T(8,128)(2,1)}) custom-call(s32[3]{0:T(128)} %broadcast_xor_fusion.place_ref, bf16[1024,1024]{1,0:T(8,128)(2,1)} %get-tuple-element.42.z_ref, bf16[1024,1024]{1,0:T(8,128)(2,1)} %q_ref.3, f32[2,1024]{1,0:T(2,128)} %get-tuple-element.38.rows_ref, bf16[8,16,1024]{2,1,0:T(8,128)(2,1)} %copy-done.1), custom_call_target="tpu_custom_call" | custom-call | flops 1 | bytes 1 | tf_op jit(solution)/shard_map/gate/pallas_call | solution.py:209
  41.0 0.0 collective-permute-start.2
  41.0 13.9 %collective-permute-done.3.refs_2_ = bf16[256,1024]{1,0:T(8,128)(2,1)} collective-permute-done((bf16[256,1024]{1,0:T(8,128)(2,1)}, bf16[256,1024]{1,0:T(8,128)(2,1)}, u32[]{:S(2)}, u32[]{:S(2)}) %collective-permute-start.3) | collective-permute-done | bytes 524320 | tf_op jit(solution)/shard_map/ppermute | solution.py:335
  54.9 1.2 collective-permute-start.9
  56.1 0.0 collective-permute-done.5.refs_8_.refs_13_
  56.1 0.2 collective-permute-start.4
  56.3 0.0 collective-permute-done.6.refs_9_.refs_14_
  56.3 0.0 collective-permute-start.8
  56.4 0.0 collective-permute-done.7.refs_5_.refs_6_.refs_10_
  56.4 0.7 collective-permute-start.10
  57.1 0.0 collective-permute-done.2.refs_1_
  57.1 1.3 collective-permute-done.4.refs_3_
  58.4 5.1 %share.6 = bf16[512,768]{1,0:T(8,128)(2,1)} custom-call(bf16[512,1024]{1,0:T(8,128)(2,1)} %get-tuple-element.43.refs_0_, bf16[512,1024]{1,0:T(8,128)(2,1)} %collective-permute-done.2.refs_1_, bf16[256,1024]{1,0:T(8,128)(2,1)} %collective-permute-done.3.refs_2_, bf16[256,1024]{1,0:T(8,128)(2,1)} %collective-permute-done.4.refs_3_, bf16[1024,512]{1,0:T(8,128)(2,1)} %refs_8_.1, ...), custom_call_target="tpu_custom_call" | custom-call | flops 1 | bytes 1 | tf_op jit(solution)/shard_map/share/pallas_call | solution.py:250
  63.5 1.3 collective-permute-start.17
  64.8 17.3 %collective-permute-done.8.refs_7_.refs_16_ = bf16[1024,256]{1,0:T(8,128)(2,1)S(1)} collective-permute-done((bf16[1024,256]{1,0:T(8,128)(2,1)}, bf16[1024,256]{1,0:T(8,128)(2,1)S(1)}, u32[]{:S(2)}, u32[]{:S(2)}) %collective-permute-start.8) | collective-permute-done | bytes 524320 | tf_op jit(solution)/shard_map/ppermute | solution.py:335
  82.1 0.0 collective-permute-done.10.refs_6_.refs_15_
  82.1 0.0 collective-permute-done.9.refs_6_.refs_4_.refs_7_.refs_11_
  82.1 0.1 collective-permute-start.12
  82.2 1.0 collective-permute-start.11
  83.1 1.8 %collective-permute-start.13 = (bf16[1024,256]{1,0:T(8,128)(2,1)S(1)}, bf16[1024,256]{1,0:T(8,128)(2,1)}, u32[]{:S(2)}, u32[]{:S(2)}) collective-permute-start(bf16[1024,256]{1,0:T(8,128)(2,1)S(1)} %collective-permute-done.8.refs_7_.refs_16_), channel_id=1, source_target_pairs={{0,16},{4,12},{8,24},{12,4},{16,0},{20,28},{24,8},{28,20},{1,17},{... | collective-permute-start | bytes 1572872 | tf_op jit(solution)/shard_map/ppermute | solution.py:378
  85.0 0.8 collective-permute-start.14
  85.7 4.2 %share.5 = bf16[512,512]{1,0:T(8,128)(2,1)} custom-call(bf16[512,1024]{1,0:T(8,128)(2,1)} %get-tuple-element.43.refs_0_, bf16[512,1024]{1,0:T(8,128)(2,1)} %collective-permute-done.2.refs_1_, bf16[256,1024]{1,0:T(8,128)(2,1)} %collective-permute-done.3.refs_2_, bf16[256,1024]{1,0:T(8,128)(2,1)} %collective-permute-done.4.refs_3_, ...), custom_call_target="tpu_custom_call" | custom-call | flops 1 | bytes 1 | tf_op jit(solution)/shard_map/share/pallas_call | solution.py:250
  89.9 6.9 %collective-permute-done.17.refs_20_ = bf16[512,768]{1,0:T(8,128)(2,1)} collective-permute-done((bf16[512,768]{1,0:T(8,128)(2,1)}, bf16[512,768]{1,0:T(8,128)(2,1)}, u32[]{:S(2)}, u32[]{:S(2)}) %collective-permute-start.17) | collective-permute-done | bytes 786464 | tf_op jit(solution)/shard_map/ppermute | solution.py:335
  96.9 0.0 collective-permute-start.18
  96.9 11.7 %collective-permute-done.12.refs_2_ = bf16[256,1024]{1,0:T(8,128)(2,1)} collective-permute-done((bf16[256,1024]{1,0:T(8,128)(2,1)}, bf16[256,1024]{1,0:T(8,128)(2,1)}, u32[]{:S(2)}, u32[]{:S(2)}) %collective-permute-start.12) | collective-permute-done | bytes 524320 | tf_op jit(solution)/shard_map/ppermute | solution.py:335
  108.6 0.0 collective-permute-done.11.refs_7_.refs_17_
  108.6 0.0 collective-permute-done.13.refs_8_.refs_18_
  108.6 0.0 collective-permute-done.14.refs_9_.refs_19_
  108.6 5.1 %share.4 = (bf16[256,768]{1,0:T(8,128)(2,1)}, bf16[256,768]{1,0:T(8,128)(2,1)}) custom-call(bf16[512,1024]{1,0:T(8,128)(2,1)} %get-tuple-element.43.refs_0_, bf16[512,1024]{1,0:T(8,128)(2,1)} %collective-permute-done.2.refs_1_, bf16[256,1024]{1,0:T(8,128)(2,1)} %collective-permute-done.3.refs_2_, bf16[256,1024]{1,0:T(8,128)(2,1)} %collective-permute-done.4.refs_3_, ...), custom_call_target="tpu_custom_call" | custom-call | flops 68719476736 | bytes 268435456 | tf_op jit(solution)/shard_map/share/pallas_call | solution.py:250
  113.7 0.0 collective-permute-start.19
  113.7 2.2 %collective-permute-start.15 = (bf16[256,768]{1,0:T(8,128)(2,1)}, bf16[256,768]{1,0:T(8,128)(2,1)S(1)}, u32[]{:S(2)}, u32[]{:S(2)}) collective-permute-start(bf16[256,768]{1,0:T(8,128)(2,1)} %get-tuple-element.56), channel_id=1, source_target_pairs={{0,1},{1,0},{2,3},{3,2},{4,5},{5,4},{6,7},{7,6},{8,9},{9,8},{10,11... | collective-permute-start | bytes 1179656 | tf_op jit(solution)/shard_map/ppermute | solution.py:335
  115.9 0.1 collective-permute-start.16
  116.0 0.7 stack.67.place_ref
  116.7 0.6 concatenate.3.spots_ref
  117.3 2.5 %collective-permute-done.18.refs_21_ = bf16[512,512]{1,0:T(8,128)(2,1)} collective-permute-done((bf16[512,512]{1,0:T(8,128)(2,1)}, bf16[512,512]{1,0:T(8,128)(2,1)}, u32[]{:S(2)}, u32[]{:S(2)}) %collective-permute-start.18) | collective-permute-done | bytes 524320 | tf_op jit(solution)/shard_map/ppermute | solution.py:335
  119.8 0.0 collective-permute-done.19.refs_3_
  119.8 0.8 copy-done.4
  120.6 10.1 %share.7 = (bf16[256,2048]{1,0:T(8,128)(2,1)}, bf16[256,2048]{1,0:T(8,128)(2,1)}) custom-call(bf16[512,1024]{1,0:T(8,128)(2,1)} %get-tuple-element.43.refs_0_, bf16[512,1024]{1,0:T(8,128)(2,1)} %collective-permute-done.2.refs_1_, bf16[256,1024]{1,0:T(8,128)(2,1)} %collective-permute-done.12.refs_2_, bf16[256,1024]{1,0:T(8,128)(2,1)} %copy-done.4, ...), custom_call_target="tpu_custom_call" | custom-call | flops 1 | bytes 1 | tf_op jit(solution)/shard_map/share/pallas_call | solution.py:250
  130.7 0.0 collective-permute-start.20
  130.8 2.8 %place.2.refs_2_.refs_4_ = bf16[256,4096]{1,0:T(8,128)(2,1)} custom-call(s32[5]{0:T(128)} %stack.67.place_ref, bf16[256,2048]{1,0:T(8,128)(2,1)} %get-tuple-element.63.refs_0_), custom_call_target="tpu_custom_call" | custom-call | flops 1 | bytes 1 | tf_op jit(solution)/shard_map/place/pallas_call | solution.py:297
  133.5 0.0 collective-permute-done.15.refs_0_.refs_1_
  133.6 2.9 %collective-permute-done.16.refs_1_.refs_3_ = bf16[256,768]{1,0:T(8,128)(2,1)} collective-permute-done((bf16[256,768]{1,0:T(8,128)(2,1)}, bf16[256,768]{1,0:T(8,128)(2,1)}, u32[]{:S(2)}, u32[]{:S(2)}) %collective-permute-start.16) | collective-permute-done | bytes 393248 | tf_op jit(solution)/shard_map/ppermute | solution.py:374
  136.5 1.2 arrived.2.place_ref
  137.7 0.0 collective-permute-done.20.refs_2_
  137.7 3.6 %place.3 = bf16[256,4096]{1,0:T(8,128)(2,1)} custom-call(s32[11]{0:T(128)} %arrived.2.place_ref, bf16[256,2048]{1,0:T(8,128)(2,1)} %get-tuple-element.63.refs_0_, bf16[256,768]{1,0:T(8,128)(2,1)} %copy-done.5, bf16[256,2048]{1,0:T(8,128)(2,1)} %collective-permute-done.20.refs_2_, ...), custom_call_target="tpu_custom_call", output_to_operand_aliasing={{}: (5, {})} | custom-call | flops 1 | bytes 1 | tf_op jit(solution)/shard_map/place/pallas_call | solution.py:297
  (10 shorter events, 0.0 us)
Async XLA Ops:
  0.0 24.5 %collective-permute-start = (bf16[1024,512]{1,0:T(8,128)(2,1)}, bf16[1024,512]{1,0:T(8,128)(2,1)S(1)}, u32[]{:S(2)}, u32[]{:S(2)}) collective-permute-start(bf16[1024,512]{1,0:T(8,128)(2,1)} %refs_8_.1), channel_id=1, source_target_pairs={{0,8},{4,20},{8,0},{12,28},{16,24},{20,4},{24,16},{28,12},{1,9},{5... | collective-permute-start | bytes 3145736 | tf_op jit(solution)/shard_map/ppermute | solution.py:378
  4.1 25.6 %collective-permute-start.1 = (bf16[1024,256]{1,0:T(8,128)(2,1)S(1)}, bf16[1024,256]{1,0:T(8,128)(2,1)S(1)}, u32[]{:S(2)}, u32[]{:S(2)}) collective-permute-start(bf16[1024,256]{1,0:T(8,128)(2,1)S(1)} %slice.6), channel_id=1, source_target_pairs={{0,2},{1,3},{2,0},{3,1},{4,6},{5,7},{6,4},{7,5},{8,10},{9,11},{10,... | collective-permute-start | bytes 1572872 | tf_op jit(solution)/shard_map/ppermute | solution.py:335
  11.4 13.1 %all-to-all-start = ((bf16[8,16,1024]{2,1,0:T(8,128)(2,1)}), bf16[8,16,1024]{2,1,0:T(8,128)(2,1)S(1)}, u32[]{:S(2)}, u32[]{:S(2)}) async-start(bf16[8,16,1024]{2,1,0:T(8,128)(2,1)} %get-tuple-element.39), calls=%async_computation | async-start | bytes 524288 | tf_op jit(solution)/shard_map/all_to_all | solution.py:355
  24.5 3.2 %copy-start = (bf16[1024,512]{1,0:T(8,128)(2,1)}, bf16[1024,512]{1,0:T(8,128)(2,1)S(1)}, u32[]{:S(2)}) copy-start(bf16[1024,512]{1,0:T(8,128)(2,1)S(1)} %collective-permute-done.refs_4_.refs_5_.refs_9_) | copy-start | bytes 3145732
  24.5 0.8 copy-start.1
  25.2 4.4 %copy-start.6 = (s32[3]{0:T(128)S(1)}, s32[3]{0:T(128)}, u32[]{:S(2)}) copy-start(s32[3]{0:T(128)} %constant.45.clone) | copy-start | bytes 40
  29.7 11.3 %copy-start.2 = (bf16[1024,256]{1,0:T(8,128)(2,1)}, bf16[1024,256]{1,0:T(8,128)(2,1)S(1)}, u32[]{:S(2)}) copy-start(bf16[1024,256]{1,0:T(8,128)(2,1)S(1)} %collective-permute-done.1.refs_7_.refs_12_) | copy-start | bytes 1572868
  29.7 25.2 %collective-permute-start.3 = (bf16[256,1024]{1,0:T(8,128)(2,1)}, bf16[256,1024]{1,0:T(8,128)(2,1)}, u32[]{:S(2)}, u32[]{:S(2)}) collective-permute-start(bf16[256,1024]{1,0:T(8,128)(2,1)} %gate.2), channel_id=1, source_target_pairs={{0,2},{1,3},{2,0},{3,1},{4,6},{5,7},{6,4},{7,5},{8,10},{9,11},{10,... | collective-permute-start | bytes 1572872 | tf_op jit(solution)/shard_map/ppermute | solution.py:335
  30.3 25.9 %collective-permute-start.5 = (bf16[1024,256]{1,0:T(8,128)(2,1)S(1)}, bf16[1024,256]{1,0:T(8,128)(2,1)}, u32[]{:S(2)}, u32[]{:S(2)}) collective-permute-start(bf16[1024,256]{1,0:T(8,128)(2,1)S(1)} %collective-permute-done.1.refs_7_.refs_12_), channel_id=1, source_target_pairs={{0,8},{4,20},{8,0},{12,28},{16,24},{20,4},{24,16},{28,12},{1,9},{5... | collective-permute-start | bytes 1572872 | tf_op jit(solution)/shard_map/ppermute | solution.py:378
  31.8 24.6 %collective-permute-start.6 = (bf16[1024,256]{1,0:T(8,128)(2,1)S(1)}, bf16[1024,256]{1,0:T(8,128)(2,1)}, u32[]{:S(2)}, u32[]{:S(2)}) collective-permute-start(bf16[1024,256]{1,0:T(8,128)(2,1)S(1)} %collective-permute-done.1.refs_7_.refs_12_), channel_id=1, source_target_pairs={{0,16},{4,12},{8,24},{12,4},{16,0},{20,28},{24,8},{28,20},{1,17},{... | collective-permute-start | bytes 1572872 | tf_op jit(solution)/shard_map/ppermute | solution.py:378
  32.3 24.1 %collective-permute-start.7 = (bf16[1024,512]{1,0:T(8,128)(2,1)}, bf16[1024,512]{1,0:T(8,128)(2,1)}, u32[]{:S(2)}, u32[]{:S(2)}) collective-permute-start(bf16[1024,512]{1,0:T(8,128)(2,1)} %refs_8_.1), channel_id=1, source_target_pairs={{0,16},{4,12},{8,24},{12,4},{16,0},{20,28},{24,8},{28,20},{1,17},{... | collective-permute-start | bytes 3145736 | tf_op jit(solution)/shard_map/ppermute | solution.py:378
  41.0 16.1 %collective-permute-start.2 = (bf16[512,1024]{1,0:T(8,128)(2,1)}, bf16[512,1024]{1,0:T(8,128)(2,1)}, u32[]{:S(2)}, u32[]{:S(2)}) collective-permute-start(bf16[512,1024]{1,0:T(8,128)(2,1)} %get-tuple-element.43.refs_0_), channel_id=1, source_target_pairs={{0,4},{4,0},{8,12},{12,8},{16,20},{20,16},{24,28},{28,24},{1,5},{5... | collective-permute-start | bytes 3145736 | tf_op jit(solution)/shard_map/ppermute | solution.py:335
  54.9 27.2 %collective-permute-start.9 = (bf16[1024,512]{1,0:T(8,128)(2,1)}, bf16[1024,512]{1,0:T(8,128)(2,1)}, u32[]{:S(2)}, u32[]{:S(2)}) collective-permute-start(bf16[1024,512]{1,0:T(8,128)(2,1)} %copy-done), channel_id=1, source_target_pairs={{0,16},{4,12},{8,24},{12,4},{16,0},{20,28},{24,8},{28,20},{1,17},{... | collective-permute-start | bytes 3145736 | tf_op jit(solution)/shard_map/ppermute | solution.py:378
  56.1 2.3 %collective-permute-start.4 = (bf16[256,1024]{1,0:T(8,128)(2,1)}, bf16[256,1024]{1,0:T(8,128)(2,1)}, u32[]{:S(2)}, u32[]{:S(2)}) collective-permute-start(bf16[256,1024]{1,0:T(8,128)(2,1)} %collective-permute-done.3.refs_2_), channel_id=1, source_target_pairs={{0,4},{4,0},{8,12},{12,8},{16,20},{20,16},{24,28},{28,24},{1,5},{5... | collective-permute-start | bytes 1572872 | tf_op jit(solution)/shard_map/ppermute | solution.py:335
  56.3 25.7 %collective-permute-start.8 = (bf16[1024,256]{1,0:T(8,128)(2,1)}, bf16[1024,256]{1,0:T(8,128)(2,1)S(1)}, u32[]{:S(2)}, u32[]{:S(2)}) collective-permute-start(bf16[1024,256]{1,0:T(8,128)(2,1)} %slice.7), channel_id=1, source_target_pairs={{0,2},{1,3},{2,0},{3,1},{4,6},{5,7},{6,4},{7,5},{8,10},{9,11},{10,... | collective-permute-start | bytes 1572872 | tf_op jit(solution)/shard_map/ppermute | solution.py:335
  56.4 25.7 %collective-permute-start.10 = (bf16[1024,256]{1,0:T(8,128)(2,1)}, bf16[1024,256]{1,0:T(8,128)(2,1)}, u32[]{:S(2)}, u32[]{:S(2)}) collective-permute-start(bf16[1024,256]{1,0:T(8,128)(2,1)} %collective-permute-done.5.refs_8_.refs_13_), channel_id=1, source_target_pairs={{0,16},{4,12},{8,24},{12,4},{16,0},{20,28},{24,8},{28,20},{1,17},{... | collective-permute-start | bytes 1572872 | tf_op jit(solution)/shard_map/ppermute | solution.py:378
  63.5 33.3 %collective-permute-start.17 = (bf16[512,768]{1,0:T(8,128)(2,1)}, bf16[512,768]{1,0:T(8,128)(2,1)}, u32[]{:S(2)}, u32[]{:S(2)}) collective-permute-start(bf16[512,768]{1,0:T(8,128)(2,1)} %share.6), channel_id=1, source_target_pairs={{0,1},{1,0},{2,3},{3,2},{4,5},{5,4},{6,7},{7,6},{8,9},{9,8},{10,11... | collective-permute-start | bytes 2359304 | tf_op jit(solution)/shard_map/ppermute | solution.py:335
  82.1 3.6 %copy-start.3 = (bf16[1024,256]{1,0:T(8,128)(2,1)}, bf16[1024,256]{1,0:T(8,128)(2,1)S(1)}, u32[]{:S(2)}) copy-start(bf16[1024,256]{1,0:T(8,128)(2,1)S(1)} %collective-permute-done.8.refs_7_.refs_16_) | copy-start | bytes 1572868
  82.1 26.5 %collective-permute-start.12 = (bf16[256,1024]{1,0:T(8,128)(2,1)}, bf16[256,1024]{1,0:T(8,128)(2,1)}, u32[]{:S(2)}, u32[]{:S(2)}) collective-permute-start(bf16[256,1024]{1,0:T(8,128)(2,1)} %get-tuple-element.54), channel_id=1, source_target_pairs={{0,2},{1,3},{2,0},{3,1},{4,6},{5,7},{6,4},{7,5},{8,10},{9,11},{10,... | collective-permute-start | bytes 1572872 | tf_op jit(solution)/shard_map/ppermute | solution.py:335
  82.2 26.4 %collective-permute-start.11 = (bf16[1024,256]{1,0:T(8,128)(2,1)S(1)}, bf16[1024,256]{1,0:T(8,128)(2,1)}, u32[]{:S(2)}, u32[]{:S(2)}) collective-permute-start(bf16[1024,256]{1,0:T(8,128)(2,1)S(1)} %collective-permute-done.8.refs_7_.refs_16_), channel_id=1, source_target_pairs={{0,8},{4,20},{8,0},{12,28},{16,24},{20,4},{24,16},{28,12},{1,9},{5... | collective-permute-start | bytes 1572872 | tf_op jit(solution)/shard_map/ppermute | solution.py:378
  83.1 25.5 %collective-permute-start.13 = (bf16[1024,256]{1,0:T(8,128)(2,1)S(1)}, bf16[1024,256]{1,0:T(8,128)(2,1)}, u32[]{:S(2)}, u32[]{:S(2)}) collective-permute-start(bf16[1024,256]{1,0:T(8,128)(2,1)S(1)} %collective-permute-done.8.refs_7_.refs_16_), channel_id=1, source_target_pairs={{0,16},{4,12},{8,24},{12,4},{16,0},{20,28},{24,8},{28,20},{1,17},{... | collective-permute-start | bytes 1572872 | tf_op jit(solution)/shard_map/ppermute | solution.py:378
  85.0 23.6 %collective-permute-start.14 = (bf16[1024,256]{1,0:T(8,128)(2,1)S(1)}, bf16[1024,256]{1,0:T(8,128)(2,1)}, u32[]{:S(2)}, u32[]{:S(2)}) collective-permute-start(bf16[1024,256]{1,0:T(8,128)(2,1)S(1)} %collective-permute-done.8.refs_7_.refs_16_), channel_id=1, source_target_pairs={{0,24},{4,28},{8,16},{12,20},{16,8},{20,12},{24,0},{28,4},{1,25},{... | collective-permute-start | bytes 1572872 | tf_op jit(solution)/shard_map/ppermute | solution.py:378
  96.9 22.9 %collective-permute-start.18 = (bf16[512,512]{1,0:T(8,128)(2,1)}, bf16[512,512]{1,0:T(8,128)(2,1)}, u32[]{:S(2)}, u32[]{:S(2)}) collective-permute-start(bf16[512,512]{1,0:T(8,128)(2,1)} %share.5), channel_id=1, source_target_pairs={{0,1},{1,0},{2,3},{3,2},{4,5},{5,4},{6,7},{7,6},{8,9},{9,8},{10,11... | collective-permute-start | bytes 1572872 | tf_op jit(solution)/shard_map/ppermute | solution.py:335
  113.7 6.1 %collective-permute-start.19 = (bf16[256,1024]{1,0:T(8,128)(2,1)}, bf16[256,1024]{1,0:T(8,128)(2,1)S(1)}, u32[]{:S(2)}, u32[]{:S(2)}) collective-permute-start(bf16[256,1024]{1,0:T(8,128)(2,1)} %collective-permute-done.12.refs_2_), channel_id=1, source_target_pairs={{0,4},{4,0},{8,12},{12,8},{16,20},{20,16},{24,28},{28,24},{1,5},{5... | collective-permute-start | bytes 1572872 | tf_op jit(solution)/shard_map/ppermute | solution.py:335
  113.7 19.8 %collective-permute-start.15 = (bf16[256,768]{1,0:T(8,128)(2,1)}, bf16[256,768]{1,0:T(8,128)(2,1)S(1)}, u32[]{:S(2)}, u32[]{:S(2)}) collective-permute-start(bf16[256,768]{1,0:T(8,128)(2,1)} %get-tuple-element.56), channel_id=1, source_target_pairs={{0,1},{1,0},{2,3},{3,2},{4,5},{5,4},{6,7},{7,6},{8,9},{9,8},{10,11... | collective-permute-start | bytes 1179656 | tf_op jit(solution)/shard_map/ppermute | solution.py:335
  115.9 20.6 %collective-permute-start.16 = (bf16[256,768]{1,0:T(8,128)(2,1)}, bf16[256,768]{1,0:T(8,128)(2,1)}, u32[]{:S(2)}, u32[]{:S(2)}) collective-permute-start(bf16[256,768]{1,0:T(8,128)(2,1)} %get-tuple-element.57), channel_id=1, source_target_pairs={{0,5},{1,4},{2,7},{3,6},{4,1},{5,0},{6,3},{7,2},{8,13},{9,12},{10,... | collective-permute-start | bytes 1179656 | tf_op jit(solution)/shard_map/ppermute | solution.py:374
  119.8 0.8 copy-start.4
  130.7 6.9 %collective-permute-start.20 = (bf16[256,2048]{1,0:T(8,128)(2,1)}, bf16[256,2048]{1,0:T(8,128)(2,1)}, u32[]{:S(2)}, u32[]{:S(2)}) collective-permute-start(bf16[256,2048]{1,0:T(8,128)(2,1)} %get-tuple-element.64), channel_id=1, source_target_pairs={{0,4},{4,0},{8,12},{12,8},{16,20},{20,16},{24,28},{28,24},{1,5},{5... | collective-permute-start | bytes 3145736 | tf_op jit(solution)/shard_map/ppermute | solution.py:335
  133.5 2.9 %copy-start.5 = (bf16[256,768]{1,0:T(8,128)(2,1)}, bf16[256,768]{1,0:T(8,128)(2,1)S(1)}, u32[]{:S(2)}) copy-start(bf16[256,768]{1,0:T(8,128)(2,1)S(1)} %collective-permute-done.15.refs_0_.refs_1_) | copy-start | bytes 1179652
